TPU v7x, 128 devices: a whole 4x4x4 slice. The times are simulated.
128 devices in a mesh: section: 4 (over z), tp: 32 (over x, y, core).
Axes of the slice: x: 4, y: 4, z: 4, core: 2. Of those that a mesh axis runs over, the one named last changes fastest.
Arguments:
- entering: bfloat16 [2, 88, 16384], P(None, None, 'tp'), may hold values from -6 to 6
- norm_gain: bfloat16 [4, 16384], P('section', 'tp'), may hold values from 0.099609375 to 1.8984375
- query_weight: bfloat16 [4, 16384, 8192], P(None, ('section', 'tp')), may hold values from -0.046875 to 0.046875
- key_matrix: bfloat16 [4, 16384, 512], P(None, ('section', 'tp')), may hold values from -0.046875 to 0.046875
- value_matrix: bfloat16 [4, 16384, 512], P(None, ('section', 'tp')), may hold values from -0.046875 to 0.046875
- output_weight: bfloat16 [4, 8192, 16384], P(None, ('section', 'tp')), may hold values from -0.0625 to 0.0625
Outputs:
- section_outputs: bfloat16 [4, 2, 88, 16384], P('section', None, None, 'tp')
All inputs are finite; a program needn't handle non-finite values.
Results may differ from a plain program's by a relative error of at most 0.017.
Values may be sent and summed in bfloat16 or wider, within the bound.
No kernel may reach another device: no remote copies, remote signals or barrier semaphores. Data moves between devices by JAX's collectives and lax.ppermute only.
A program may use at most 128 MiB of HBM per device.

v0:
```python
import functools
import math

import jax
import jax.numpy as jnp
from jax import lax
from jax.experimental import pallas as pl
from jax.experimental.pallas import tpu as pltpu
from jax.sharding import Mesh, PartitionSpec as P


ALL = ("z", "x", "y", "c")
HEAD = 128
SEQ = 88
COLS = 256
WIDTH = 16384
SLAB = 2304
OCOLS = 4096
ROWS = 352
VMEM_LIMIT = 48 * 1024 * 1024
f32 = jnp.float32
bf16 = jnp.bfloat16
SMEM = pl.BlockSpec(memory_space=pltpu.SMEM)
PARAMS = pltpu.CompilerParams(vmem_limit_bytes=VMEM_LIMIT)


def dot(a, b, contract=((1,), (0,))):
    return lax.dot_general(a, b, (contract, ((), ())), preferred_element_type=f32)


def whole(*shape):
    return pl.BlockSpec(shape, lambda s: (0,) * len(shape))


def cost(flops, size):
    return pl.CostEstimate(flops=flops, bytes_accessed=size, transcendentals=0)


def masks():
    rows = lax.broadcasted_iota(jnp.int32, (SEQ, 128), 0)
    lanes = lax.broadcasted_iota(jnp.int32, (SEQ, 128), 1)
    return rows == lanes, lanes <= rows


def slab_in_kernel(scalars, q_ref, k_ref, v_ref, *outs):
    for k, out in enumerate(outs):
        at = lax.rem(scalars[0] + k, 4)
        out[:, :2048] = q_ref[0, :, pl.ds(pl.multiple_of(at * 2048, 2048), 2048)]
        out[:, 2048:2176] = k_ref[0, :, pl.ds(pl.multiple_of(at * 128, 128), 128)]
        out[:, 2176:] = v_ref[0, :, pl.ds(pl.multiple_of(at * 128, 128), 128)]


def slab_in(layer, scalars, q, k, v):
    return pl.pallas_call(
        slab_in_kernel,
        grid=(4,),
        in_specs=[
            SMEM,
            pl.BlockSpec((1, 32, 8192), lambda s: (layer, s, 0)),
            pl.BlockSpec((1, 32, 512), lambda s: (layer, s, 0)),
            pl.BlockSpec((1, 32, 512), lambda s: (layer, s, 0)),
        ],
        out_specs=[pl.BlockSpec((32, SLAB), lambda s: (s, 0))] * 4,
        out_shape=[jax.ShapeDtypeStruct((128, SLAB), bf16)] * 4,
        compiler_params=PARAMS,
        cost_estimate=cost(0, 4_700_000),
        name="slab_in",
    )(scalars, q, k, v)


def slab_out_kernel(scalars, o_ref, *outs):
    for k, out in enumerate(outs):
        at = lax.rem(scalars[1] + k, 4) * COLS
        for s in range(16):
            out[:, COLS * s : COLS * s + COLS] = o_ref[
                0, :, pl.ds(pl.multiple_of(at + 1024 * s, COLS), COLS)
            ]


def slab_out(layer, scalars, o):
    return pl.pallas_call(
        slab_out_kernel,
        grid=(4,),
        in_specs=[SMEM, pl.BlockSpec((1, 16, WIDTH), lambda s: (layer, s, 0))],
        out_specs=[pl.BlockSpec((16, OCOLS), lambda s: (s, 0))] * 4,
        out_shape=[jax.ShapeDtypeStruct((64, OCOLS), bf16)] * 4,
        compiler_params=PARAMS,
        cost_estimate=cost(0, 4_200_000),
        name="slab_out",
    )(scalars, o)


def project_kernel(layer, scalars, *refs):
    xs, gain_ref, ws, kvs, refs = refs[:4], refs[4], refs[5:13], refs[13:21], refs[21:]
    out_ref, xg_ref, ss_ref, kv_ref = refs
    z, core = scalars[0], scalars[2]

    @pl.when(pl.program_id(0) == 0)
    def _():
        gains = gain_ref[lax.rem(z - layer + 4, 4)]
        at = lax.broadcasted_iota(jnp.int32, (4, COLS), 0)
        total = jnp.zeros((SEQ, 1), f32)
        parts = []
        for k in range(4):
            wide = xs[k][...].astype(f32)
            total += jnp.sum(wide * wide, axis=1, keepdims=True)
            gain = jnp.sum(jnp.where(at == lax.rem(z - k + 4, 4), gains, 0.0), axis=0, keepdims=True)
            scaled = wide * gain
            turned = jnp.concatenate([scaled[:, 128:], scaled[:, :128]], axis=1)
            parts.append(jnp.where(core == 1, turned, scaled))
        scaled = jnp.concatenate(parts, axis=1)
        xg_ref[...] = scaled.astype(bf16)
        padded = jnp.concatenate([scaled, jnp.zeros((128 - SEQ, 1024), f32)], axis=0).astype(bf16)
        eye, _ = masks()
        row = jnp.sum(jnp.where(eye, total, 0.0), axis=0, keepdims=True)
        high = row.astype(bf16).astype(f32)
        which = lax.broadcasted_iota(jnp.int32, (8, 128), 0)
        ss_ref[...] = jnp.where(which == 0, high, jnp.where(which == 1, row - high, 0.0))
        kv = dot(padded, jnp.concatenate([w[...] for w in kvs], axis=0))
        kv_ref[:128] = kv[:, :128].T
        kv_ref[128:] = kv[:, 128:].T

    q = dot(xg_ref[...], jnp.concatenate([w[...] for w in ws], axis=0))
    for h in range(4):
        out_ref[h] = jnp.concatenate(
            [kv_ref[...], ss_ref[...], q[:, HEAD * h : HEAD * h + HEAD]], axis=0
        ).astype(bf16)


def project(layer, scalars, xs, gains, weights):
    return pl.pallas_call(
        functools.partial(project_kernel, layer),
        grid=(4,),
        in_specs=[SMEM]
        + [whole(SEQ, COLS)] * 4
        + [whole(4, 4, COLS)]
        + [pl.BlockSpec((128, 512), lambda s: (0, s))] * 8
        + [pl.BlockSpec((128, 256), lambda s: (0, 8))] * 8,
        out_specs=pl.BlockSpec((4, ROWS, 128), lambda s: (s, 0, 0)),
        out_shape=jax.ShapeDtypeStruct((16, ROWS, 128), bf16),
        scratch_shapes=[
            pltpu.VMEM((SEQ, 1024), bf16),
            pltpu.VMEM((8, 128), f32),
            pltpu.VMEM((256, 128), f32),
        ],
        compiler_params=PARAMS,
        cost_estimate=cost(2 * SEQ * 1024 * SLAB, 6_500_000),
        name="project",
    )(scalars, *xs, gains, *weights, *weights)


def attend_kernel(recv_ref, out_ref, acc):
    step = pl.program_id(0)

    @pl.when(step == 0)
    def _():
        acc[...] = jnp.sum(recv_ref[...].astype(f32), axis=0)

    @pl.when(step > 0)
    def _():
        acc[...] += jnp.sum(recv_ref[...].astype(f32), axis=0)

    @pl.when(step == 3)
    def _():
        total = acc[256:257] + acc[257:258]
        row = lax.rsqrt(total * (1.0 / WIDTH) + 1e-05)
        eye, causal = masks()
        column = jnp.sum(jnp.where(eye, row, 0.0), axis=1, keepdims=True)
        q = (acc[264:] * column).astype(bf16)
        keys = (acc[:128] * row).astype(bf16)
        values = (acc[128:256] * row).astype(bf16)
        scores = dot(q, keys) * (1.0 / math.sqrt(HEAD))
        weights = jnp.where(causal, jnp.exp(scores), 0.0)
        shares = (weights / jnp.sum(weights, axis=1, keepdims=True)).astype(bf16)
        out_ref[...] = dot(shares, values, ((1,), (1,))).astype(bf16)


def attend(received):
    return pl.pallas_call(
        attend_kernel,
        grid=(4,),
        in_specs=[pl.BlockSpec((4, ROWS, 128), lambda s: (s, 0, 0))],
        out_specs=whole(SEQ, HEAD),
        out_shape=jax.ShapeDtypeStruct((SEQ, HEAD), bf16),
        scratch_shapes=[pltpu.VMEM((ROWS, 128), f32)],
        compiler_params=PARAMS,
        cost_estimate=cost(6_000_000, 1_500_000),
        name="attend",
    )(received)


def output_kernel(scalars, *refs):
    mixed, ws, out_ref, mixed_ref = refs[:4], refs[4:12], refs[12], refs[13]

    @pl.when(pl.program_id(0) == 0)
    def _():
        parts = []
        for part in mixed:
            part = part[...].astype(f32)
            turned = jnp.concatenate([part[:, 64:], part[:, :64]], axis=1)
            parts.append(jnp.where(scalars[2] == 1, turned, part))
        mixed_ref[...] = jnp.concatenate(parts, axis=1).astype(bf16)

    o = dot(mixed_ref[...], jnp.concatenate([w[...] for w in ws], axis=0))
    for i in range(4):
        out_ref[i] = o[:, COLS * i : COLS * i + COLS].astype(bf16)


def output(scalars, mixed, weights):
    return pl.pallas_call(
        output_kernel,
        grid=(4,),
        in_specs=[SMEM]
        + [whole(SEQ, HEAD)] * 4
        + [pl.BlockSpec((64, 1024), lambda s: (0, s))] * 8,
        out_specs=pl.BlockSpec((4, SEQ, COLS), lambda s: (s, 0, 0)),
        out_shape=jax.ShapeDtypeStruct((16, SEQ, COLS), bf16),
        scratch_shapes=[pltpu.VMEM((SEQ, 512), bf16)],
        compiler_params=PARAMS,
        cost_estimate=cost(2 * SEQ * 512 * OCOLS, 5_000_000),
        name="output",
    )(scalars, *mixed, *weights)


def close_kernel(recv_ref, x_ref, out_ref):
    out_ref[...] = (x_ref[...].astype(f32) + jnp.sum(recv_ref[...].astype(f32), axis=0)).astype(bf16)


def close(received, x):
    return pl.pallas_call(
        close_kernel,
        grid=(1,),
        in_specs=[whole(16, SEQ, COLS), whole(SEQ, COLS)],
        out_specs=whole(SEQ, COLS),
        out_shape=jax.ShapeDtypeStruct((SEQ, COLS), bf16),
        compiler_params=PARAMS,
        cost_estimate=cost(400_000, 800_000),
        name="close",
    )(received, x)


def exchange(value, axes):
    return lax.all_to_all(value, axes, 0, 0, tiled=True)


def shift(value, axis, by):
    return lax.ppermute(value, axis, [(i, (i + by) % 4) for i in range(4)])


def line(value, axis):
    return [value] + [shift(value, axis, k) for k in range(1, 4)]


def after(gate, values):
    return lax.optimization_barrier((gate, values))


def relay(slabs, axis):
    return [slabs[0]] + [shift(slabs[k], axis, k) for k in range(1, 4)]


def swapped(pieces):
    others = [lax.ppermute(piece, "c", [(0, 1), (1, 0)]) for piece in pieces]
    return [side for pair in zip(pieces, others) for side in pair]


def body(entering, norm_gain, query_weight, key_matrix, value_matrix, output_weight):
    plane, across, along, core = (lax.axis_index(name) for name in ALL)
    slot = 2 * core + lax.rem(along, 2)
    scalars = jnp.stack([plane, along, core]).astype(jnp.int32)

    rounds = []
    for r in range(4):
        pairs = []
        for p in range(4):
            for t in range(32):
                s = (t // 8 - r) % 4
                pairs.append((32 * p + t, 32 * p + 2 * ((2 * t) % 16 + s % 2) + s // 2))
        s = lax.rem(across - r + 4, 4)
        piece = lax.dynamic_slice(entering, (s // 2, 0, lax.rem(s, 2) * COLS), (1, SEQ, COLS))[0]
        gain = lax.dynamic_slice(norm_gain, (0, lax.rem(s, 2) * COLS), (1, COLS))
        piece = jnp.concatenate([piece, jnp.broadcast_to(gain, (8, COLS))], axis=0)
        rounds.append(lax.ppermute(piece, ALL, pairs))
    rounds = jnp.stack(rounds)
    xs = [
        lax.dynamic_index_in_dim(rounds, lax.rem(plane - k - slot + 8, 4), 0, keepdims=False)[:SEQ]
        for k in range(4)
    ]
    gains = jnp.stack([rounds[:, SEQ][lax.rem(p - slot + 4, 4)] for p in range(4)])
    gains = jnp.stack(line(gains, "z")).astype(f32)

    slabs = [slab_in(layer, scalars, query_weight, key_matrix, value_matrix) for layer in range(4)]
    cuts = [slab_out(layer, scalars, output_weight) for layer in range(4)]
    ins = swapped(relay(slabs[0], "z"))
    outs = relay(cuts[0], "y")
    xs, (slabs, cuts) = after(xs, (slabs[1:], cuts[1:]))
    states = []
    for layer in range(4):
        xs, outs = after(xs, outs)
        partial = project(layer, scalars, xs, gains, ins)
        partial, outs = after(partial, outs)
        if layer < 3:
            partial, slab = after(partial, slabs[layer])
            ins = relay(slab, "z")
        outs = swapped(outs)
        mixed = line(attend(exchange(partial, ("x", "y"))), "y")
        if layer < 3:
            mixed, ins = after(mixed, ins)
        partial = output(scalars, mixed, outs)
        if layer < 3:
            partial, (ins, cut) = after(partial, (ins, cuts[layer]))
            ins = swapped(ins)
            outs = relay(cut, "y")
        x = close(exchange(partial, ("z", "x")), xs[0])
        states.append(x)
        if layer < 3:
            xs = line(x, "z")

    states = jnp.stack(states)
    rounds = []
    for k in range(4):
        pairs = [
            (2 * i + c, 32 * ((2 * c + i % 2 + k) % 4) + i // 2) for i in range(64) for c in range(2)
        ]
        piece = lax.dynamic_index_in_dim(states, lax.rem(slot + k, 4), 0, keepdims=False)
        rounds.append(lax.ppermute(piece, ALL, pairs))
    rounds = jnp.stack(rounds)
    pieces = [
        lax.dynamic_index_in_dim(rounds, lax.rem(plane - s + 4, 4), 0, keepdims=False) for s in range(4)
    ]
    return jnp.stack(
        [jnp.concatenate(pieces[:2], axis=1), jnp.concatenate(pieces[2:], axis=1)]
    )[None]


def solution(mesh):
    fine = Mesh(mesh.devices.reshape(4, 4, 4, 2), ALL)
    tp = ("x", "y", "c")
    rows = P(None, ALL, None)
    return jax.shard_map(
        body,
        mesh=fine,
        in_specs=(P(None, None, tp), P("z", tp), rows, rows, rows, rows),
        out_specs=P("z", None, None, tp),
        check_vma=False,
    )
```

profile of v0, /device:TPU:5, one launch (start us, length us, event | category | flops | bytes accessed | tf_op | source)
XLA Modules:
  0.0 481.7 jit_solution(16838189512131527884)
XLA Ops:
  24.7 20.6 %collective-permute-done.7 = bf16[4,256]{1,0:T(4,128)(2,1)S(1)} collective-permute-done((bf16[4,256]{1,0:T(4,128)(2,1)S(1)}, bf16[4,256]{1,0:T(4,128)(2,1)S(1)}, u32[]{:S(2)}, u32[]{:S(2)}) %collective-permute-start.7) | collective-permute-done | bytes 2080 | tf_op jit(solution)/shard_map/ppermute | solution.py:247
  59.3 7.3 %collective-permute-done.5.refs_8_ = bf16[64,4096]{1,0:T(8,128)(2,1)S(1)} collective-permute-done((bf16[64,4096]{1,0:T(8,128)(2,1)S(1)}, bf16[64,4096]{1,0:T(8,128)(2,1)S(1)}, u32[]{:S(2)}, u32[]{:S(2)}) %collective-permute-start.5) | collective-permute-done | bytes 524320 | tf_op jit(solution)/shard_map/ppermute | solution.py:247
  99.1 5.2 %project.4 = bf16[16,352,128]{2,1,0:T(8,128)(2,1)} custom-call(s32[3]{0:T(128)S(1)} %pad_add_fusion.scalars, bf16[88,256]{1,0:T(8,128)(2,1)S(1)} %get-tuple-element.215.refs_0_.x_ref, bf16[88,256]{1,0:T(8,128)(2,1)S(1)} %get-tuple-element.216.refs_1_, bf16[88,256]{1,0:T(8,128)(2,1)S(1)} %get-tuple-element.217.refs_2_, ...), custom_call_target="tpu_custom_call" | custom-call | flops 415236096 | bytes 6500000 | tf_op jit(solution)/shard_map/project/pallas_call | solution.py:131
  104.3 10.6 %all-to-all-start = ((bf16[16,352,128]{2,1,0:T(8,128)(2,1)}), bf16[16,352,128]{2,1,0:T(8,128)(2,1)S(1)}, u32[]{:S(2)}, u32[]{:S(2)}) async-start(bf16[16,352,128]{2,1,0:T(8,128)(2,1)} %project.4), calls=%async_computation | async-start | bytes 2883584 | tf_op jit(solution)/shard_map/all_to_all | solution.py:243
  122.1 6.6 %collective-permute-done.20.refs_7_.refs_15_ = bf16[128,2304]{1,0:T(8,128)(2,1)S(1)} collective-permute-done((bf16[128,2304]{1,0:T(8,128)(2,1)}, bf16[128,2304]{1,0:T(8,128)(2,1)S(1)}, u32[]{:S(2)}, u32[]{:S(2)}) %collective-permute-start.20) | collective-permute-done | bytes 589856 | tf_op jit(solution)/shard_map/ppermute | solution.py:247
  128.6 5.6 %collective-permute-start.25 = (bf16[64,4096]{1,0:T(8,128)(2,1)}, bf16[64,4096]{1,0:T(8,128)(2,1)}, u32[]{:S(2)}, u32[]{:S(2)}) collective-permute-start(bf16[64,4096]{1,0:T(8,128)(2,1)} %copy-done.18), channel_id=1, source_target_pairs={{0,1},{1,0},{2,3},{3,2},{4,5},{5,4},{6,7},{7,6},{8,9},{9,8},{10,11... | collective-permute-start | bytes 1572872 | tf_op jit(solution)/shard_map/ppermute | solution.py:263
  134.3 7.8 %collective-permute-done.21.refs_9_.refs_17_ = bf16[128,2304]{1,0:T(8,128)(2,1)S(1)} collective-permute-done((bf16[128,2304]{1,0:T(8,128)(2,1)}, bf16[128,2304]{1,0:T(8,128)(2,1)S(1)}, u32[]{:S(2)}, u32[]{:S(2)}) %collective-permute-start.21) | collective-permute-done | bytes 589856 | tf_op jit(solution)/shard_map/ppermute | solution.py:247
  177.6 6.2 %collective-permute-start.35 = (bf16[128,2304]{1,0:T(8,128)(2,1)}, bf16[128,2304]{1,0:T(8,128)(2,1)}, u32[]{:S(2)}, u32[]{:S(2)}) collective-permute-start(bf16[128,2304]{1,0:T(8,128)(2,1)} %copy-done.4), channel_id=1, source_target_pairs={{0,1},{1,0},{2,3},{3,2},{4,5},{5,4},{6,7},{7,6},{8,9},{9,8},{10,11... | collective-permute-start | bytes 1769480 | tf_op jit(solution)/shard_map/ppermute | solution.py:263
  217.7 5.8 %collective-permute-start.43 = (bf16[64,4096]{1,0:T(8,128)(2,1)}, bf16[64,4096]{1,0:T(8,128)(2,1)}, u32[]{:S(2)}, u32[]{:S(2)}) collective-permute-start(bf16[64,4096]{1,0:T(8,128)(2,1)} %copy-done.16), channel_id=1, source_target_pairs={{0,1},{1,0},{2,3},{3,2},{4,5},{5,4},{6,7},{7,6},{8,9},{9,8},{10,11... | collective-permute-start | bytes 1572872 | tf_op jit(solution)/shard_map/ppermute | solution.py:263
  226.1 18.8 %collective-permute-start.45 = (bf16[64,4096]{1,0:T(8,128)(2,1)}, bf16[64,4096]{1,0:T(8,128)(2,1)}, u32[]{:S(2)}, u32[]{:S(2)}) collective-permute-start(bf16[64,4096]{1,0:T(8,128)(2,1)} %collective-permute-done.31.refs_8_), channel_id=1, source_target_pairs={{0,1},{1,0},{2,3},{3,2},{4,5},{5,4},{6,7},{7,6},{8,9},{9,8},{10,11... | collective-permute-start | bytes 1572872 | tf_op jit(solution)/shard_map/ppermute | solution.py:263
  269.7 5.6 %collective-permute-start.53 = (bf16[128,2304]{1,0:T(8,128)(2,1)S(1)}, bf16[128,2304]{1,0:T(8,128)(2,1)}, u32[]{:S(2)}, u32[]{:S(2)}) collective-permute-start(bf16[128,2304]{1,0:T(8,128)(2,1)S(1)} %get-tuple-element.305.refs_5_.refs_13_), channel_id=1, source_target_pairs={{0,1},{1,0},{2,3},{3,2},{4,5},{5,4},{6,7},{7,6},{8,9},{9,8},{10,11... | collective-permute-start | bytes 1769480 | tf_op jit(solution)/shard_map/ppermute | solution.py:263
  275.3 5.9 %collective-permute-start.55 = (bf16[128,2304]{1,0:T(8,128)(2,1)S(1)}, bf16[128,2304]{1,0:T(8,128)(2,1)}, u32[]{:S(2)}, u32[]{:S(2)}) collective-permute-start(bf16[128,2304]{1,0:T(8,128)(2,1)S(1)} %copy-done.7), channel_id=1, source_target_pairs={{0,1},{1,0},{2,3},{3,2},{4,5},{5,4},{6,7},{7,6},{8,9},{9,8},{10,11... | collective-permute-start | bytes 1769480 | tf_op jit(solution)/shard_map/ppermute | solution.py:263
  298.9 9.6 %collective-permute-start.49 = (bf16[88,256]{1,0:T(8,128)(2,1)S(1)}, bf16[88,256]{1,0:T(8,128)(2,1)S(1)}, u32[]{:S(2)}, u32[]{:S(2)}) collective-permute-start(bf16[88,256]{1,0:T(8,128)(2,1)S(1)} %close.5.refs_0_.x_ref), channel_id=1, source_target_pairs={{0,96},{32,0},{64,32},{96,64},{1,97},{33,1},{65,33},{97,65},{2,98}... | collective-permute-start | bytes 135176 | tf_op jit(solution)/shard_map/ppermute | solution.py:247
  323.3 5.8 %collective-permute-start.63 = (bf16[64,4096]{1,0:T(8,128)(2,1)}, bf16[64,4096]{1,0:T(8,128)(2,1)}, u32[]{:S(2)}, u32[]{:S(2)}) collective-permute-start(bf16[64,4096]{1,0:T(8,128)(2,1)} %copy-done.10), channel_id=1, source_target_pairs={{0,1},{1,0},{2,3},{3,2},{4,5},{5,4},{6,7},{7,6},{8,9},{9,8},{10,11... | collective-permute-start | bytes 1572872 | tf_op jit(solution)/shard_map/ppermute | solution.py:263
  331.6 18.8 %collective-permute-start.65 = (bf16[64,4096]{1,0:T(8,128)(2,1)}, bf16[64,4096]{1,0:T(8,128)(2,1)}, u32[]{:S(2)}, u32[]{:S(2)}) collective-permute-start(bf16[64,4096]{1,0:T(8,128)(2,1)} %collective-permute-done.51.refs_8_), channel_id=1, source_target_pairs={{0,1},{1,0},{2,3},{3,2},{4,5},{5,4},{6,7},{7,6},{8,9},{9,8},{10,11... | collective-permute-start | bytes 1572872 | tf_op jit(solution)/shard_map/ppermute | solution.py:263
  370.1 5.1 %all-to-all-start.5 = ((bf16[16,88,256]{2,1,0:T(8,128)(2,1)}), bf16[16,88,256]{2,1,0:T(8,128)(2,1)S(1)}, u32[]{:S(2)}, u32[]{:S(2)}) async-start(bf16[16,88,256]{2,1,0:T(8,128)(2,1)} %output.6), calls=%async_computation.5 | async-start | bytes 1441792 | tf_op jit(solution)/shard_map/all_to_all | solution.py:243
  375.3 5.6 %collective-permute-start.73 = (bf16[128,2304]{1,0:T(8,128)(2,1)S(1)}, bf16[128,2304]{1,0:T(8,128)(2,1)S(1)}, u32[]{:S(2)}, u32[]{:S(2)}) collective-permute-start(bf16[128,2304]{1,0:T(8,128)(2,1)S(1)} %get-tuple-element.348.refs_5_.refs_13_), channel_id=1, source_target_pairs={{0,1},{1,0},{2,3},{3,2},{4,5},{5,4},{6,7},{7,6},{8,9},{9,8},{10,11... | collective-permute-start | bytes 1769480 | tf_op jit(solution)/shard_map/ppermute | solution.py:263
  380.9 5.1 %collective-permute-start.75 = (bf16[128,2304]{1,0:T(8,128)(2,1)S(1)}, bf16[128,2304]{1,0:T(8,128)(2,1)}, u32[]{:S(2)}, u32[]{:S(2)}) collective-permute-start(bf16[128,2304]{1,0:T(8,128)(2,1)S(1)} %collective-permute-done.61.refs_9_.refs_17_), channel_id=1, source_target_pairs={{0,1},{1,0},{2,3},{3,2},{4,5},{5,4},{6,7},{7,6},{8,9},{9,8},{10,11... | collective-permute-start | bytes 1769480 | tf_op jit(solution)/shard_map/ppermute | solution.py:263
  406.5 4.9 %project.7 = bf16[16,352,128]{2,1,0:T(8,128)(2,1)} custom-call(s32[3]{0:T(128)S(1)} %pad_add_fusion.scalars, bf16[88,256]{1,0:T(8,128)(2,1)S(1)} %close.6.refs_0_.x_ref, bf16[88,256]{1,0:T(8,128)(2,1)S(1)} %collective-permute-done.67.refs_1_, bf16[88,256]{1,0:T(8,128)(2,1)S(1)} %collective-permute-done.68.refs_2_, ...), custom_call_target="tpu_custom_call" | custom-call | flops 415236096 | bytes 6500000 | tf_op jit(solution)/shard_map/project/pallas_call | solution.py:131
  415.9 5.3 %collective-permute-start.80 = (bf16[64,4096]{1,0:T(8,128)(2,1)S(1)}, bf16[64,4096]{1,0:T(8,128)(2,1)S(1)}, u32[]{:S(2)}, u32[]{:S(2)}) collective-permute-start(bf16[64,4096]{1,0:T(8,128)(2,1)S(1)} %copy-done.9), channel_id=1, source_target_pairs={{0,1},{1,0},{2,3},{3,2},{4,5},{5,4},{6,7},{7,6},{8,9},{9,8},{10,11... | collective-permute-start | bytes 1572872 | tf_op jit(solution)/shard_map/ppermute | solution.py:263
  421.8 7.5 %all-to-all-done.6.recv_ref = bf16[16,352,128]{2,1,0:T(8,128)(2,1)S(1)} async-done(((bf16[16,352,128]{2,1,0:T(8,128)(2,1)}), bf16[16,352,128]{2,1,0:T(8,128)(2,1)S(1)}, u32[]{:S(2)}, u32[]{:S(2)}) %all-to-all-start.6) | async-done | bytes 1441824 | tf_op jit(solution)/shard_map/all_to_all | solution.py:243
  441.1 7.6 %all-to-all-start.7 = ((bf16[16,88,256]{2,1,0:T(8,128)(2,1)}), bf16[16,88,256]{2,1,0:T(8,128)(2,1)S(1)}, u32[]{:S(2)}, u32[]{:S(2)}) async-start(bf16[16,88,256]{2,1,0:T(8,128)(2,1)} %output.7), calls=%async_computation.7 | async-start | bytes 1441792 | tf_op jit(solution)/shard_map/all_to_all | solution.py:243
  448.7 7.7 %all-to-all-done.7.recv_ref = bf16[16,88,256]{2,1,0:T(8,128)(2,1)S(1)} async-done(((bf16[16,88,256]{2,1,0:T(8,128)(2,1)}), bf16[16,88,256]{2,1,0:T(8,128)(2,1)S(1)}, u32[]{:S(2)}, u32[]{:S(2)}) %all-to-all-start.7) | async-done | bytes 720928 | tf_op jit(solution)/shard_map/all_to_all | solution.py:243
  456.6 12.5 %collective-permute-start.84 = (bf16[88,256]{1,0:T(8,128)(2,1)S(1)}, bf16[88,256]{1,0:T(8,128)(2,1)S(1)}, u32[]{:S(2)}, u32[]{:S(2)}) collective-permute-start(bf16[88,256]{1,0:T(8,128)(2,1)S(1)} %get-tuple-element.373), channel_id=1, source_target_pairs={{0,0},{1,64},{2,32},{3,96},{4,1},{5,65},{6,33},{7,97},{8,2},{9,66}... | collective-permute-start | bytes 135176 | tf_op jit(solution)/shard_map/ppermute | solution.py:326
  (282 shorter events, 279.3 us)
Async XLA Ops:
  15.6 38.8 %collective-permute-start.4 = (bf16[64,4096]{1,0:T(8,128)(2,1)}, bf16[64,4096]{1,0:T(8,128)(2,1)S(1)}, u32[]{:S(2)}, u32[]{:S(2)}) collective-permute-start(bf16[64,4096]{1,0:T(8,128)(2,1)} %get-tuple-element.212), channel_id=1, source_target_pairs={{0,2},{2,4},{4,6},{6,0},{1,3},{3,5},{5,7},{7,1},{8,10},{10,12},{12... | collective-permute-start | bytes 1572872 | tf_op jit(solution)/shard_map/ppermute | solution.py:247
  18.1 40.7 %collective-permute-start.11 = (bf16[128,2304]{1,0:T(8,128)(2,1)S(1)}, bf16[128,2304]{1,0:T(8,128)(2,1)}, u32[]{:S(2)}, u32[]{:S(2)}) collective-permute-start(bf16[128,2304]{1,0:T(8,128)(2,1)S(1)} %get-tuple-element.220), channel_id=1, source_target_pairs={{0,32},{32,64},{64,96},{96,0},{1,33},{33,65},{65,97},{97,1},{2,34}... | collective-permute-start | bytes 1769480 | tf_op jit(solution)/shard_map/ppermute | solution.py:247
  19.8 39.1 %collective-permute-start.13 = (bf16[128,2304]{1,0:T(8,128)(2,1)S(1)}, bf16[128,2304]{1,0:T(8,128)(2,1)}, u32[]{:S(2)}, u32[]{:S(2)}) collective-permute-start(bf16[128,2304]{1,0:T(8,128)(2,1)S(1)} %get-tuple-element.221), channel_id=1, source_target_pairs={{0,64},{32,96},{64,0},{96,32},{1,65},{33,97},{65,1},{97,33},{2,66}... | collective-permute-start | bytes 1769480 | tf_op jit(solution)/shard_map/ppermute | solution.py:247
  23.1 36.2 %collective-permute-start.15 = (bf16[128,2304]{1,0:T(8,128)(2,1)S(1)}, bf16[128,2304]{1,0:T(8,128)(2,1)}, u32[]{:S(2)}, u32[]{:S(2)}) collective-permute-start(bf16[128,2304]{1,0:T(8,128)(2,1)S(1)} %get-tuple-element.222), channel_id=1, source_target_pairs={{0,96},{32,0},{64,32},{96,64},{1,97},{33,1},{65,33},{97,65},{2,98}... | collective-permute-start | bytes 1769480 | tf_op jit(solution)/shard_map/ppermute | solution.py:247
  54.4 44.7 %collective-permute-start.10 = (bf16[128,2304]{1,0:T(8,128)(2,1)S(1)}, bf16[128,2304]{1,0:T(8,128)(2,1)}, u32[]{:S(2)}, u32[]{:S(2)}) collective-permute-start(bf16[128,2304]{1,0:T(8,128)(2,1)S(1)} %get-tuple-element.219.refs_5_.refs_13_), channel_id=1, source_target_pairs={{0,1},{1,0},{2,3},{3,2},{4,5},{5,4},{6,7},{7,6},{8,9},{9,8},{10,11... | collective-permute-start | bytes 1769480 | tf_op jit(solution)/shard_map/ppermute | solution.py:263
  58.7 40.4 %collective-permute-start.12 = (bf16[128,2304]{1,0:T(8,128)(2,1)}, bf16[128,2304]{1,0:T(8,128)(2,1)}, u32[]{:S(2)}, u32[]{:S(2)}) collective-permute-start(bf16[128,2304]{1,0:T(8,128)(2,1)} %collective-permute-done.11.refs_7_.refs_15_), channel_id=1, source_target_pairs={{0,1},{1,0},{2,3},{3,2},{4,5},{5,4},{6,7},{7,6},{8,9},{9,8},{10,11... | collective-permute-start | bytes 1769480 | tf_op jit(solution)/shard_map/ppermute | solution.py:263
  58.8 40.3 %collective-permute-start.14 = (bf16[128,2304]{1,0:T(8,128)(2,1)}, bf16[128,2304]{1,0:T(8,128)(2,1)}, u32[]{:S(2)}, u32[]{:S(2)}) collective-permute-start(bf16[128,2304]{1,0:T(8,128)(2,1)} %collective-permute-done.13.refs_9_.refs_17_), channel_id=1, source_target_pairs={{0,1},{1,0},{2,3},{3,2},{4,5},{5,4},{6,7},{7,6},{8,9},{9,8},{10,11... | collective-permute-start | bytes 1769480 | tf_op jit(solution)/shard_map/ppermute | solution.py:263
  59.3 39.9 %collective-permute-start.16 = (bf16[128,2304]{1,0:T(8,128)(2,1)}, bf16[128,2304]{1,0:T(8,128)(2,1)}, u32[]{:S(2)}, u32[]{:S(2)}) collective-permute-start(bf16[128,2304]{1,0:T(8,128)(2,1)} %collective-permute-done.15.refs_11_.refs_19_), channel_id=1, source_target_pairs={{0,1},{1,0},{2,3},{3,2},{4,5},{5,4},{6,7},{7,6},{8,9},{9,8},{10,11... | collective-permute-start | bytes 1769480 | tf_op jit(solution)/shard_map/ppermute | solution.py:263
  66.7 32.4 %collective-permute-start.6 = (bf16[64,4096]{1,0:T(8,128)(2,1)}, bf16[64,4096]{1,0:T(8,128)(2,1)S(1)}, u32[]{:S(2)}, u32[]{:S(2)}) collective-permute-start(bf16[64,4096]{1,0:T(8,128)(2,1)} %get-tuple-element.214), channel_id=1, source_target_pairs={{0,6},{2,0},{4,2},{6,4},{1,7},{3,1},{5,3},{7,5},{8,14},{10,8},{12,... | collective-permute-start | bytes 1572872 | tf_op jit(solution)/shard_map/ppermute | solution.py:247
  104.3 42.4 %all-to-all-start = ((bf16[16,352,128]{2,1,0:T(8,128)(2,1)}), bf16[16,352,128]{2,1,0:T(8,128)(2,1)S(1)}, u32[]{:S(2)}, u32[]{:S(2)}) async-start(bf16[16,352,128]{2,1,0:T(8,128)(2,1)} %project.4), calls=%async_computation | async-start | bytes 2883584 | tf_op jit(solution)/shard_map/all_to_all | solution.py:243
  118.7 39.5 %collective-permute-start.23 = (bf16[64,4096]{1,0:T(8,128)(2,1)}, bf16[64,4096]{1,0:T(8,128)(2,1)}, u32[]{:S(2)}, u32[]{:S(2)}) collective-permute-start(bf16[64,4096]{1,0:T(8,128)(2,1)} %copy-done.12), channel_id=1, source_target_pairs={{0,1},{1,0},{2,3},{3,2},{4,5},{5,4},{6,7},{7,6},{8,9},{9,8},{10,11... | collective-permute-start | bytes 1572872 | tf_op jit(solution)/shard_map/ppermute | solution.py:263
  122.1 36.1 %collective-permute-start.24 = (bf16[64,4096]{1,0:T(8,128)(2,1)}, bf16[64,4096]{1,0:T(8,128)(2,1)}, u32[]{:S(2)}, u32[]{:S(2)}) collective-permute-start(bf16[64,4096]{1,0:T(8,128)(2,1)} %copy-done.14), channel_id=1, source_target_pairs={{0,1},{1,0},{2,3},{3,2},{4,5},{5,4},{6,7},{7,6},{8,9},{9,8},{10,11... | collective-permute-start | bytes 1572872 | tf_op jit(solution)/shard_map/ppermute | solution.py:263
  172.7 32.1 %collective-permute-start.33 = (bf16[128,2304]{1,0:T(8,128)(2,1)S(1)}, bf16[128,2304]{1,0:T(8,128)(2,1)}, u32[]{:S(2)}, u32[]{:S(2)}) collective-permute-start(bf16[128,2304]{1,0:T(8,128)(2,1)S(1)} %copy-done.3), channel_id=1, source_target_pairs={{0,1},{1,0},{2,3},{3,2},{4,5},{5,4},{6,7},{7,6},{8,9},{9,8},{10,11... | collective-permute-start | bytes 1769480 | tf_op jit(solution)/shard_map/ppermute | solution.py:263
  210.8 34.9 %all-to-all-start.2 = ((bf16[16,352,128]{2,1,0:T(8,128)(2,1)}), bf16[16,352,128]{2,1,0:T(8,128)(2,1)S(1)}, u32[]{:S(2)}, u32[]{:S(2)}) async-start(bf16[16,352,128]{2,1,0:T(8,128)(2,1)} %project.5), calls=%async_computation.2 | async-start | bytes 2883584 | tf_op jit(solution)/shard_map/all_to_all | solution.py:243
  217.7 39.5 %collective-permute-start.43 = (bf16[64,4096]{1,0:T(8,128)(2,1)}, bf16[64,4096]{1,0:T(8,128)(2,1)}, u32[]{:S(2)}, u32[]{:S(2)}) collective-permute-start(bf16[64,4096]{1,0:T(8,128)(2,1)} %copy-done.16), channel_id=1, source_target_pairs={{0,1},{1,0},{2,3},{3,2},{4,5},{5,4},{6,7},{7,6},{8,9},{9,8},{10,11... | collective-permute-start | bytes 1572872 | tf_op jit(solution)/shard_map/ppermute | solution.py:263
  223.5 33.7 %collective-permute-start.44 = (bf16[64,4096]{1,0:T(8,128)(2,1)}, bf16[64,4096]{1,0:T(8,128)(2,1)}, u32[]{:S(2)}, u32[]{:S(2)}) collective-permute-start(bf16[64,4096]{1,0:T(8,128)(2,1)} %collective-permute-done.30.refs_6_), channel_id=1, source_target_pairs={{0,1},{1,0},{2,3},{3,2},{4,5},{5,4},{6,7},{7,6},{8,9},{9,8},{10,11... | collective-permute-start | bytes 1572872 | tf_op jit(solution)/shard_map/ppermute | solution.py:263
  226.1 31.1 %collective-permute-start.45 = (bf16[64,4096]{1,0:T(8,128)(2,1)}, bf16[64,4096]{1,0:T(8,128)(2,1)}, u32[]{:S(2)}, u32[]{:S(2)}) collective-permute-start(bf16[64,4096]{1,0:T(8,128)(2,1)} %collective-permute-done.31.refs_8_), channel_id=1, source_target_pairs={{0,1},{1,0},{2,3},{3,2},{4,5},{5,4},{6,7},{7,6},{8,9},{9,8},{10,11... | collective-permute-start | bytes 1572872 | tf_op jit(solution)/shard_map/ppermute | solution.py:263
  269.7 41.7 %collective-permute-start.53 = (bf16[128,2304]{1,0:T(8,128)(2,1)S(1)}, bf16[128,2304]{1,0:T(8,128)(2,1)}, u32[]{:S(2)}, u32[]{:S(2)}) collective-permute-start(bf16[128,2304]{1,0:T(8,128)(2,1)S(1)} %get-tuple-element.305.refs_5_.refs_13_), channel_id=1, source_target_pairs={{0,1},{1,0},{2,3},{3,2},{4,5},{5,4},{6,7},{7,6},{8,9},{9,8},{10,11... | collective-permute-start | bytes 1769480 | tf_op jit(solution)/shard_map/ppermute | solution.py:263
  275.3 36.1 %collective-permute-start.54 = (bf16[128,2304]{1,0:T(8,128)(2,1)S(1)}, bf16[128,2304]{1,0:T(8,128)(2,1)}, u32[]{:S(2)}, u32[]{:S(2)}) collective-permute-start(bf16[128,2304]{1,0:T(8,128)(2,1)S(1)} %collective-permute-done.40.refs_7_.refs_15_), channel_id=1, source_target_pairs={{0,1},{1,0},{2,3},{3,2},{4,5},{5,4},{6,7},{7,6},{8,9},{9,8},{10,11... | collective-permute-start | bytes 1769480 | tf_op jit(solution)/shard_map/ppermute | solution.py:263
  275.3 36.1 %collective-permute-start.55 = (bf16[128,2304]{1,0:T(8,128)(2,1)S(1)}, bf16[128,2304]{1,0:T(8,128)(2,1)}, u32[]{:S(2)}, u32[]{:S(2)}) collective-permute-start(bf16[128,2304]{1,0:T(8,128)(2,1)S(1)} %copy-done.7), channel_id=1, source_target_pairs={{0,1},{1,0},{2,3},{3,2},{4,5},{5,4},{6,7},{7,6},{8,9},{9,8},{10,11... | collective-permute-start | bytes 1769480 | tf_op jit(solution)/shard_map/ppermute | solution.py:263
  316.3 34.1 %all-to-all-start.4 = ((bf16[16,352,128]{2,1,0:T(8,128)(2,1)}), bf16[16,352,128]{2,1,0:T(8,128)(2,1)S(1)}, u32[]{:S(2)}, u32[]{:S(2)}) async-start(bf16[16,352,128]{2,1,0:T(8,128)(2,1)} %project.6), calls=%async_computation.4 | async-start | bytes 2883584 | tf_op jit(solution)/shard_map/all_to_all | solution.py:243
  323.3 38.6 %collective-permute-start.63 = (bf16[64,4096]{1,0:T(8,128)(2,1)}, bf16[64,4096]{1,0:T(8,128)(2,1)}, u32[]{:S(2)}, u32[]{:S(2)}) collective-permute-start(bf16[64,4096]{1,0:T(8,128)(2,1)} %copy-done.10), channel_id=1, source_target_pairs={{0,1},{1,0},{2,3},{3,2},{4,5},{5,4},{6,7},{7,6},{8,9},{9,8},{10,11... | collective-permute-start | bytes 1572872 | tf_op jit(solution)/shard_map/ppermute | solution.py:263
  329.1 32.8 %collective-permute-start.64 = (bf16[64,4096]{1,0:T(8,128)(2,1)}, bf16[64,4096]{1,0:T(8,128)(2,1)}, u32[]{:S(2)}, u32[]{:S(2)}) collective-permute-start(bf16[64,4096]{1,0:T(8,128)(2,1)} %collective-permute-done.50.refs_6_), channel_id=1, source_target_pairs={{0,1},{1,0},{2,3},{3,2},{4,5},{5,4},{6,7},{7,6},{8,9},{9,8},{10,11... | collective-permute-start | bytes 1572872 | tf_op jit(solution)/shard_map/ppermute | solution.py:263
  375.3 31.2 %collective-permute-start.73 = (bf16[128,2304]{1,0:T(8,128)(2,1)S(1)}, bf16[128,2304]{1,0:T(8,128)(2,1)S(1)}, u32[]{:S(2)}, u32[]{:S(2)}) collective-permute-start(bf16[128,2304]{1,0:T(8,128)(2,1)S(1)} %get-tuple-element.348.refs_5_.refs_13_), channel_id=1, source_target_pairs={{0,1},{1,0},{2,3},{3,2},{4,5},{5,4},{6,7},{7,6},{8,9},{9,8},{10,11... | collective-permute-start | bytes 1769480 | tf_op jit(solution)/shard_map/ppermute | solution.py:263
  (105 other events, 1213.5 us)
where the time goes:
time: 491 us; the launch traced here: 482 us
  starting transfers between devices  253 us (52%)
  waiting for transfers between devices  139 us (28%)
  Pallas kernels  67.2 us (14%)
  local copies, waits for them, and re-layouts  19.8 us (4%)
    ppermute x32, starting transfers between devices, swapped(): others = [lax.ppermute(piece, 'c', [(0, 1), (1, 0)]) for piece in pieces]  120 us
    ppermute x48, waiting for transfers between devices, shift(): return lax.ppermute(value, axis, [(i, (i + by) % 4) for i in range(4)])  119 us
    ppermute x48, starting transfers between devices, shift(): return lax.ppermute(value, axis, [(i, (i + by) % 4) for i in range(4)])  61 us
    all_to_all x8, starting transfers between devices, exchange(): return lax.all_to_all(value, axes, 0, 0, tiled=True)  44.8 us
    ppermute x8, starting transfers between devices, body(): rounds.append(lax.ppermute(piece, ALL, pairs))  27.7 us
    pallas_call x4, Pallas kernels, project(): pl.pallas_call(functools.partial(project_kernel, layer), grid=(4,), in_sp...  19.9 us
    pallas_call x4, Pallas kernels, output(): pl.pallas_call(output_kernel, grid=(4,), in_specs=[SMEM] + [whole(SEQ, HE...  17.9 us
    unnamed x66, local copies, waits for them, and re-layouts  17.2 us
  transfers between devices with their start and end apart: 96, of which 36 were waited for; matrix products, arithmetic and copies ran while one was open for 0% of the time, Pallas kernels for 6%

commit v1 on v0

v1 whole, which is shorter than its diff:
```python
import functools
import math

import jax
import jax.numpy as jnp
from jax import lax
from jax.experimental import pallas as pl
from jax.experimental.pallas import tpu as pltpu
from jax.sharding import Mesh, PartitionSpec as P


ALL = ("z", "x", "y", "c")
HEAD = 128
SEQ = 88
COLS = 256
WIDTH = 16384
SLAB = 2304
OCOLS = 4096
ROWS = 352
VMEM_LIMIT = 48 * 1024 * 1024
f32 = jnp.float32
bf16 = jnp.bfloat16
SMEM = pl.BlockSpec(memory_space=pltpu.SMEM)
PARAMS = pltpu.CompilerParams(vmem_limit_bytes=VMEM_LIMIT)


def dot(a, b, contract=((1,), (0,))):
    return lax.dot_general(a, b, (contract, ((), ())), preferred_element_type=f32)


def whole(*shape):
    return pl.BlockSpec(shape, lambda s: (0,) * len(shape))


def cost(flops, size):
    return pl.CostEstimate(flops=flops, bytes_accessed=size, transcendentals=0)


def masks():
    rows = lax.broadcasted_iota(jnp.int32, (SEQ, 128), 0)
    lanes = lax.broadcasted_iota(jnp.int32, (SEQ, 128), 1)
    return rows == lanes, lanes <= rows


def slab_in_kernel(scalars, q_ref, k_ref, v_ref, *outs):
    for k, out in enumerate(outs):
        at = lax.bitwise_xor(scalars[0], k)
        out[:, :2048] = q_ref[0, :, pl.ds(pl.multiple_of(at * 2048, 2048), 2048)]
        out[:, 2048:2176] = k_ref[0, :, pl.ds(pl.multiple_of(at * 128, 128), 128)]
        out[:, 2176:] = v_ref[0, :, pl.ds(pl.multiple_of(at * 128, 128), 128)]


def slab_in(layer, scalars, q, k, v):
    return pl.pallas_call(
        slab_in_kernel,
        grid=(2,),
        in_specs=[
            SMEM,
            pl.BlockSpec((1, 64, 8192), lambda s: (layer, s, 0)),
            pl.BlockSpec((1, 64, 512), lambda s: (layer, s, 0)),
            pl.BlockSpec((1, 64, 512), lambda s: (layer, s, 0)),
        ],
        out_specs=[pl.BlockSpec((64, SLAB), lambda s: (s, 0))] * 4,
        out_shape=[pltpu.HBM((128, SLAB), bf16)] * 4,
        compiler_params=PARAMS,
        cost_estimate=cost(0, 4_700_000),
        name="slab_in",
    )(scalars, q, k, v)


def slab_out_kernel(scalars, o_ref, *outs):
    for k, out in enumerate(outs):
        at = lax.bitwise_xor(scalars[1], k) * COLS
        for s in range(16):
            out[:, COLS * s : COLS * s + COLS] = o_ref[
                0, :, pl.ds(pl.multiple_of(at + 1024 * s, COLS), COLS)
            ]


def slab_out(layer, scalars, o):
    return pl.pallas_call(
        slab_out_kernel,
        grid=(2,),
        in_specs=[SMEM, pl.BlockSpec((1, 32, WIDTH), lambda s: (layer, s, 0))],
        out_specs=[pl.BlockSpec((32, OCOLS), lambda s: (s, 0))] * 4,
        out_shape=[pltpu.HBM((64, OCOLS), bf16)] * 4,
        compiler_params=PARAMS,
        cost_estimate=cost(0, 4_200_000),
        name="slab_out",
    )(scalars, o)


def join_kernel(*refs):
    for k, ref in enumerate(refs[:4]):
        refs[4][k] = ref[...]


def join(pieces):
    rows, columns = pieces[0].shape
    half = rows // 2
    return pl.pallas_call(
        join_kernel,
        grid=(2,),
        in_specs=[pl.BlockSpec((half, columns), lambda s: (s, 0))] * 4,
        out_specs=pl.BlockSpec((4, half, columns), lambda s: (0, s, 0)),
        out_shape=pltpu.HBM((4, rows, columns), bf16),
        compiler_params=PARAMS,
        cost_estimate=cost(0, 4_500_000),
        name="join",
    )(*pieces)


def project_kernel(layer, scalars, *refs):
    xs, pieces, refs = refs[:4], refs[4:8], refs[8:]
    gain_ref, own, other, kv_own, kv_other, out_ref, joined_ref, xg_ref, ss_ref, kv_ref = refs
    z, core = scalars[0], scalars[2]
    for k in range(4):
        joined_ref[k] = pieces[k][...]

    @pl.when(pl.program_id(0) == 0)
    def _():
        at = lax.broadcasted_iota(jnp.int32, (4, COLS), 0) == lax.bitwise_xor(z, layer)
        total = jnp.zeros((SEQ, 1), f32)
        low, high = [], []
        for k in range(4):
            wide = xs[k][...].astype(f32)
            total += jnp.sum(wide * wide, axis=1, keepdims=True)
            scaled = wide * jnp.sum(jnp.where(at, gain_ref[k], 0.0), axis=0, keepdims=True)
            low.append(scaled[:, :128])
            high.append(scaled[:, 128:])
        scaled = jnp.where(
            core == 1, jnp.concatenate(high + low, axis=1), jnp.concatenate(low + high, axis=1)
        )
        xg_ref[...] = scaled.astype(bf16)
        padded = jnp.concatenate([scaled, jnp.zeros((128 - SEQ, 1024), f32)], axis=0).astype(bf16)
        eye, _ = masks()
        row = jnp.sum(jnp.where(eye, total, 0.0), axis=0, keepdims=True)
        coarse = row.astype(bf16).astype(f32)
        which = lax.broadcasted_iota(jnp.int32, (8, 128), 0)
        ss_ref[...] = jnp.where(which == 0, coarse, jnp.where(which == 1, row - coarse, 0.0))
        kv = dot(padded[:, :512], kv_own[...].reshape(512, 256))
        kv += dot(padded[:, 512:], kv_other[...].reshape(512, 256))
        kv_ref[:128] = kv[:, :128].T
        kv_ref[128:] = kv[:, 128:].T

    q = dot(xg_ref[:, :512], own[...].reshape(512, 512))
    q += dot(xg_ref[:, 512:], other[...].reshape(512, 512))
    for h in range(4):
        out_ref[h] = jnp.concatenate(
            [kv_ref[...], ss_ref[...], q[:, HEAD * h : HEAD * h + HEAD]], axis=0
        ).astype(bf16)


def project(layer, scalars, xs, gains, weights, pieces):
    return pl.pallas_call(
        functools.partial(project_kernel, layer),
        grid=(4,),
        in_specs=[SMEM]
        + [whole(SEQ, COLS)] * 4
        + [pl.BlockSpec((64, 1024), lambda s: (0, s))] * 4
        + [whole(4, 4, COLS)]
        + [pl.BlockSpec((4, 128, 512), lambda s: (0, 0, s))] * 2
        + [pl.BlockSpec((4, 128, 256), lambda s: (0, 0, 8))] * 2,
        out_specs=[
            pl.BlockSpec((4, ROWS, 128), lambda s: (s, 0, 0)),
            pl.BlockSpec((4, 64, 1024), lambda s: (0, 0, s)),
        ],
        out_shape=[pltpu.HBM((16, ROWS, 128), bf16), pltpu.HBM((4, 64, OCOLS), bf16)],
        scratch_shapes=[
            pltpu.VMEM((SEQ, 1024), bf16),
            pltpu.VMEM((8, 128), f32),
            pltpu.VMEM((256, 128), f32),
        ],
        compiler_params=PARAMS,
        cost_estimate=cost(2 * SEQ * 1024 * SLAB, 10_000_000),
        name="project",
    )(scalars, *xs, *pieces, gains, *weights, *weights)


def attend_kernel(recv_ref, out_ref, acc):
    step = pl.program_id(0)

    @pl.when(step == 0)
    def _():
        acc[...] = jnp.sum(recv_ref[...].astype(f32), axis=0)

    @pl.when(step > 0)
    def _():
        acc[...] += jnp.sum(recv_ref[...].astype(f32), axis=0)

    @pl.when(step == 3)
    def _():
        total = acc[256:257] + acc[257:258]
        row = lax.rsqrt(total * (1.0 / WIDTH) + 1e-05)
        eye, causal = masks()
        column = jnp.sum(jnp.where(eye, row, 0.0), axis=1, keepdims=True)
        q = (acc[264:] * column).astype(bf16)
        keys = (acc[:128] * row).astype(bf16)
        values = (acc[128:256] * row).astype(bf16)
        scores = dot(q, keys) * (1.0 / math.sqrt(HEAD))
        weights = jnp.where(causal, jnp.exp(scores), 0.0)
        shares = (weights / jnp.sum(weights, axis=1, keepdims=True)).astype(bf16)
        out_ref[...] = dot(shares, values, ((1,), (1,))).astype(bf16)


def attend(received):
    return pl.pallas_call(
        attend_kernel,
        grid=(4,),
        in_specs=[pl.BlockSpec((4, ROWS, 128), lambda s: (s, 0, 0))],
        out_specs=whole(SEQ, HEAD),
        out_shape=jax.ShapeDtypeStruct((SEQ, HEAD), bf16),
        scratch_shapes=[pltpu.VMEM((ROWS, 128), f32)],
        compiler_params=PARAMS,
        cost_estimate=cost(6_000_000, 1_500_000),
        name="attend",
    )(received)


def output_kernel(scalars, *refs):
    mixed, own, other, mixed_ref = refs[:4], refs[4], refs[5], refs[-1]
    if len(refs) == 8:
        out_ref = refs[6]
    else:
        pieces, out_ref, joined_ref = refs[6:10], refs[10], refs[11]
        for k in range(4):
            joined_ref[k] = pieces[k][...]

    @pl.when(pl.program_id(0) == 0)
    def _():
        parts = [part[...].astype(f32) for part in mixed]
        low, high = [part[:, :64] for part in parts], [part[:, 64:] for part in parts]
        mixed_ref[...] = jnp.where(
            scalars[2] == 1, jnp.concatenate(high + low, axis=1), jnp.concatenate(low + high, axis=1)
        ).astype(bf16)

    o = dot(mixed_ref[:, :256], own[...].reshape(256, 1024))
    o += dot(mixed_ref[:, 256:], other[...].reshape(256, 1024))
    for i in range(4):
        out_ref[i] = o[:, COLS * i : COLS * i + COLS].astype(bf16)


def output(scalars, mixed, weights, pieces):
    specs = [SMEM] + [whole(SEQ, HEAD)] * 4 + [pl.BlockSpec((4, 64, 1024), lambda s: (0, 0, s))] * 2
    outs = [pltpu.HBM((16, SEQ, COLS), bf16)]
    out_specs = [pl.BlockSpec((4, SEQ, COLS), lambda s: (s, 0, 0))]
    if pieces:
        specs += [pl.BlockSpec((32, SLAB), lambda s: (s, 0))] * 4
        outs.append(pltpu.HBM((4, 128, SLAB), bf16))
        out_specs.append(pl.BlockSpec((4, 32, SLAB), lambda s: (0, s, 0)))
    return pl.pallas_call(
        output_kernel,
        grid=(4,),
        in_specs=specs,
        out_specs=out_specs,
        out_shape=outs,
        scratch_shapes=[pltpu.VMEM((SEQ, 512), bf16)],
        compiler_params=PARAMS,
        cost_estimate=cost(2 * SEQ * 512 * OCOLS, 10_000_000),
        name="output",
    )(scalars, *mixed, *weights, *pieces)


def close_kernel(recv_ref, x_ref, out_ref):
    out_ref[...] = (x_ref[...].astype(f32) + jnp.sum(recv_ref[...].astype(f32), axis=0)).astype(bf16)


def close(received, x):
    return pl.pallas_call(
        close_kernel,
        grid=(1,),
        in_specs=[whole(16, SEQ, COLS), whole(SEQ, COLS)],
        out_specs=whole(SEQ, COLS),
        out_shape=jax.ShapeDtypeStruct((SEQ, COLS), bf16),
        compiler_params=PARAMS,
        cost_estimate=cost(400_000, 800_000),
        name="close",
    )(received, x)


def exchange(value, axes):
    return lax.all_to_all(value, axes, 0, 0, tiled=True)


def across_line(value, axis, by):
    return lax.ppermute(value, axis, [(i, i ^ by) for i in range(4)])


def line(value, axis):
    near, far = (across_line(value, axis, by) for by in (1, 2))
    return [value, near, far, across_line(near, axis, 2)]


def after(gate, values):
    return lax.optimization_barrier((gate, values))


def relay(slabs, axis):
    return [slabs[0]] + [across_line(slabs[k], axis, k) for k in range(1, 4)]


def swapped(joined):
    return joined, lax.ppermute(joined, "c", [(0, 1), (1, 0)])


def body(entering, norm_gain, query_weight, key_matrix, value_matrix, output_weight):
    plane, across, along, core = (lax.axis_index(name) for name in ALL)
    slot = 2 * core + lax.rem(along, 2)
    scalars = jnp.stack([plane, along, core]).astype(jnp.int32)

    gains = jnp.concatenate(line(norm_gain, "z"), axis=0)
    slab = slab_in(0, scalars, query_weight, key_matrix, value_matrix)
    gains, slab = after(gains, slab)
    ins = relay(slab, "z")

    rounds = []
    for r in range(4):
        pairs = []
        for p in range(4):
            for t in range(32):
                s = (t // 8 - r) % 4
                pairs.append((32 * p + t, 32 * p + 2 * ((2 * t) % 16 + s % 2) + s // 2))
        s = lax.rem(across - r + 4, 4)
        piece = lax.dynamic_slice(entering, (s // 2, 0, lax.rem(s, 2) * COLS), (1, SEQ, COLS))[0]
        gain = lax.dynamic_slice(gains, (0, lax.rem(s, 2) * COLS), (4, COLS))
        piece = jnp.concatenate([piece, gain, gain], axis=0)
        rounds.append(lax.ppermute(piece, ALL, pairs))
    rounds = jnp.stack(rounds)
    rounds, scalars = after(rounds, scalars)
    cut = slab_out(0, scalars, output_weight)
    outs = relay(cut, "y")
    lines = [
        lax.dynamic_index_in_dim(rounds, lax.rem(lax.bitwise_xor(plane, k) - slot + 4, 4), 0, keepdims=False)
        for k in range(4)
    ]
    xs = [part[:SEQ] for part in lines]
    gains = jnp.stack([part[SEQ : SEQ + 4] for part in lines]).astype(f32)

    slabs = [slab_in(layer, scalars, query_weight, key_matrix, value_matrix) for layer in range(1, 4)]
    cuts = [slab_out(layer, scalars, output_weight) for layer in range(1, 4)]
    ins, (outs, slabs, cuts) = after(ins, (outs, slabs, cuts))
    ins = swapped(join(ins))
    states = []
    for layer in range(4):
        xs, outs = after(xs, outs)
        partial, outs = project(layer, scalars, xs, gains, ins, outs)
        if layer < 3:
            partial, slab = after(partial, slabs[layer])
            ins = relay(slab, "z")
        received, outs = after(exchange(partial, ("x", "y")), swapped(outs))
        mixed = line(attend(received), "y")
        if layer < 3:
            mixed, ins = after(mixed, ins)
            partial, ins = output(scalars, mixed, outs, ins)
            partial, cut = after(partial, cuts[layer])
            outs = relay(cut, "y")
            ins = swapped(ins)
        else:
            partial = output(scalars, mixed, outs, [])[0]
        x = close(exchange(partial, ("z", "x")), xs[0])
        states.append(x)
        if layer < 3:
            xs = line(x, "z")

    states = jnp.stack(states)
    rounds = []
    for k in range(4):
        pairs = [
            (2 * i + c, 32 * ((2 * c + i % 2 + k) % 4) + i // 2) for i in range(64) for c in range(2)
        ]
        piece = lax.dynamic_index_in_dim(states, lax.rem(slot + k, 4), 0, keepdims=False)
        rounds.append(lax.ppermute(piece, ALL, pairs))
    rounds = jnp.stack(rounds)
    pieces = [
        lax.dynamic_index_in_dim(rounds, lax.rem(plane - s + 4, 4), 0, keepdims=False) for s in range(4)
    ]
    return jnp.stack(
        [jnp.concatenate(pieces[:2], axis=1), jnp.concatenate(pieces[2:], axis=1)]
    )[None]


def solution(mesh):
    fine = Mesh(mesh.devices.reshape(4, 4, 4, 2), ALL)
    tp = ("x", "y", "c")
    rows = P(None, ALL, None)
    return jax.shard_map(
        body,
        mesh=fine,
        in_specs=(P(None, None, tp), P("z", tp), rows, rows, rows, rows),
        out_specs=P("z", None, None, tp),
        check_vma=False,
    )
```

time: 491 us -> 420 us (0.86); the launches traced: 482 us -> 416 us
  starting transfers between devices: 253 us -> 142 us
  waiting for transfers between devices: 139 us -> 168 us
  blocking collectives: 0 us -> 23.2 us
    ppermute x80 -> x56, starting transfers between devices: 181 us -> 76.8 us  [the longest x48 62.9 us: across_line(): return lax.ppermute(value, axis, [(i, i ^ by) for i in range(4)])]
    all_to_all x8 -> x7, waiting for transfers between devices: 15.2 us -> 77.1 us  [exchange(): return lax.all_to_all(value, axes, 0, 0, tiled=True)]
    ppermute x80 -> x56, waiting for transfers between devices: 119 us -> 77.1 us  [the longest x48 72.7 us: across_line(): return lax.ppermute(value, axis, [(i, i ^ by) for i in range(4)])]
    all_to_all x0 -> x1, blocking collectives: none -> 23.2 us  [exchange(): return lax.all_to_all(value, axes, 0, 0, tiled=True)]
    ppermute x8, waiting for transfers between devices: 5.59 us -> 13.6 us  [body(): rounds.append(lax.ppermute(piece, ALL, pairs))]
    all_to_all x8 -> x7, starting transfers between devices: 44.8 us -> 39 us  [exchange(): return lax.all_to_all(value, axes, 0, 0, tiled=True)]
    unnamed x66 -> x74, local copies, waits for them, and re-layouts: 17.2 us -> 14.8 us
    pallas_call x12 -> x13, Pallas kernels: 44.1 us -> 42.2 us  [the longest x4 18.4 us: output(): pl.pallas_call(output_kernel, grid=(4,), in_specs=specs, out_specs=out_sp...]
  transfers between devices with their start and end apart: 96 -> 71, of which waited for: 36 -> 34; matrix products, arithmetic and copies ran while one was open for 0% -> 0% of each run, Pallas kernels for 6% -> 5%
where the time goes in v1:
time: 420 us; the launch traced here: 416 us
  waiting for transfers between devices  168 us (40%)
  starting transfers between devices  142 us (34%)
  Pallas kernels  65.3 us (16%)
  blocking collectives  23.2 us (6%)
  local copies, waits for them, and re-layouts  15.7 us (4%)
    all_to_all x7, waiting for transfers between devices, exchange(): return lax.all_to_all(value, axes, 0, 0, tiled=True)  77.1 us
    ppermute x48, waiting for transfers between devices, across_line(): return lax.ppermute(value, axis, [(i, i ^ by) for i in range(4)])  72.7 us
    ppermute x48, starting transfers between devices, across_line(): return lax.ppermute(value, axis, [(i, i ^ by) for i in range(4)])  62.9 us
    all_to_all x7, starting transfers between devices, exchange(): return lax.all_to_all(value, axes, 0, 0, tiled=True)  39 us
    ppermute x8, starting transfers between devices, body(): rounds.append(lax.ppermute(piece, ALL, pairs))  26.5 us
    all_to_all x1, blocking collectives, exchange(): return lax.all_to_all(value, axes, 0, 0, tiled=True)  23.2 us
    pallas_call x4, Pallas kernels, project(): pl.pallas_call(functools.partial(project_kernel, layer), grid=(4,), in_sp...  20 us
    pallas_call x4, Pallas kernels, output(): pl.pallas_call(output_kernel, grid=(4,), in_specs=specs, out_specs=out_sp...  18.4 us
  transfers between devices with their start and end apart: 71, of which 34 were waited for; matrix products, arithmetic and copies ran while one was open for 0% of the time, Pallas kernels for 5%

profile of v1, /device:TPU:5, one launch (start us, length us, event | category | flops | bytes accessed | tf_op | source)
XLA Modules:
  0.0 415.8 jit_solution(13371485201340321406)
XLA Ops:
  22.3 5.8 %collective-permute-done.5 = bf16[96,256]{1,0:T(8,128)(2,1)S(1)} collective-permute-done((bf16[96,256]{1,0:T(8,128)(2,1)S(1)}, bf16[96,256]{1,0:T(8,128)(2,1)S(1)}, u32[]{:S(2)}, u32[]{:S(2)}) %collective-permute-start.5) | collective-permute-done | bytes 49184 | tf_op jit(solution)/shard_map/ppermute | solution.py:327
  36.0 10.2 %collective-permute-done.10.refs_5_ = bf16[64,4096]{1,0:T(8,128)(2,1)S(1)} collective-permute-done((bf16[64,4096]{1,0:T(8,128)(2,1)}, bf16[64,4096]{1,0:T(8,128)(2,1)S(1)}, u32[]{:S(2)}, u32[]{:S(2)}) %collective-permute-start.10) | collective-permute-done | bytes 524320 | tf_op jit(solution)/shard_map/ppermute | solution.py:286
  75.2 5.0 %project.4 = (bf16[16,352,128]{2,1,0:T(8,128)(2,1)}, bf16[4,64,4096]{2,1,0:T(8,128)(2,1)}) custom-call(s32[3]{0:T(128)S(1)} %pad_add_fusion.scalars, bf16[88,256]{1,0:T(8,128)(2,1)S(1)} %get-tuple-element.231.refs_0_.x_ref, bf16[88,256]{1,0:T(8,128)(2,1)S(1)} %get-tuple-element.232.refs_1_, bf16[88,256]{1,0:T(8,128)(2,1)S(1)} %get-tuple-element.233.refs_2_, ...), custom_call_target="tpu_custom_call" | custom-call | flops 415236096 | bytes 10000000 | tf_op jit(solution)/shard_map/project/pallas_call | solution.py:155
  80.6 8.3 %all-to-all-start = ((bf16[16,352,128]{2,1,0:T(8,128)(2,1)}), bf16[16,352,128]{2,1,0:T(8,128)(2,1)S(1)}, u32[]{:S(2)}, u32[]{:S(2)}) async-start(bf16[16,352,128]{2,1,0:T(8,128)(2,1)} %get-tuple-element.248), calls=%async_computation | async-start | bytes 2883584 | tf_op jit(solution)/shard_map/all_to_all | solution.py:282
  92.7 15.1 %all-to-all-done.recv_ref = bf16[16,352,128]{2,1,0:T(8,128)(2,1)S(1)} async-done(((bf16[16,352,128]{2,1,0:T(8,128)(2,1)}), bf16[16,352,128]{2,1,0:T(8,128)(2,1)S(1)}, u32[]{:S(2)}, u32[]{:S(2)}) %all-to-all-start) | async-done | bytes 1441824 | tf_op jit(solution)/shard_map/all_to_all | solution.py:282
  120.2 5.1 %output.4 = (bf16[16,88,256]{2,1,0:T(8,128)(2,1)}, bf16[4,128,2304]{2,1,0:T(8,128)(2,1)}) custom-call(s32[3]{0:T(128)S(1)} %copy-done.27, bf16[88,128]{1,0:T(8,128)(2,1)S(1)} %attend.4.refs_0_, bf16[88,128]{1,0:T(8,128)(2,1)S(1)} %collective-permute-done.15.refs_1_, bf16[88,128]{1,0:T(8,128)(2,1)S(1)} %collective-permute-done.16.refs_2_, ...), custom_call_target="tpu_custom_call" | custom-call | flops 369098752 | bytes 10000000 | tf_op jit(solution)/shard_map/output/pallas_call | solution.py:251
  127.6 6.0 %all-to-all-start.1 = ((bf16[16,88,256]{2,1,0:T(8,128)(2,1)}), bf16[16,88,256]{2,1,0:T(8,128)(2,1)S(1)}, u32[]{:S(2)}, u32[]{:S(2)}) async-start(bf16[16,88,256]{2,1,0:T(8,128)(2,1)} %get-tuple-element.270), calls=%async_computation.1 | async-start | bytes 1441792 | tf_op jit(solution)/shard_map/all_to_all | solution.py:282
  137.4 7.9 %all-to-all-done.1.recv_ref = bf16[16,88,256]{2,1,0:T(8,128)(2,1)S(1)} async-done(((bf16[16,88,256]{2,1,0:T(8,128)(2,1)}), bf16[16,88,256]{2,1,0:T(8,128)(2,1)S(1)}, u32[]{:S(2)}, u32[]{:S(2)}) %all-to-all-start.1) | async-done | bytes 720928 | tf_op jit(solution)/shard_map/all_to_all | solution.py:282
  150.3 9.6 %collective-permute-done.25.refs_6_ = bf16[64,4096]{1,0:T(8,128)(2,1)S(1)} collective-permute-done((bf16[64,4096]{1,0:T(8,128)(2,1)}, bf16[64,4096]{1,0:T(8,128)(2,1)S(1)}, u32[]{:S(2)}, u32[]{:S(2)}) %collective-permute-start.25) | collective-permute-done | bytes 524320 | tf_op jit(solution)/shard_map/ppermute | solution.py:286
  163.6 5.0 %project.5 = (bf16[16,352,128]{2,1,0:T(8,128)(2,1)}, bf16[4,64,4096]{2,1,0:T(8,128)(2,1)}) custom-call(s32[3]{0:T(128)S(1)} %copy-done.28, bf16[88,256]{1,0:T(8,128)(2,1)S(1)} %close.4.refs_0_.x_ref, bf16[88,256]{1,0:T(8,128)(2,1)S(1)} %collective-permute-done.21.refs_1_, bf16[88,256]{1,0:T(8,128)(2,1)S(1)} %collective-permute-done.22.refs_2_, ...), custom_call_target="tpu_custom_call" | custom-call | flops 415236096 | bytes 10000000 | tf_op jit(solution)/shard_map/project/pallas_call | solution.py:155
  179.0 15.2 %all-to-all-done.2.recv_ref = bf16[16,352,128]{2,1,0:T(8,128)(2,1)S(1)} async-done(((bf16[16,352,128]{2,1,0:T(8,128)(2,1)}), bf16[16,352,128]{2,1,0:T(8,128)(2,1)S(1)}, u32[]{:S(2)}, u32[]{:S(2)}) %all-to-all-start.2) | async-done | bytes 1441824 | tf_op jit(solution)/shard_map/all_to_all | solution.py:282
  208.3 5.1 %output.5 = (bf16[16,88,256]{2,1,0:T(8,128)(2,1)}, bf16[4,128,2304]{2,1,0:T(8,128)(2,1)}) custom-call(s32[3]{0:T(128)S(1)} %copy-done.29, bf16[88,128]{1,0:T(8,128)(2,1)S(1)} %attend.5.refs_0_, bf16[88,128]{1,0:T(8,128)(2,1)S(1)} %collective-permute-done.29.refs_1_, bf16[88,128]{1,0:T(8,128)(2,1)S(1)} %collective-permute-done.30.refs_2_, ...), custom_call_target="tpu_custom_call" | custom-call | flops 369098752 | bytes 10000000 | tf_op jit(solution)/shard_map/output/pallas_call | solution.py:251
  223.9 7.9 %all-to-all-done.3.recv_ref = bf16[16,88,256]{2,1,0:T(8,128)(2,1)S(1)} async-done(((bf16[16,88,256]{2,1,0:T(8,128)(2,1)}), bf16[16,88,256]{2,1,0:T(8,128)(2,1)S(1)}, u32[]{:S(2)}, u32[]{:S(2)}) %all-to-all-start.3) | async-done | bytes 720928 | tf_op jit(solution)/shard_map/all_to_all | solution.py:282
  236.1 10.1 %collective-permute-done.39.refs_6_ = bf16[64,4096]{1,0:T(8,128)(2,1)S(1)} collective-permute-done((bf16[64,4096]{1,0:T(8,128)(2,1)}, bf16[64,4096]{1,0:T(8,128)(2,1)S(1)}, u32[]{:S(2)}, u32[]{:S(2)}) %collective-permute-start.39) | collective-permute-done | bytes 524320 | tf_op jit(solution)/shard_map/ppermute | solution.py:286
  250.0 5.0 %project.6 = (bf16[16,352,128]{2,1,0:T(8,128)(2,1)}, bf16[4,64,4096]{2,1,0:T(8,128)(2,1)}) custom-call(s32[3]{0:T(128)S(1)} %copy-done.30, bf16[88,256]{1,0:T(8,128)(2,1)S(1)} %close.5.refs_0_.x_ref, bf16[88,256]{1,0:T(8,128)(2,1)S(1)} %collective-permute-done.35.refs_1_, bf16[88,256]{1,0:T(8,128)(2,1)S(1)} %collective-permute-done.36.refs_2_, ...), custom_call_target="tpu_custom_call" | custom-call | flops 415236096 | bytes 10000000 | tf_op jit(solution)/shard_map/project/pallas_call | solution.py:155
  265.6 15.2 %all-to-all-done.4.recv_ref = bf16[16,352,128]{2,1,0:T(8,128)(2,1)S(1)} async-done(((bf16[16,352,128]{2,1,0:T(8,128)(2,1)}), bf16[16,352,128]{2,1,0:T(8,128)(2,1)S(1)}, u32[]{:S(2)}, u32[]{:S(2)}) %all-to-all-start.4) | async-done | bytes 1441824 | tf_op jit(solution)/shard_map/all_to_all | solution.py:282
  294.9 5.1 %output.6 = (bf16[16,88,256]{2,1,0:T(8,128)(2,1)}, bf16[4,128,2304]{2,1,0:T(8,128)(2,1)}) custom-call(s32[3]{0:T(128)S(1)} %copy-done.31, bf16[88,128]{1,0:T(8,128)(2,1)S(1)} %attend.6.refs_0_, bf16[88,128]{1,0:T(8,128)(2,1)S(1)} %collective-permute-done.43.refs_1_, bf16[88,128]{1,0:T(8,128)(2,1)S(1)} %collective-permute-done.44.refs_2_, ...), custom_call_target="tpu_custom_call" | custom-call | flops 369098752 | bytes 10000000 | tf_op jit(solution)/shard_map/output/pallas_call | solution.py:251
  310.5 7.9 %all-to-all-done.5.recv_ref = bf16[16,88,256]{2,1,0:T(8,128)(2,1)S(1)} async-done(((bf16[16,88,256]{2,1,0:T(8,128)(2,1)}), bf16[16,88,256]{2,1,0:T(8,128)(2,1)S(1)}, u32[]{:S(2)}, u32[]{:S(2)}) %all-to-all-start.5) | async-done | bytes 720928 | tf_op jit(solution)/shard_map/all_to_all | solution.py:282
  322.6 10.2 %collective-permute-done.53.refs_6_ = bf16[64,4096]{1,0:T(8,128)(2,1)S(1)} collective-permute-done((bf16[64,4096]{1,0:T(8,128)(2,1)}, bf16[64,4096]{1,0:T(8,128)(2,1)S(1)}, u32[]{:S(2)}, u32[]{:S(2)}) %collective-permute-start.53) | collective-permute-done | bytes 524320 | tf_op jit(solution)/shard_map/ppermute | solution.py:286
  336.5 5.0 %project.7 = (bf16[16,352,128]{2,1,0:T(8,128)(2,1)}, bf16[4,64,4096]{2,1,0:T(8,128)(2,1)}) custom-call(s32[3]{0:T(128)S(1)} %copy-done.32, bf16[88,256]{1,0:T(8,128)(2,1)S(1)} %close.6.refs_0_.x_ref, bf16[88,256]{1,0:T(8,128)(2,1)S(1)} %collective-permute-done.49.refs_1_, bf16[88,256]{1,0:T(8,128)(2,1)S(1)} %collective-permute-done.50.refs_2_, ...), custom_call_target="tpu_custom_call" | custom-call | flops 415236096 | bytes 10000000 | tf_op jit(solution)/shard_map/project/pallas_call | solution.py:155
  343.7 23.2 %all_to_all.40.recv_ref = bf16[16,352,128]{2,1,0:T(8,128)(2,1)S(1)} all-to-all(bf16[16,352,128]{2,1,0:T(8,128)(2,1)} %get-tuple-element.366), channel_id=1, replica_groups=mesh['z'=4,'x'=4,'y'=4,'c'=2] {'x','y'}, dimensions={0} | all-to-all | bytes 2883584 | tf_op jit(solution)/shard_map/all_to_all | solution.py:282
  378.0 6.8 %all-to-all-start.7 = ((bf16[16,88,256]{2,1,0:T(8,128)(2,1)}), bf16[16,88,256]{2,1,0:T(8,128)(2,1)S(1)}, u32[]{:S(2)}, u32[]{:S(2)}) async-start(bf16[16,88,256]{2,1,0:T(8,128)(2,1)} %output.7), calls=%async_computation.7 | async-start | bytes 1441792 | tf_op jit(solution)/shard_map/all_to_all | solution.py:282
  384.8 7.7 %all-to-all-done.7.recv_ref = bf16[16,88,256]{2,1,0:T(8,128)(2,1)S(1)} async-done(((bf16[16,88,256]{2,1,0:T(8,128)(2,1)}), bf16[16,88,256]{2,1,0:T(8,128)(2,1)S(1)}, u32[]{:S(2)}, u32[]{:S(2)}) %all-to-all-start.7) | async-done | bytes 720928 | tf_op jit(solution)/shard_map/all_to_all | solution.py:282
  392.7 10.4 %collective-permute-start.60 = (bf16[88,256]{1,0:T(8,128)(2,1)S(1)}, bf16[88,256]{1,0:T(8,128)(2,1)S(1)}, u32[]{:S(2)}, u32[]{:S(2)}) collective-permute-start(bf16[88,256]{1,0:T(8,128)(2,1)S(1)} %get-tuple-element.383), channel_id=1, source_target_pairs={{0,0},{1,64},{2,32},{3,96},{4,1},{5,65},{6,33},{7,97},{8,2},{9,66}... | collective-permute-start | bytes 135176 | tf_op jit(solution)/shard_map/ppermute | solution.py:372
  (236 shorter events, 202.4 us)
Async XLA Ops:
  32.0 35.0 %collective-permute-start.7 = (bf16[128,2304]{1,0:T(8,128)(2,1)S(1)}, bf16[128,2304]{1,0:T(8,128)(2,1)S(1)}, u32[]{:S(2)}, u32[]{:S(2)}) collective-permute-start(bf16[128,2304]{1,0:T(8,128)(2,1)S(1)} %copy-done.36), channel_id=1, source_target_pairs={{0,32},{32,0},{64,96},{96,64},{1,33},{33,1},{65,97},{97,65},{2,34}... | collective-permute-start | bytes 1769480 | tf_op jit(solution)/shard_map/ppermute | solution.py:286
  32.9 34.2 %collective-permute-start.8 = (bf16[128,2304]{1,0:T(8,128)(2,1)S(1)}, bf16[128,2304]{1,0:T(8,128)(2,1)S(1)}, u32[]{:S(2)}, u32[]{:S(2)}) collective-permute-start(bf16[128,2304]{1,0:T(8,128)(2,1)S(1)} %copy-done.35), channel_id=1, source_target_pairs={{0,64},{32,96},{64,0},{96,32},{1,65},{33,97},{65,1},{97,33},{2,66}... | collective-permute-start | bytes 1769480 | tf_op jit(solution)/shard_map/ppermute | solution.py:286
  34.3 32.8 %collective-permute-start.9 = (bf16[128,2304]{1,0:T(8,128)(2,1)S(1)}, bf16[128,2304]{1,0:T(8,128)(2,1)S(1)}, u32[]{:S(2)}, u32[]{:S(2)}) collective-permute-start(bf16[128,2304]{1,0:T(8,128)(2,1)S(1)} %copy-done.34), channel_id=1, source_target_pairs={{0,96},{32,64},{64,32},{96,0},{1,97},{33,65},{65,33},{97,1},{2,98}... | collective-permute-start | bytes 1769480 | tf_op jit(solution)/shard_map/ppermute | solution.py:286
  36.0 26.9 %collective-permute-start.11 = (bf16[64,4096]{1,0:T(8,128)(2,1)}, bf16[64,4096]{1,0:T(8,128)(2,1)S(1)}, u32[]{:S(2)}, u32[]{:S(2)}) collective-permute-start(bf16[64,4096]{1,0:T(8,128)(2,1)} %get-tuple-element.201), channel_id=1, source_target_pairs={{0,4},{2,6},{4,0},{6,2},{1,5},{3,7},{5,1},{7,3},{8,12},{10,14},{12... | collective-permute-start | bytes 1572872 | tf_op jit(solution)/shard_map/ppermute | solution.py:286
  80.2 27.7 %collective-permute-start.14 = (bf16[4,64,4096]{2,1,0:T(8,128)(2,1)}, bf16[4,64,4096]{2,1,0:T(8,128)(2,1)}, u32[]{:S(2)}, u32[]{:S(2)}) collective-permute-start(bf16[4,64,4096]{2,1,0:T(8,128)(2,1)} %get-tuple-element.259.refs_4_), channel_id=1, source_target_pairs={{0,1},{1,0},{2,3},{3,2},{4,5},{5,4},{6,7},{7,6},{8,9},{9,8},{10,11... | collective-permute-start | bytes 6291464 | tf_op jit(solution)/shard_map/ppermute | solution.py:303
  80.6 27.3 %all-to-all-start = ((bf16[16,352,128]{2,1,0:T(8,128)(2,1)}), bf16[16,352,128]{2,1,0:T(8,128)(2,1)S(1)}, u32[]{:S(2)}, u32[]{:S(2)}) async-start(bf16[16,352,128]{2,1,0:T(8,128)(2,1)} %get-tuple-element.248), calls=%async_computation | async-start | bytes 2883584 | tf_op jit(solution)/shard_map/all_to_all | solution.py:282
  88.9 24.9 %collective-permute-start.18 = (bf16[128,2304]{1,0:T(8,128)(2,1)}, bf16[128,2304]{1,0:T(8,128)(2,1)}, u32[]{:S(2)}, u32[]{:S(2)}) collective-permute-start(bf16[128,2304]{1,0:T(8,128)(2,1)} %get-tuple-element.252), channel_id=1, source_target_pairs={{0,32},{32,0},{64,96},{96,64},{1,33},{33,1},{65,97},{97,65},{2,34}... | collective-permute-start | bytes 1769480 | tf_op jit(solution)/shard_map/ppermute | solution.py:286
  89.6 26.8 %collective-permute-start.19 = (bf16[128,2304]{1,0:T(8,128)(2,1)}, bf16[128,2304]{1,0:T(8,128)(2,1)}, u32[]{:S(2)}, u32[]{:S(2)}) collective-permute-start(bf16[128,2304]{1,0:T(8,128)(2,1)} %get-tuple-element.253), channel_id=1, source_target_pairs={{0,64},{32,96},{64,0},{96,32},{1,65},{33,97},{65,1},{97,33},{2,66}... | collective-permute-start | bytes 1769480 | tf_op jit(solution)/shard_map/ppermute | solution.py:286
  90.7 27.7 %collective-permute-start.20 = (bf16[128,2304]{1,0:T(8,128)(2,1)}, bf16[128,2304]{1,0:T(8,128)(2,1)}, u32[]{:S(2)}, u32[]{:S(2)}) collective-permute-start(bf16[128,2304]{1,0:T(8,128)(2,1)} %get-tuple-element.254), channel_id=1, source_target_pairs={{0,96},{32,64},{64,32},{96,0},{1,97},{33,65},{65,33},{97,1},{2,98}... | collective-permute-start | bytes 1769480 | tf_op jit(solution)/shard_map/ppermute | solution.py:286
  125.3 36.6 %collective-permute-start.27 = (bf16[4,128,2304]{2,1,0:T(8,128)(2,1)}, bf16[4,128,2304]{2,1,0:T(8,128)(2,1)}, u32[]{:S(2)}, u32[]{:S(2)}) collective-permute-start(bf16[4,128,2304]{2,1,0:T(8,128)(2,1)} %get-tuple-element.283.refs_9_.refs_11_), channel_id=1, source_target_pairs={{0,1},{1,0},{2,3},{3,2},{4,5},{5,4},{6,7},{7,6},{8,9},{9,8},{10,11... | collective-permute-start | bytes 7077896 | tf_op jit(solution)/shard_map/ppermute | solution.py:303
  134.7 25.2 %collective-permute-start.25 = (bf16[64,4096]{1,0:T(8,128)(2,1)}, bf16[64,4096]{1,0:T(8,128)(2,1)S(1)}, u32[]{:S(2)}, u32[]{:S(2)}) collective-permute-start(bf16[64,4096]{1,0:T(8,128)(2,1)} %get-tuple-element.273), channel_id=1, source_target_pairs={{0,4},{2,6},{4,0},{6,2},{1,5},{3,7},{5,1},{7,3},{8,12},{10,14},{12... | collective-permute-start | bytes 1572872 | tf_op jit(solution)/shard_map/ppermute | solution.py:286
  168.6 25.7 %collective-permute-start.28 = (bf16[4,64,4096]{2,1,0:T(8,128)(2,1)}, bf16[4,64,4096]{2,1,0:T(8,128)(2,1)}, u32[]{:S(2)}, u32[]{:S(2)}) collective-permute-start(bf16[4,64,4096]{2,1,0:T(8,128)(2,1)} %get-tuple-element.300.refs_4_), channel_id=1, source_target_pairs={{0,1},{1,0},{2,3},{3,2},{4,5},{5,4},{6,7},{7,6},{8,9},{9,8},{10,11... | collective-permute-start | bytes 6291464 | tf_op jit(solution)/shard_map/ppermute | solution.py:303
  175.2 25.3 %collective-permute-start.32 = (bf16[128,2304]{1,0:T(8,128)(2,1)}, bf16[128,2304]{1,0:T(8,128)(2,1)}, u32[]{:S(2)}, u32[]{:S(2)}) collective-permute-start(bf16[128,2304]{1,0:T(8,128)(2,1)} %get-tuple-element.293), channel_id=1, source_target_pairs={{0,32},{32,0},{64,96},{96,64},{1,33},{33,1},{65,97},{97,65},{2,34}... | collective-permute-start | bytes 1769480 | tf_op jit(solution)/shard_map/ppermute | solution.py:286
  176.4 28.2 %collective-permute-start.33 = (bf16[128,2304]{1,0:T(8,128)(2,1)}, bf16[128,2304]{1,0:T(8,128)(2,1)}, u32[]{:S(2)}, u32[]{:S(2)}) collective-permute-start(bf16[128,2304]{1,0:T(8,128)(2,1)} %get-tuple-element.294), channel_id=1, source_target_pairs={{0,64},{32,96},{64,0},{96,32},{1,65},{33,97},{65,1},{97,33},{2,66}... | collective-permute-start | bytes 1769480 | tf_op jit(solution)/shard_map/ppermute | solution.py:286
  178.8 27.8 %collective-permute-start.34 = (bf16[128,2304]{1,0:T(8,128)(2,1)}, bf16[128,2304]{1,0:T(8,128)(2,1)}, u32[]{:S(2)}, u32[]{:S(2)}) collective-permute-start(bf16[128,2304]{1,0:T(8,128)(2,1)} %get-tuple-element.295), channel_id=1, source_target_pairs={{0,96},{32,64},{64,32},{96,0},{1,97},{33,65},{65,33},{97,1},{2,98}... | collective-permute-start | bytes 1769480 | tf_op jit(solution)/shard_map/ppermute | solution.py:286
  213.5 34.8 %collective-permute-start.41 = (bf16[4,128,2304]{2,1,0:T(8,128)(2,1)}, bf16[4,128,2304]{2,1,0:T(8,128)(2,1)}, u32[]{:S(2)}, u32[]{:S(2)}) collective-permute-start(bf16[4,128,2304]{2,1,0:T(8,128)(2,1)} %get-tuple-element.324.refs_9_.refs_11_), channel_id=1, source_target_pairs={{0,1},{1,0},{2,3},{3,2},{4,5},{5,4},{6,7},{7,6},{8,9},{9,8},{10,11... | collective-permute-start | bytes 7077896 | tf_op jit(solution)/shard_map/ppermute | solution.py:303
  221.1 25.2 %collective-permute-start.39 = (bf16[64,4096]{1,0:T(8,128)(2,1)}, bf16[64,4096]{1,0:T(8,128)(2,1)S(1)}, u32[]{:S(2)}, u32[]{:S(2)}) collective-permute-start(bf16[64,4096]{1,0:T(8,128)(2,1)} %get-tuple-element.314), channel_id=1, source_target_pairs={{0,4},{2,6},{4,0},{6,2},{1,5},{3,7},{5,1},{7,3},{8,12},{10,14},{12... | collective-permute-start | bytes 1572872 | tf_op jit(solution)/shard_map/ppermute | solution.py:286
  254.9 25.9 %collective-permute-start.42 = (bf16[4,64,4096]{2,1,0:T(8,128)(2,1)}, bf16[4,64,4096]{2,1,0:T(8,128)(2,1)}, u32[]{:S(2)}, u32[]{:S(2)}) collective-permute-start(bf16[4,64,4096]{2,1,0:T(8,128)(2,1)} %get-tuple-element.341.refs_4_), channel_id=1, source_target_pairs={{0,1},{1,0},{2,3},{3,2},{4,5},{5,4},{6,7},{7,6},{8,9},{9,8},{10,11... | collective-permute-start | bytes 6291464 | tf_op jit(solution)/shard_map/ppermute | solution.py:303
  261.7 25.3 %collective-permute-start.46 = (bf16[128,2304]{1,0:T(8,128)(2,1)}, bf16[128,2304]{1,0:T(8,128)(2,1)}, u32[]{:S(2)}, u32[]{:S(2)}) collective-permute-start(bf16[128,2304]{1,0:T(8,128)(2,1)} %get-tuple-element.334), channel_id=1, source_target_pairs={{0,32},{32,0},{64,96},{96,64},{1,33},{33,1},{65,97},{97,65},{2,34}... | collective-permute-start | bytes 1769480 | tf_op jit(solution)/shard_map/ppermute | solution.py:286
  262.9 28.2 %collective-permute-start.47 = (bf16[128,2304]{1,0:T(8,128)(2,1)}, bf16[128,2304]{1,0:T(8,128)(2,1)}, u32[]{:S(2)}, u32[]{:S(2)}) collective-permute-start(bf16[128,2304]{1,0:T(8,128)(2,1)} %get-tuple-element.335), channel_id=1, source_target_pairs={{0,64},{32,96},{64,0},{96,32},{1,65},{33,97},{65,1},{97,33},{2,66}... | collective-permute-start | bytes 1769480 | tf_op jit(solution)/shard_map/ppermute | solution.py:286
  265.3 27.8 %collective-permute-start.48 = (bf16[128,2304]{1,0:T(8,128)(2,1)}, bf16[128,2304]{1,0:T(8,128)(2,1)}, u32[]{:S(2)}, u32[]{:S(2)}) collective-permute-start(bf16[128,2304]{1,0:T(8,128)(2,1)} %get-tuple-element.336), channel_id=1, source_target_pairs={{0,96},{32,64},{64,32},{96,0},{1,97},{33,65},{65,33},{97,1},{2,98}... | collective-permute-start | bytes 1769480 | tf_op jit(solution)/shard_map/ppermute | solution.py:286
  300.0 34.8 %collective-permute-start.55 = (bf16[4,128,2304]{2,1,0:T(8,128)(2,1)}, bf16[4,128,2304]{2,1,0:T(8,128)(2,1)}, u32[]{:S(2)}, u32[]{:S(2)}) collective-permute-start(bf16[4,128,2304]{2,1,0:T(8,128)(2,1)} %get-tuple-element.365.refs_9_.refs_11_), channel_id=1, source_target_pairs={{0,1},{1,0},{2,3},{3,2},{4,5},{5,4},{6,7},{7,6},{8,9},{9,8},{10,11... | collective-permute-start | bytes 7077896 | tf_op jit(solution)/shard_map/ppermute | solution.py:303
  307.6 25.2 %collective-permute-start.53 = (bf16[64,4096]{1,0:T(8,128)(2,1)}, bf16[64,4096]{1,0:T(8,128)(2,1)S(1)}, u32[]{:S(2)}, u32[]{:S(2)}) collective-permute-start(bf16[64,4096]{1,0:T(8,128)(2,1)} %get-tuple-element.355), channel_id=1, source_target_pairs={{0,4},{2,6},{4,0},{6,2},{1,5},{3,7},{5,1},{7,3},{8,12},{10,14},{12... | collective-permute-start | bytes 1572872 | tf_op jit(solution)/shard_map/ppermute | solution.py:286
  341.5 25.4 %collective-permute-start.56 = (bf16[4,64,4096]{2,1,0:T(8,128)(2,1)}, bf16[4,64,4096]{2,1,0:T(8,128)(2,1)S(1)}, u32[]{:S(2)}, u32[]{:S(2)}) collective-permute-start(bf16[4,64,4096]{2,1,0:T(8,128)(2,1)} %get-tuple-element.369.refs_4_), channel_id=1, source_target_pairs={{0,1},{1,0},{2,3},{3,2},{4,5},{5,4},{6,7},{7,6},{8,9},{9,8},{10,11... | collective-permute-start | bytes 6291464 | tf_op jit(solution)/shard_map/ppermute | solution.py:303
  (84 other events, 1159.5 us)

commit v2 on v1

--- a/solution.py
+++ b/solution.py
@@ -16,8 +16,8 @@
 WIDTH = 16384
 SLAB = 2304
 OCOLS = 4096
-ROWS = 352
-VMEM_LIMIT = 48 * 1024 * 1024
+ROWS = 272
+VMEM_LIMIT = 52 * 1024 * 1024
 f32 = jnp.float32
 bf16 = jnp.bfloat16
 SMEM = pl.BlockSpec(memory_space=pltpu.SMEM)
@@ -112,42 +112,42 @@
 
 def project_kernel(layer, scalars, *refs):
     xs, pieces, refs = refs[:4], refs[4:8], refs[8:]
-    gain_ref, own, other, kv_own, kv_other, out_ref, joined_ref, xg_ref, ss_ref, kv_ref = refs
+    gain_ref, own, other, kv_own, kv_other, out_ref, joined_ref, xg_ref, lead_ref = refs
     z, core = scalars[0], scalars[2]
     for k in range(4):
         joined_ref[k] = pieces[k][...]
 
     @pl.when(pl.program_id(0) == 0)
     def _():
-        at = lax.broadcasted_iota(jnp.int32, (4, COLS), 0) == lax.bitwise_xor(z, layer)
+        rows = lax.broadcasted_iota(jnp.int32, (4, COLS), 0)
+        gains = gain_ref[lax.bitwise_xor(z, layer)]
         total = jnp.zeros((SEQ, 1), f32)
         low, high = [], []
         for k in range(4):
             wide = xs[k][...].astype(f32)
             total += jnp.sum(wide * wide, axis=1, keepdims=True)
-            scaled = wide * jnp.sum(jnp.where(at, gain_ref[k], 0.0), axis=0, keepdims=True)
+            at = rows == lax.bitwise_xor(z, k)
+            scaled = wide * jnp.sum(jnp.where(at, gains, 0.0), axis=0, keepdims=True)
             low.append(scaled[:, :128])
             high.append(scaled[:, 128:])
-        scaled = jnp.where(
+        xg_ref[...] = jnp.where(
             core == 1, jnp.concatenate(high + low, axis=1), jnp.concatenate(low + high, axis=1)
-        )
-        xg_ref[...] = scaled.astype(bf16)
-        padded = jnp.concatenate([scaled, jnp.zeros((128 - SEQ, 1024), f32)], axis=0).astype(bf16)
+        ).astype(bf16)
         eye, _ = masks()
         row = jnp.sum(jnp.where(eye, total, 0.0), axis=0, keepdims=True)
         coarse = row.astype(bf16).astype(f32)
         which = lax.broadcasted_iota(jnp.int32, (8, 128), 0)
-        ss_ref[...] = jnp.where(which == 0, coarse, jnp.where(which == 1, row - coarse, 0.0))
-        kv = dot(padded[:, :512], kv_own[...].reshape(512, 256))
-        kv += dot(padded[:, 512:], kv_other[...].reshape(512, 256))
-        kv_ref[:128] = kv[:, :128].T
-        kv_ref[128:] = kv[:, 128:].T
+        lead_ref[:8] = jnp.where(which == 0, coarse, jnp.where(which == 1, row - coarse, 0.0))
+        kv = dot(xg_ref[:, :512], kv_own[...].reshape(512, 256))
+        kv += dot(xg_ref[:, 512:], kv_other[...].reshape(512, 256))
+        lead_ref[8 : 8 + SEQ] = kv[:, :128]
+        lead_ref[8 + SEQ :] = kv[:, 128:]
 
     q = dot(xg_ref[:, :512], own[...].reshape(512, 512))
     q += dot(xg_ref[:, 512:], other[...].reshape(512, 512))
     for h in range(4):
         out_ref[h] = jnp.concatenate(
-            [kv_ref[...], ss_ref[...], q[:, HEAD * h : HEAD * h + HEAD]], axis=0
+            [lead_ref[...], q[:, HEAD * h : HEAD * h + HEAD]], axis=0
         ).astype(bf16)
 
 
@@ -165,14 +165,13 @@
             pl.BlockSpec((4, ROWS, 128), lambda s: (s, 0, 0)),
             pl.BlockSpec((4, 64, 1024), lambda s: (0, 0, s)),
         ],
-        out_shape=[pltpu.HBM((16, ROWS, 128), bf16), pltpu.HBM((4, 64, OCOLS), bf16)],
-        scratch_shapes=[
-            pltpu.VMEM((SEQ, 1024), bf16),
-            pltpu.VMEM((8, 128), f32),
-            pltpu.VMEM((256, 128), f32),
+        out_shape=[
+            jax.ShapeDtypeStruct((16, ROWS, 128), bf16),
+            jax.ShapeDtypeStruct((4, 64, OCOLS), bf16),
         ],
-        compiler_params=PARAMS,
-        cost_estimate=cost(2 * SEQ * 1024 * SLAB, 10_000_000),
+        scratch_shapes=[pltpu.VMEM((SEQ, 1024), bf16), pltpu.VMEM((8 + 2 * SEQ, 128), f32)],
+        compiler_params=PARAMS,
+        cost_estimate=cost(2 * SEQ * 1024 * SLAB, 6_000_000),
         name="project",
     )(scalars, *xs, *pieces, gains, *weights, *weights)
 
@@ -190,17 +189,19 @@
 
     @pl.when(step == 3)
     def _():
-        total = acc[256:257] + acc[257:258]
-        row = lax.rsqrt(total * (1.0 / WIDTH) + 1e-05)
-        eye, causal = masks()
+        row = lax.rsqrt((acc[0:1] + acc[1:2]) * (1.0 / WIDTH) + 1e-05)
+        eye, _ = masks()
         column = jnp.sum(jnp.where(eye, row, 0.0), axis=1, keepdims=True)
-        q = (acc[264:] * column).astype(bf16)
-        keys = (acc[:128] * row).astype(bf16)
-        values = (acc[128:256] * row).astype(bf16)
-        scores = dot(q, keys) * (1.0 / math.sqrt(HEAD))
+        keys, values, queries = (
+            (acc[8 + SEQ * k : 8 + SEQ * k + SEQ] * column).astype(bf16) for k in range(3)
+        )
+        scores = dot(queries, keys, ((1,), (1,))) * (1.0 / math.sqrt(HEAD))
+        causal = lax.broadcasted_iota(jnp.int32, (SEQ, SEQ), 0) >= lax.broadcasted_iota(
+            jnp.int32, (SEQ, SEQ), 1
+        )
         weights = jnp.where(causal, jnp.exp(scores), 0.0)
         shares = (weights / jnp.sum(weights, axis=1, keepdims=True)).astype(bf16)
-        out_ref[...] = dot(shares, values, ((1,), (1,))).astype(bf16)
+        out_ref[...] = dot(shares, values).astype(bf16)
 
 
 def attend(received):
@@ -212,7 +213,7 @@
         out_shape=jax.ShapeDtypeStruct((SEQ, HEAD), bf16),
         scratch_shapes=[pltpu.VMEM((ROWS, 128), f32)],
         compiler_params=PARAMS,
-        cost_estimate=cost(6_000_000, 1_500_000),
+        cost_estimate=cost(6_000_000, 1_200_000),
         name="attend",
     )(received)
 
@@ -308,10 +309,7 @@
     slot = 2 * core + lax.rem(along, 2)
     scalars = jnp.stack([plane, along, core]).astype(jnp.int32)
 
-    gains = jnp.concatenate(line(norm_gain, "z"), axis=0)
-    slab = slab_in(0, scalars, query_weight, key_matrix, value_matrix)
-    gains, slab = after(gains, slab)
-    ins = relay(slab, "z")
+    inward = lambda layer: slab_in(layer, scalars, query_weight, key_matrix, value_matrix)
 
     rounds = []
     for r in range(4):
@@ -322,39 +320,49 @@
                 pairs.append((32 * p + t, 32 * p + 2 * ((2 * t) % 16 + s % 2) + s // 2))
         s = lax.rem(across - r + 4, 4)
         piece = lax.dynamic_slice(entering, (s // 2, 0, lax.rem(s, 2) * COLS), (1, SEQ, COLS))[0]
-        gain = lax.dynamic_slice(gains, (0, lax.rem(s, 2) * COLS), (4, COLS))
-        piece = jnp.concatenate([piece, gain, gain], axis=0)
+        gain = lax.dynamic_slice(norm_gain, (0, lax.rem(s, 2) * COLS), (1, COLS))
+        piece = jnp.concatenate([piece, jnp.broadcast_to(gain, (8, COLS))], axis=0)
         rounds.append(lax.ppermute(piece, ALL, pairs))
+    rounds, (slab, cut) = after(rounds, (inward(0), slab_out(0, scalars, output_weight)))
+    ins = relay(slab, "z")
+    outs = relay(cut, "y")
     rounds = jnp.stack(rounds)
-    rounds, scalars = after(rounds, scalars)
-    cut = slab_out(0, scalars, output_weight)
-    outs = relay(cut, "y")
-    lines = [
-        lax.dynamic_index_in_dim(rounds, lax.rem(lax.bitwise_xor(plane, k) - slot + 4, 4), 0, keepdims=False)
+    xs = [
+        lax.dynamic_index_in_dim(
+            rounds, lax.rem(lax.bitwise_xor(plane, k) - slot + 4, 4), 0, keepdims=False
+        )[:SEQ]
         for k in range(4)
     ]
-    xs = [part[:SEQ] for part in lines]
-    gains = jnp.stack([part[SEQ : SEQ + 4] for part in lines]).astype(f32)
-
-    slabs = [slab_in(layer, scalars, query_weight, key_matrix, value_matrix) for layer in range(1, 4)]
-    cuts = [slab_out(layer, scalars, output_weight) for layer in range(1, 4)]
-    ins, (outs, slabs, cuts) = after(ins, (outs, slabs, cuts))
+    gains = jnp.stack(
+        [
+            lax.dynamic_index_in_dim(rounds[:, SEQ], lax.rem(p - slot + 4, 4), 0, keepdims=False)
+            for p in range(4)
+        ]
+    )
+    ahead = inward(1)
+    ins, (outs, ahead, xs, gains) = after(ins, (outs, ahead, xs, gains))
     ins = swapped(join(ins))
+    gains = jnp.stack(line(gains, "z")).astype(f32)
     states = []
     for layer in range(4):
         xs, outs = after(xs, outs)
         partial, outs = project(layer, scalars, xs, gains, ins, outs)
         if layer < 3:
-            partial, slab = after(partial, slabs[layer])
+            partial, (slab, scalars) = after(partial, (ahead, scalars))
             ins = relay(slab, "z")
+            cut = slab_out(layer + 1, scalars, output_weight)
+            if layer < 2:
+                ahead = inward(layer + 2)
         received, outs = after(exchange(partial, ("x", "y")), swapped(outs))
+        if layer < 3:
+            received, (cut, ahead) = after(received, (cut, ahead))
         mixed = line(attend(received), "y")
         if layer < 3:
-            mixed, ins = after(mixed, ins)
+            mixed, (ins, cut) = after(mixed, (ins, cut))
+            outs_next = relay(cut, "y")
             partial, ins = output(scalars, mixed, outs, ins)
-            partial, cut = after(partial, cuts[layer])
-            outs = relay(cut, "y")
             ins = swapped(ins)
+            outs = outs_next
         else:
             partial = output(scalars, mixed, outs, [])[0]
         x = close(exchange(partial, ("z", "x")), xs[0])

time: 420 us -> 402 us (0.957)
  local copies, waits for them, and re-layouts: 15.7 us -> 3.2 us
  waiting for transfers between devices: 168 us -> 163 us
  Pallas kernels: 65.3 us -> 70 us
    ppermute x48, waiting for transfers between devices: 72.7 us -> 105 us  [across_line(): return lax.ppermute(value, axis, [(i, i ^ by) for i in range(4)])]
    all_to_all x7, waiting for transfers between devices: 77.1 us -> 52.2 us  [exchange(): return lax.all_to_all(value, axes, 0, 0, tiled=True)]
    unnamed x74 -> x26, local copies, waits for them, and re-layouts: 14.8 us -> 1.42 us
    ppermute x8, waiting for transfers between devices: 13.6 us -> 5.66 us  [body(): rounds.append(lax.ppermute(piece, ALL, pairs))]
    ppermute x8, waiting for transfers between devices: 4.45 us -> 0.02 us  [swapped(): return (joined, lax.ppermute(joined, 'c', [(0, 1), (1, 0)]))]
  transfers between devices with their start and end apart: 71 -> 71, of which waited for: 34 -> 35; matrix products, arithmetic and copies ran while one was open for 0% -> 0% of each run, Pallas kernels for 5% -> 6%
where the time goes in v2:
time: 402 us; the launch traced here: 398 us
  waiting for transfers between devices  163 us (41%)
  starting transfers between devices  141 us (35%)
  Pallas kernels  70 us (17%)
  blocking collectives  19.8 us (5%)
    ppermute x48, waiting for transfers between devices, across_line(): return lax.ppermute(value, axis, [(i, i ^ by) for i in range(4)])  105 us
    ppermute x48, starting transfers between devices, across_line(): return lax.ppermute(value, axis, [(i, i ^ by) for i in range(4)])  61.8 us
    all_to_all x7, waiting for transfers between devices, exchange(): return lax.all_to_all(value, axes, 0, 0, tiled=True)  52.2 us
    all_to_all x7, starting transfers between devices, exchange(): return lax.all_to_all(value, axes, 0, 0, tiled=True)  36.1 us
    ppermute x8, starting transfers between devices, body(): rounds.append(lax.ppermute(piece, ALL, pairs))  27.6 us
    pallas_call x4, Pallas kernels, project(): pl.pallas_call(functools.partial(project_kernel, layer), grid=(4,), in_sp...  21.7 us
    pallas_call x4, Pallas kernels, output(): pl.pallas_call(output_kernel, grid=(4,), in_specs=specs, out_specs=out_sp...  20.3 us
    all_to_all x1, blocking collectives, exchange(): return lax.all_to_all(value, axes, 0, 0, tiled=True)  19.8 us
  transfers between devices with their start and end apart: 71, of which 35 were waited for; matrix products, arithmetic and copies ran while one was open for 0% of the time, Pallas kernels for 6%

profile of v2, /device:TPU:5, one launch (start us, length us, event | category | flops | bytes accessed | tf_op | source)
XLA Modules:
  0.0 397.9 jit_solution(13154168906879279375)
XLA Ops:
  23.5 8.7 %collective-permute-done.7.refs_5_ = bf16[64,4096]{1,0:T(8,128)(2,1)S(1)} collective-permute-done((bf16[64,4096]{1,0:T(8,128)(2,1)S(1)}, bf16[64,4096]{1,0:T(8,128)(2,1)S(1)}, u32[]{:S(2)}, u32[]{:S(2)}) %collective-permute-start.7) | collective-permute-done | bytes 524320 | tf_op jit(solution)/shard_map/ppermute | solution.py:287
  35.2 5.8 %collective-permute-done.8.refs_6_ = bf16[64,4096]{1,0:T(8,128)(2,1)} collective-permute-done((bf16[64,4096]{1,0:T(8,128)(2,1)}, bf16[64,4096]{1,0:T(8,128)(2,1)}, u32[]{:S(2)}, u32[]{:S(2)}) %collective-permute-start.8) | collective-permute-done | bytes 524320 | tf_op jit(solution)/shard_map/ppermute | solution.py:287
  40.9 12.9 %collective-permute-done.9.refs_7_ = bf16[64,4096]{1,0:T(8,128)(2,1)} collective-permute-done((bf16[64,4096]{1,0:T(8,128)(2,1)}, bf16[64,4096]{1,0:T(8,128)(2,1)}, u32[]{:S(2)}, u32[]{:S(2)}) %collective-permute-start.9) | collective-permute-done | bytes 524320 | tf_op jit(solution)/shard_map/ppermute | solution.py:287
  67.2 5.5 %project.4 = (bf16[16,272,128]{2,1,0:T(8,128)(2,1)}, bf16[4,64,4096]{2,1,0:T(8,128)(2,1)}) custom-call(s32[3]{0:T(128)S(1)} %pad_add_fusion.scalars, bf16[88,256]{1,0:T(8,128)(2,1)S(1)} %get-tuple-element.233.refs_0_.x_ref, bf16[88,256]{1,0:T(8,128)(2,1)S(1)} %get-tuple-element.234.refs_1_, bf16[88,256]{1,0:T(8,128)(2,1)S(1)} %get-tuple-element.235.refs_2_, ...), custom_call_target="tpu_custom_call" | custom-call | flops 415236096 | bytes 6000000 | tf_op jit(solution)/shard_map/project/pallas_call | solution.py:155
  74.4 7.4 %all-to-all-start = ((bf16[16,272,128]{2,1,0:T(8,128)(2,1)}), bf16[16,272,128]{2,1,0:T(8,128)(2,1)S(1)}, u32[]{:S(2)}, u32[]{:S(2)}) async-start(bf16[16,272,128]{2,1,0:T(8,128)(2,1)} %get-tuple-element.252), calls=%async_computation | async-start | bytes 2228224 | tf_op jit(solution)/shard_map/all_to_all | solution.py:283
  91.3 6.0 %all-to-all-done.recv_ref = bf16[16,272,128]{2,1,0:T(8,128)(2,1)S(1)} async-done(((bf16[16,272,128]{2,1,0:T(8,128)(2,1)}), bf16[16,272,128]{2,1,0:T(8,128)(2,1)S(1)}, u32[]{:S(2)}, u32[]{:S(2)}) %all-to-all-start) | async-done | bytes 1114144 | tf_op jit(solution)/shard_map/all_to_all | solution.py:283
  103.0 7.7 %collective-permute-done.19.refs_8_ = bf16[128,2304]{1,0:T(8,128)(2,1)} collective-permute-done((bf16[128,2304]{1,0:T(8,128)(2,1)}, bf16[128,2304]{1,0:T(8,128)(2,1)}, u32[]{:S(2)}, u32[]{:S(2)}) %collective-permute-start.19) | collective-permute-done | bytes 589856 | tf_op jit(solution)/shard_map/ppermute | solution.py:287
  112.7 5.3 %output.4 = (bf16[16,88,256]{2,1,0:T(8,128)(2,1)}, bf16[4,128,2304]{2,1,0:T(8,128)(2,1)}) custom-call(s32[3]{0:T(128)S(1)} %pad_add_fusion.scalars, bf16[88,128]{1,0:T(8,128)(2,1)S(1)} %attend.4.refs_0_, bf16[88,128]{1,0:T(8,128)(2,1)S(1)} %collective-permute-done.15.refs_1_, bf16[88,128]{1,0:T(8,128)(2,1)S(1)} %collective-permute-done.16.refs_2_, ...), custom_call_target="tpu_custom_call" | custom-call | flops 369098752 | bytes 10000000 | tf_op jit(solution)/shard_map/output/pallas_call | solution.py:252
  128.8 7.9 %all-to-all-done.1.recv_ref = bf16[16,88,256]{2,1,0:T(8,128)(2,1)S(1)} async-done(((bf16[16,88,256]{2,1,0:T(8,128)(2,1)}), bf16[16,88,256]{2,1,0:T(8,128)(2,1)S(1)}, u32[]{:S(2)}, u32[]{:S(2)}) %all-to-all-start.1) | async-done | bytes 720928 | tf_op jit(solution)/shard_map/all_to_all | solution.py:283
  141.0 10.4 %collective-permute-done.25.refs_6_ = bf16[64,4096]{1,0:T(8,128)(2,1)} collective-permute-done((bf16[64,4096]{1,0:T(8,128)(2,1)}, bf16[64,4096]{1,0:T(8,128)(2,1)}, u32[]{:S(2)}, u32[]{:S(2)}) %collective-permute-start.25) | collective-permute-done | bytes 524320 | tf_op jit(solution)/shard_map/ppermute | solution.py:287
  153.4 5.6 %project.5 = (bf16[16,272,128]{2,1,0:T(8,128)(2,1)}, bf16[4,64,4096]{2,1,0:T(8,128)(2,1)}) custom-call(s32[3]{0:T(128)S(1)} %pad_add_fusion.scalars, bf16[88,256]{1,0:T(8,128)(2,1)S(1)} %close.4.refs_0_.x_ref, bf16[88,256]{1,0:T(8,128)(2,1)S(1)} %collective-permute-done.21.refs_1_, bf16[88,256]{1,0:T(8,128)(2,1)S(1)} %collective-permute-done.22.refs_2_, ...), custom_call_target="tpu_custom_call" | custom-call | flops 415236096 | bytes 6000000 | tf_op jit(solution)/shard_map/project/pallas_call | solution.py:155
  175.1 6.0 %all-to-all-done.2.recv_ref = bf16[16,272,128]{2,1,0:T(8,128)(2,1)S(1)} async-done(((bf16[16,272,128]{2,1,0:T(8,128)(2,1)}), bf16[16,272,128]{2,1,0:T(8,128)(2,1)S(1)}, u32[]{:S(2)}, u32[]{:S(2)}) %all-to-all-start.2) | async-done | bytes 1114144 | tf_op jit(solution)/shard_map/all_to_all | solution.py:283
  186.9 8.1 %collective-permute-done.33.refs_8_ = bf16[128,2304]{1,0:T(8,128)(2,1)S(1)} collective-permute-done((bf16[128,2304]{1,0:T(8,128)(2,1)}, bf16[128,2304]{1,0:T(8,128)(2,1)S(1)}, u32[]{:S(2)}, u32[]{:S(2)}) %collective-permute-start.33) | collective-permute-done | bytes 589856 | tf_op jit(solution)/shard_map/ppermute | solution.py:287
  212.5 7.9 %all-to-all-done.3.recv_ref = bf16[16,88,256]{2,1,0:T(8,128)(2,1)S(1)} async-done(((bf16[16,88,256]{2,1,0:T(8,128)(2,1)}), bf16[16,88,256]{2,1,0:T(8,128)(2,1)S(1)}, u32[]{:S(2)}, u32[]{:S(2)}) %all-to-all-start.3) | async-done | bytes 720928 | tf_op jit(solution)/shard_map/all_to_all | solution.py:283
  224.7 10.3 %collective-permute-done.39.refs_6_ = bf16[64,4096]{1,0:T(8,128)(2,1)S(1)} collective-permute-done((bf16[64,4096]{1,0:T(8,128)(2,1)}, bf16[64,4096]{1,0:T(8,128)(2,1)S(1)}, u32[]{:S(2)}, u32[]{:S(2)}) %collective-permute-start.39) | collective-permute-done | bytes 524320 | tf_op jit(solution)/shard_map/ppermute | solution.py:287
  255.6 8.8 %all-to-all-done.4.recv_ref = bf16[16,272,128]{2,1,0:T(8,128)(2,1)S(1)} async-done(((bf16[16,272,128]{2,1,0:T(8,128)(2,1)}), bf16[16,272,128]{2,1,0:T(8,128)(2,1)S(1)}, u32[]{:S(2)}, u32[]{:S(2)}) %all-to-all-start.4) | async-done | bytes 1114144 | tf_op jit(solution)/shard_map/all_to_all | solution.py:283
  270.1 8.2 %collective-permute-done.47.refs_8_ = bf16[128,2304]{1,0:T(8,128)(2,1)S(1)} collective-permute-done((bf16[128,2304]{1,0:T(8,128)(2,1)}, bf16[128,2304]{1,0:T(8,128)(2,1)S(1)}, u32[]{:S(2)}, u32[]{:S(2)}) %collective-permute-start.47) | collective-permute-done | bytes 589856 | tf_op jit(solution)/shard_map/ppermute | solution.py:287
  295.8 7.9 %all-to-all-done.5.recv_ref = bf16[16,88,256]{2,1,0:T(8,128)(2,1)S(1)} async-done(((bf16[16,88,256]{2,1,0:T(8,128)(2,1)}), bf16[16,88,256]{2,1,0:T(8,128)(2,1)S(1)}, u32[]{:S(2)}, u32[]{:S(2)}) %all-to-all-start.5) | async-done | bytes 720928 | tf_op jit(solution)/shard_map/all_to_all | solution.py:283
  308.0 10.3 %collective-permute-done.53.refs_6_ = bf16[64,4096]{1,0:T(8,128)(2,1)S(1)} collective-permute-done((bf16[64,4096]{1,0:T(8,128)(2,1)}, bf16[64,4096]{1,0:T(8,128)(2,1)S(1)}, u32[]{:S(2)}, u32[]{:S(2)}) %collective-permute-start.53) | collective-permute-done | bytes 524320 | tf_op jit(solution)/shard_map/ppermute | solution.py:287
  320.5 5.3 %project.7 = (bf16[16,272,128]{2,1,0:T(8,128)(2,1)}, bf16[4,64,4096]{2,1,0:T(8,128)(2,1)}) custom-call(s32[3]{0:T(128)S(1)} %pad_add_fusion.scalars, bf16[88,256]{1,0:T(8,128)(2,1)S(1)} %close.6.refs_0_.x_ref, bf16[88,256]{1,0:T(8,128)(2,1)S(1)} %collective-permute-done.49.refs_1_, bf16[88,256]{1,0:T(8,128)(2,1)S(1)} %collective-permute-done.50.refs_2_, ...), custom_call_target="tpu_custom_call" | custom-call | flops 415236096 | bytes 6000000 | tf_op jit(solution)/shard_map/project/pallas_call | solution.py:155
  328.0 19.8 %all_to_all.40.recv_ref = bf16[16,272,128]{2,1,0:T(8,128)(2,1)S(1)} all-to-all(bf16[16,272,128]{2,1,0:T(8,128)(2,1)} %get-tuple-element.392), channel_id=1, replica_groups=mesh['z'=4,'x'=4,'y'=4,'c'=2] {'x','y'}, dimensions={0} | all-to-all | bytes 2228224 | tf_op jit(solution)/shard_map/all_to_all | solution.py:283
  360.2 6.7 %all-to-all-start.7 = ((bf16[16,88,256]{2,1,0:T(8,128)(2,1)}), bf16[16,88,256]{2,1,0:T(8,128)(2,1)S(1)}, u32[]{:S(2)}, u32[]{:S(2)}) async-start(bf16[16,88,256]{2,1,0:T(8,128)(2,1)} %output.7), calls=%async_computation.7 | async-start | bytes 1441792 | tf_op jit(solution)/shard_map/all_to_all | solution.py:283
  366.9 7.7 %all-to-all-done.7.recv_ref = bf16[16,88,256]{2,1,0:T(8,128)(2,1)S(1)} async-done(((bf16[16,88,256]{2,1,0:T(8,128)(2,1)}), bf16[16,88,256]{2,1,0:T(8,128)(2,1)S(1)}, u32[]{:S(2)}, u32[]{:S(2)}) %all-to-all-start.7) | async-done | bytes 720928 | tf_op jit(solution)/shard_map/all_to_all | solution.py:283
  374.7 10.4 %collective-permute-start.60 = (bf16[88,256]{1,0:T(8,128)(2,1)S(1)}, bf16[88,256]{1,0:T(8,128)(2,1)S(1)}, u32[]{:S(2)}, u32[]{:S(2)}) collective-permute-start(bf16[88,256]{1,0:T(8,128)(2,1)S(1)} %get-tuple-element.409), channel_id=1, source_target_pairs={{0,0},{1,64},{2,32},{3,96},{4,1},{5,65},{6,33},{7,97},{8,2},{9,66}... | collective-permute-start | bytes 135176 | tf_op jit(solution)/shard_map/ppermute | solution.py:380
  (193 shorter events, 197.1 us)
Async XLA Ops:
  18.5 35.4 %collective-permute-start.4 = (bf16[128,2304]{1,0:T(8,128)(2,1)}, bf16[128,2304]{1,0:T(8,128)(2,1)S(1)}, u32[]{:S(2)}, u32[]{:S(2)}) collective-permute-start(bf16[128,2304]{1,0:T(8,128)(2,1)} %get-tuple-element.210), channel_id=1, source_target_pairs={{0,32},{32,0},{64,96},{96,64},{1,33},{33,1},{65,97},{97,65},{2,34}... | collective-permute-start | bytes 1769480 | tf_op jit(solution)/shard_map/ppermute | solution.py:287
  20.2 33.7 %collective-permute-start.5 = (bf16[128,2304]{1,0:T(8,128)(2,1)}, bf16[128,2304]{1,0:T(8,128)(2,1)S(1)}, u32[]{:S(2)}, u32[]{:S(2)}) collective-permute-start(bf16[128,2304]{1,0:T(8,128)(2,1)} %get-tuple-element.211), channel_id=1, source_target_pairs={{0,64},{32,96},{64,0},{96,32},{1,65},{33,97},{65,1},{97,33},{2,66}... | collective-permute-start | bytes 1769480 | tf_op jit(solution)/shard_map/ppermute | solution.py:287
  23.5 30.4 %collective-permute-start.6 = (bf16[128,2304]{1,0:T(8,128)(2,1)}, bf16[128,2304]{1,0:T(8,128)(2,1)}, u32[]{:S(2)}, u32[]{:S(2)}) collective-permute-start(bf16[128,2304]{1,0:T(8,128)(2,1)} %get-tuple-element.212), channel_id=1, source_target_pairs={{0,96},{32,64},{64,32},{96,0},{1,97},{33,65},{65,33},{97,1},{2,98}... | collective-permute-start | bytes 1769480 | tf_op jit(solution)/shard_map/ppermute | solution.py:287
  32.2 21.6 %collective-permute-start.9 = (bf16[64,4096]{1,0:T(8,128)(2,1)}, bf16[64,4096]{1,0:T(8,128)(2,1)}, u32[]{:S(2)}, u32[]{:S(2)}) collective-permute-start(bf16[64,4096]{1,0:T(8,128)(2,1)} %get-tuple-element.216), channel_id=1, source_target_pairs={{0,6},{2,4},{4,2},{6,0},{1,7},{3,5},{5,3},{7,1},{8,14},{10,12},{12... | collective-permute-start | bytes 1572872 | tf_op jit(solution)/shard_map/ppermute | solution.py:287
  72.7 24.6 %collective-permute-start.14 = (bf16[4,64,4096]{2,1,0:T(8,128)(2,1)}, bf16[4,64,4096]{2,1,0:T(8,128)(2,1)}, u32[]{:S(2)}, u32[]{:S(2)}) collective-permute-start(bf16[4,64,4096]{2,1,0:T(8,128)(2,1)} %get-tuple-element.276.refs_4_), channel_id=1, source_target_pairs={{0,1},{1,0},{2,3},{3,2},{4,5},{5,4},{6,7},{7,6},{8,9},{9,8},{10,11... | collective-permute-start | bytes 6291464 | tf_op jit(solution)/shard_map/ppermute | solution.py:304
  74.4 22.8 %all-to-all-start = ((bf16[16,272,128]{2,1,0:T(8,128)(2,1)}), bf16[16,272,128]{2,1,0:T(8,128)(2,1)S(1)}, u32[]{:S(2)}, u32[]{:S(2)}) async-start(bf16[16,272,128]{2,1,0:T(8,128)(2,1)} %get-tuple-element.252), calls=%async_computation | async-start | bytes 2228224 | tf_op jit(solution)/shard_map/all_to_all | solution.py:283
  81.8 28.9 %collective-permute-start.19 = (bf16[128,2304]{1,0:T(8,128)(2,1)}, bf16[128,2304]{1,0:T(8,128)(2,1)}, u32[]{:S(2)}, u32[]{:S(2)}) collective-permute-start(bf16[128,2304]{1,0:T(8,128)(2,1)} %get-tuple-element.266), channel_id=1, source_target_pairs={{0,64},{32,96},{64,0},{96,32},{1,65},{33,97},{65,1},{97,33},{2,66}... | collective-permute-start | bytes 1769480 | tf_op jit(solution)/shard_map/ppermute | solution.py:287
  84.9 27.8 %collective-permute-start.20 = (bf16[128,2304]{1,0:T(8,128)(2,1)}, bf16[128,2304]{1,0:T(8,128)(2,1)}, u32[]{:S(2)}, u32[]{:S(2)}) collective-permute-start(bf16[128,2304]{1,0:T(8,128)(2,1)} %get-tuple-element.267), channel_id=1, source_target_pairs={{0,96},{32,64},{64,32},{96,0},{1,97},{33,65},{65,33},{97,1},{2,98}... | collective-permute-start | bytes 1769480 | tf_op jit(solution)/shard_map/ppermute | solution.py:287
  118.0 35.4 %collective-permute-start.27 = (bf16[4,128,2304]{2,1,0:T(8,128)(2,1)}, bf16[4,128,2304]{2,1,0:T(8,128)(2,1)}, u32[]{:S(2)}, u32[]{:S(2)}) collective-permute-start(bf16[4,128,2304]{2,1,0:T(8,128)(2,1)} %get-tuple-element.295.refs_9_.refs_11_), channel_id=1, source_target_pairs={{0,1},{1,0},{2,3},{3,2},{4,5},{5,4},{6,7},{7,6},{8,9},{9,8},{10,11... | collective-permute-start | bytes 7077896 | tf_op jit(solution)/shard_map/ppermute | solution.py:304
  126.1 25.3 %collective-permute-start.25 = (bf16[64,4096]{1,0:T(8,128)(2,1)}, bf16[64,4096]{1,0:T(8,128)(2,1)}, u32[]{:S(2)}, u32[]{:S(2)}) collective-permute-start(bf16[64,4096]{1,0:T(8,128)(2,1)} %get-tuple-element.285), channel_id=1, source_target_pairs={{0,4},{2,6},{4,0},{6,2},{1,5},{3,7},{5,1},{7,3},{8,12},{10,14},{12... | collective-permute-start | bytes 1572872 | tf_op jit(solution)/shard_map/ppermute | solution.py:287
  128.5 24.9 %collective-permute-start.26 = (bf16[64,4096]{1,0:T(8,128)(2,1)}, bf16[64,4096]{1,0:T(8,128)(2,1)}, u32[]{:S(2)}, u32[]{:S(2)}) collective-permute-start(bf16[64,4096]{1,0:T(8,128)(2,1)} %get-tuple-element.286), channel_id=1, source_target_pairs={{0,6},{2,4},{4,2},{6,0},{1,7},{3,5},{5,3},{7,1},{8,14},{10,12},{12... | collective-permute-start | bytes 1572872 | tf_op jit(solution)/shard_map/ppermute | solution.py:287
  159.0 22.1 %collective-permute-start.28 = (bf16[4,64,4096]{2,1,0:T(8,128)(2,1)}, bf16[4,64,4096]{2,1,0:T(8,128)(2,1)}, u32[]{:S(2)}, u32[]{:S(2)}) collective-permute-start(bf16[4,64,4096]{2,1,0:T(8,128)(2,1)} %get-tuple-element.326.refs_4_), channel_id=1, source_target_pairs={{0,1},{1,0},{2,3},{3,2},{4,5},{5,4},{6,7},{7,6},{8,9},{9,8},{10,11... | collective-permute-start | bytes 6291464 | tf_op jit(solution)/shard_map/ppermute | solution.py:304
  166.8 28.1 %collective-permute-start.33 = (bf16[128,2304]{1,0:T(8,128)(2,1)}, bf16[128,2304]{1,0:T(8,128)(2,1)S(1)}, u32[]{:S(2)}, u32[]{:S(2)}) collective-permute-start(bf16[128,2304]{1,0:T(8,128)(2,1)} %get-tuple-element.316), channel_id=1, source_target_pairs={{0,64},{32,96},{64,0},{96,32},{1,65},{33,97},{65,1},{97,33},{2,66}... | collective-permute-start | bytes 1769480 | tf_op jit(solution)/shard_map/ppermute | solution.py:287
  169.2 27.8 %collective-permute-start.34 = (bf16[128,2304]{1,0:T(8,128)(2,1)}, bf16[128,2304]{1,0:T(8,128)(2,1)}, u32[]{:S(2)}, u32[]{:S(2)}) collective-permute-start(bf16[128,2304]{1,0:T(8,128)(2,1)} %get-tuple-element.317), channel_id=1, source_target_pairs={{0,96},{32,64},{64,32},{96,0},{1,97},{33,65},{65,33},{97,1},{2,98}... | collective-permute-start | bytes 1769480 | tf_op jit(solution)/shard_map/ppermute | solution.py:287
  202.3 34.8 %collective-permute-start.41 = (bf16[4,128,2304]{2,1,0:T(8,128)(2,1)}, bf16[4,128,2304]{2,1,0:T(8,128)(2,1)}, u32[]{:S(2)}, u32[]{:S(2)}) collective-permute-start(bf16[4,128,2304]{2,1,0:T(8,128)(2,1)} %get-tuple-element.345.refs_9_.refs_11_), channel_id=1, source_target_pairs={{0,1},{1,0},{2,3},{3,2},{4,5},{5,4},{6,7},{7,6},{8,9},{9,8},{10,11... | collective-permute-start | bytes 7077896 | tf_op jit(solution)/shard_map/ppermute | solution.py:304
  209.8 25.1 %collective-permute-start.39 = (bf16[64,4096]{1,0:T(8,128)(2,1)}, bf16[64,4096]{1,0:T(8,128)(2,1)S(1)}, u32[]{:S(2)}, u32[]{:S(2)}) collective-permute-start(bf16[64,4096]{1,0:T(8,128)(2,1)} %get-tuple-element.335), channel_id=1, source_target_pairs={{0,4},{2,6},{4,0},{6,2},{1,5},{3,7},{5,1},{7,3},{8,12},{10,14},{12... | collective-permute-start | bytes 1572872 | tf_op jit(solution)/shard_map/ppermute | solution.py:287
  212.2 24.9 %collective-permute-start.40 = (bf16[64,4096]{1,0:T(8,128)(2,1)}, bf16[64,4096]{1,0:T(8,128)(2,1)}, u32[]{:S(2)}, u32[]{:S(2)}) collective-permute-start(bf16[64,4096]{1,0:T(8,128)(2,1)} %get-tuple-element.336), channel_id=1, source_target_pairs={{0,6},{2,4},{4,2},{6,0},{1,7},{3,5},{5,3},{7,1},{8,14},{10,12},{12... | collective-permute-start | bytes 1572872 | tf_op jit(solution)/shard_map/ppermute | solution.py:287
  242.4 21.9 %collective-permute-start.42 = (bf16[4,64,4096]{2,1,0:T(8,128)(2,1)}, bf16[4,64,4096]{2,1,0:T(8,128)(2,1)}, u32[]{:S(2)}, u32[]{:S(2)}) collective-permute-start(bf16[4,64,4096]{2,1,0:T(8,128)(2,1)} %get-tuple-element.372.refs_4_), channel_id=1, source_target_pairs={{0,1},{1,0},{2,3},{3,2},{4,5},{5,4},{6,7},{7,6},{8,9},{9,8},{10,11... | collective-permute-start | bytes 6291464 | tf_op jit(solution)/shard_map/ppermute | solution.py:304
  250.2 28.1 %collective-permute-start.47 = (bf16[128,2304]{1,0:T(8,128)(2,1)}, bf16[128,2304]{1,0:T(8,128)(2,1)S(1)}, u32[]{:S(2)}, u32[]{:S(2)}) collective-permute-start(bf16[128,2304]{1,0:T(8,128)(2,1)} %get-tuple-element.362), channel_id=1, source_target_pairs={{0,64},{32,96},{64,0},{96,32},{1,65},{33,97},{65,1},{97,33},{2,66}... | collective-permute-start | bytes 1769480 | tf_op jit(solution)/shard_map/ppermute | solution.py:287
  252.6 27.8 %collective-permute-start.48 = (bf16[128,2304]{1,0:T(8,128)(2,1)}, bf16[128,2304]{1,0:T(8,128)(2,1)}, u32[]{:S(2)}, u32[]{:S(2)}) collective-permute-start(bf16[128,2304]{1,0:T(8,128)(2,1)} %get-tuple-element.363), channel_id=1, source_target_pairs={{0,96},{32,64},{64,32},{96,0},{1,97},{33,65},{65,33},{97,1},{2,98}... | collective-permute-start | bytes 1769480 | tf_op jit(solution)/shard_map/ppermute | solution.py:287
  285.6 34.8 %collective-permute-start.55 = (bf16[4,128,2304]{2,1,0:T(8,128)(2,1)}, bf16[4,128,2304]{2,1,0:T(8,128)(2,1)}, u32[]{:S(2)}, u32[]{:S(2)}) collective-permute-start(bf16[4,128,2304]{2,1,0:T(8,128)(2,1)} %get-tuple-element.391.refs_9_.refs_11_), channel_id=1, source_target_pairs={{0,1},{1,0},{2,3},{3,2},{4,5},{5,4},{6,7},{7,6},{8,9},{9,8},{10,11... | collective-permute-start | bytes 7077896 | tf_op jit(solution)/shard_map/ppermute | solution.py:304
  293.1 25.1 %collective-permute-start.53 = (bf16[64,4096]{1,0:T(8,128)(2,1)}, bf16[64,4096]{1,0:T(8,128)(2,1)S(1)}, u32[]{:S(2)}, u32[]{:S(2)}) collective-permute-start(bf16[64,4096]{1,0:T(8,128)(2,1)} %get-tuple-element.381), channel_id=1, source_target_pairs={{0,4},{2,6},{4,0},{6,2},{1,5},{3,7},{5,1},{7,3},{8,12},{10,14},{12... | collective-permute-start | bytes 1572872 | tf_op jit(solution)/shard_map/ppermute | solution.py:287
  295.5 24.9 %collective-permute-start.54 = (bf16[64,4096]{1,0:T(8,128)(2,1)}, bf16[64,4096]{1,0:T(8,128)(2,1)}, u32[]{:S(2)}, u32[]{:S(2)}) collective-permute-start(bf16[64,4096]{1,0:T(8,128)(2,1)} %get-tuple-element.382), channel_id=1, source_target_pairs={{0,6},{2,4},{4,2},{6,0},{1,7},{3,5},{5,3},{7,1},{8,14},{10,12},{12... | collective-permute-start | bytes 1572872 | tf_op jit(solution)/shard_map/ppermute | solution.py:287
  325.8 22.0 %collective-permute-start.56 = (bf16[4,64,4096]{2,1,0:T(8,128)(2,1)}, bf16[4,64,4096]{2,1,0:T(8,128)(2,1)S(1)}, u32[]{:S(2)}, u32[]{:S(2)}) collective-permute-start(bf16[4,64,4096]{2,1,0:T(8,128)(2,1)} %get-tuple-element.395.refs_4_), channel_id=1, source_target_pairs={{0,1},{1,0},{2,3},{3,2},{4,5},{5,4},{6,7},{7,6},{8,9},{9,8},{10,11... | collective-permute-start | bytes 6291464 | tf_op jit(solution)/shard_map/ppermute | solution.py:304
  (60 other events, 793.9 us)

commit v3 on v2

--- a/solution.py
+++ b/solution.py
@@ -297,7 +297,9 @@
 
 
 def relay(slabs, axis):
-    return [slabs[0]] + [across_line(slabs[k], axis, k) for k in range(1, 4)]
+    near = [across_line(slabs[k], axis, k) for k in (1, 3)]
+    near, far = after(near, slabs[2])
+    return [slabs[0], near[0], across_line(far, axis, 2), near[1]]
 
 
 def swapped(joined):
@@ -346,10 +348,13 @@
     states = []
     for layer in range(4):
         xs, outs = after(xs, outs)
+        if layer < 3:
+            xs, slab = after(xs, ahead)
+            ins_next = relay(slab, "z")
         partial, outs = project(layer, scalars, xs, gains, ins, outs)
         if layer < 3:
-            partial, (slab, scalars) = after(partial, (ahead, scalars))
-            ins = relay(slab, "z")
+            ins = ins_next
+            partial, scalars = after(partial, scalars)
             cut = slab_out(layer + 1, scalars, output_weight)
             if layer < 2:
                 ahead = inward(layer + 2)

time: 402 us -> 378 us (0.940)
  waiting for transfers between devices: 163 us -> 144 us
  starting transfers between devices: 141 us -> 135 us
    all_to_all x7, waiting for transfers between devices: 52.2 us -> 20.2 us  [exchange(): return lax.all_to_all(value, axes, 0, 0, tiled=True)]
    ppermute x48, starting transfers between devices: 61.8 us -> 48.1 us  [across_line(): return lax.ppermute(value, axis, [(i, i ^ by) for i in range(4)])]
    ppermute x48, waiting for transfers between devices: 105 us -> 114 us  [across_line(): return lax.ppermute(value, axis, [(i, i ^ by) for i in range(4)])]
    all_to_all x7, starting transfers between devices: 36.1 us -> 42.6 us  [exchange(): return lax.all_to_all(value, axes, 0, 0, tiled=True)]
  transfers between devices with their start and end apart: 71 -> 71, of which waited for: 35 -> 48; matrix products, arithmetic and copies ran while one was open for 0% -> 0% of each run, Pallas kernels for 6% -> 7%
where the time goes in v3:
time: 378 us; the launch traced here: 376 us
  waiting for transfers between devices  144 us (38%)
  starting transfers between devices  135 us (36%)
  Pallas kernels  69.9 us (18%)
  blocking collectives  22.2 us (6%)
  local copies, waits for them, and re-layouts  4.53 us (1%)
    ppermute x48, waiting for transfers between devices, across_line(): return lax.ppermute(value, axis, [(i, i ^ by) for i in range(4)])  114 us
    ppermute x48, starting transfers between devices, across_line(): return lax.ppermute(value, axis, [(i, i ^ by) for i in range(4)])  48.1 us
    all_to_all x7, starting transfers between devices, exchange(): return lax.all_to_all(value, axes, 0, 0, tiled=True)  42.6 us
    ppermute x8, starting transfers between devices, body(): rounds.append(lax.ppermute(piece, ALL, pairs))  26.6 us
    all_to_all x1, blocking collectives, exchange(): return lax.all_to_all(value, axes, 0, 0, tiled=True)  22.2 us
    pallas_call x4, Pallas kernels, project(): pl.pallas_call(functools.partial(project_kernel, layer), grid=(4,), in_sp...  21.7 us
    pallas_call x4, Pallas kernels, output(): pl.pallas_call(output_kernel, grid=(4,), in_specs=specs, out_specs=out_sp...  20.5 us
    all_to_all x7, waiting for transfers between devices, exchange(): return lax.all_to_all(value, axes, 0, 0, tiled=True)  20.2 us
  transfers between devices with their start and end apart: 71, of which 48 were waited for; matrix products, arithmetic and copies ran while one was open for 0% of the time, Pallas kernels for 7%

profile of v3, /device:TPU:5, one launch (start us, length us, event | category | flops | bytes accessed | tf_op | source)
XLA Modules:
  0.0 376.4 jit_solution(8220061627241087654)
XLA Ops:
  22.4 10.4 %collective-permute-done.4.refs_1_ = bf16[128,2304]{1,0:T(8,128)(2,1)S(1)} collective-permute-done((bf16[128,2304]{1,0:T(8,128)(2,1)}, bf16[128,2304]{1,0:T(8,128)(2,1)S(1)}, u32[]{:S(2)}, u32[]{:S(2)}) %collective-permute-start.4) | collective-permute-done | bytes 589856 | tf_op jit(solution)/shard_map/ppermute | solution.py:287
  41.7 12.3 %collective-permute-done.9.refs_6_ = bf16[64,4096]{1,0:T(8,128)(2,1)} collective-permute-done((bf16[64,4096]{1,0:T(8,128)(2,1)}, bf16[64,4096]{1,0:T(8,128)(2,1)}, u32[]{:S(2)}, u32[]{:S(2)}) %collective-permute-start.9) | collective-permute-done | bytes 524320 | tf_op jit(solution)/shard_map/ppermute | solution.py:287
  65.3 5.5 %project.4 = (bf16[16,272,128]{2,1,0:T(8,128)(2,1)}, bf16[4,64,4096]{2,1,0:T(8,128)(2,1)}) custom-call(s32[3]{0:T(128)S(1)} %pad_add_fusion.scalars, bf16[88,256]{1,0:T(8,128)(2,1)S(1)} %get-tuple-element.283.refs_0_.x_ref, bf16[88,256]{1,0:T(8,128)(2,1)S(1)} %get-tuple-element.284.refs_1_, bf16[88,256]{1,0:T(8,128)(2,1)S(1)} %get-tuple-element.285.refs_2_, ...), custom_call_target="tpu_custom_call" | custom-call | flops 415236096 | bytes 6000000 | tf_op jit(solution)/shard_map/project/pallas_call | solution.py:155
  74.3 6.1 %all-to-all-start = ((bf16[16,272,128]{2,1,0:T(8,128)(2,1)}), bf16[16,272,128]{2,1,0:T(8,128)(2,1)S(1)}, u32[]{:S(2)}, u32[]{:S(2)}) async-start(bf16[16,272,128]{2,1,0:T(8,128)(2,1)} %get-tuple-element.298), calls=%async_computation | async-start | bytes 2228224 | tf_op jit(solution)/shard_map/all_to_all | solution.py:283
  80.4 7.9 %collective-permute-done.18.refs_7_ = bf16[128,2304]{1,0:T(8,128)(2,1)S(1)} collective-permute-done((bf16[128,2304]{1,0:T(8,128)(2,1)}, bf16[128,2304]{1,0:T(8,128)(2,1)S(1)}, u32[]{:S(2)}, u32[]{:S(2)}) %collective-permute-start.18) | collective-permute-done | bytes 589856 | tf_op jit(solution)/shard_map/ppermute | solution.py:287
  105.0 5.4 %output.4 = (bf16[16,88,256]{2,1,0:T(8,128)(2,1)}, bf16[4,128,2304]{2,1,0:T(8,128)(2,1)}) custom-call(s32[3]{0:T(128)S(1)} %pad_add_fusion.scalars, bf16[88,128]{1,0:T(8,128)(2,1)S(1)} %attend.4.refs_0_, bf16[88,128]{1,0:T(8,128)(2,1)S(1)} %collective-permute-done.15.refs_1_, bf16[88,128]{1,0:T(8,128)(2,1)S(1)} %collective-permute-done.16.refs_2_, ...), custom_call_target="tpu_custom_call" | custom-call | flops 369098752 | bytes 10000000 | tf_op jit(solution)/shard_map/output/pallas_call | solution.py:252
  114.8 6.3 %all-to-all-start.1 = ((bf16[16,88,256]{2,1,0:T(8,128)(2,1)}), bf16[16,88,256]{2,1,0:T(8,128)(2,1)S(1)}, u32[]{:S(2)}, u32[]{:S(2)}) async-start(bf16[16,88,256]{2,1,0:T(8,128)(2,1)} %get-tuple-element.331), calls=%async_computation.1 | async-start | bytes 1441792 | tf_op jit(solution)/shard_map/all_to_all | solution.py:283
  121.2 5.4 %collective-permute-done.24.refs_5_ = bf16[64,4096]{1,0:T(8,128)(2,1)S(1)} collective-permute-done((bf16[64,4096]{1,0:T(8,128)(2,1)}, bf16[64,4096]{1,0:T(8,128)(2,1)S(1)}, u32[]{:S(2)}, u32[]{:S(2)}) %collective-permute-start.24) | collective-permute-done | bytes 524320 | tf_op jit(solution)/shard_map/ppermute | solution.py:287
  141.7 5.5 %project.5 = (bf16[16,272,128]{2,1,0:T(8,128)(2,1)}, bf16[4,64,4096]{2,1,0:T(8,128)(2,1)}) custom-call(s32[3]{0:T(128)S(1)} %pad_add_fusion.scalars, bf16[88,256]{1,0:T(8,128)(2,1)S(1)} %close.4.refs_0_.x_ref, bf16[88,256]{1,0:T(8,128)(2,1)S(1)} %collective-permute-done.21.refs_1_, bf16[88,256]{1,0:T(8,128)(2,1)S(1)} %collective-permute-done.22.refs_2_, ...), custom_call_target="tpu_custom_call" | custom-call | flops 415236096 | bytes 6000000 | tf_op jit(solution)/shard_map/project/pallas_call | solution.py:155
  151.7 6.3 %all-to-all-start.2 = ((bf16[16,272,128]{2,1,0:T(8,128)(2,1)}), bf16[16,272,128]{2,1,0:T(8,128)(2,1)S(1)}, u32[]{:S(2)}, u32[]{:S(2)}) async-start(bf16[16,272,128]{2,1,0:T(8,128)(2,1)} %get-tuple-element.358), calls=%async_computation.2 | async-start | bytes 2228224 | tf_op jit(solution)/shard_map/all_to_all | solution.py:283
  158.0 6.6 %collective-permute-done.32.refs_7_ = bf16[128,2304]{1,0:T(8,128)(2,1)S(1)} collective-permute-done((bf16[128,2304]{1,0:T(8,128)(2,1)}, bf16[128,2304]{1,0:T(8,128)(2,1)S(1)}, u32[]{:S(2)}, u32[]{:S(2)}) %collective-permute-start.32) | collective-permute-done | bytes 589856 | tf_op jit(solution)/shard_map/ppermute | solution.py:287
  192.1 5.3 %all-to-all-start.3 = ((bf16[16,88,256]{2,1,0:T(8,128)(2,1)}), bf16[16,88,256]{2,1,0:T(8,128)(2,1)S(1)}, u32[]{:S(2)}, u32[]{:S(2)}) async-start(bf16[16,88,256]{2,1,0:T(8,128)(2,1)} %get-tuple-element.391), calls=%async_computation.3 | async-start | bytes 1441792 | tf_op jit(solution)/shard_map/all_to_all | solution.py:283
  197.4 6.5 %collective-permute-done.38.refs_5_ = bf16[64,4096]{1,0:T(8,128)(2,1)S(1)} collective-permute-done((bf16[64,4096]{1,0:T(8,128)(2,1)}, bf16[64,4096]{1,0:T(8,128)(2,1)S(1)}, u32[]{:S(2)}, u32[]{:S(2)}) %collective-permute-start.38) | collective-permute-done | bytes 524320 | tf_op jit(solution)/shard_map/ppermute | solution.py:287
  219.2 5.3 %project.6 = (bf16[16,272,128]{2,1,0:T(8,128)(2,1)}, bf16[4,64,4096]{2,1,0:T(8,128)(2,1)}) custom-call(s32[3]{0:T(128)S(1)} %pad_add_fusion.scalars, bf16[88,256]{1,0:T(8,128)(2,1)S(1)} %close.5.refs_0_.x_ref, bf16[88,256]{1,0:T(8,128)(2,1)S(1)} %collective-permute-done.35.refs_1_, bf16[88,256]{1,0:T(8,128)(2,1)S(1)} %collective-permute-done.36.refs_2_, ...), custom_call_target="tpu_custom_call" | custom-call | flops 415236096 | bytes 6000000 | tf_op jit(solution)/shard_map/project/pallas_call | solution.py:155
  227.7 6.1 %all-to-all-start.4 = ((bf16[16,272,128]{2,1,0:T(8,128)(2,1)}), bf16[16,272,128]{2,1,0:T(8,128)(2,1)S(1)}, u32[]{:S(2)}, u32[]{:S(2)}) async-start(bf16[16,272,128]{2,1,0:T(8,128)(2,1)} %get-tuple-element.418), calls=%async_computation.4 | async-start | bytes 2228224 | tf_op jit(solution)/shard_map/all_to_all | solution.py:283
  233.7 8.1 %collective-permute-done.46.refs_7_ = bf16[128,2304]{1,0:T(8,128)(2,1)S(1)} collective-permute-done((bf16[128,2304]{1,0:T(8,128)(2,1)}, bf16[128,2304]{1,0:T(8,128)(2,1)S(1)}, u32[]{:S(2)}, u32[]{:S(2)}) %collective-permute-start.46) | collective-permute-done | bytes 589856 | tf_op jit(solution)/shard_map/ppermute | solution.py:287
  267.7 6.4 %all-to-all-start.5 = ((bf16[16,88,256]{2,1,0:T(8,128)(2,1)}), bf16[16,88,256]{2,1,0:T(8,128)(2,1)S(1)}, u32[]{:S(2)}, u32[]{:S(2)}) async-start(bf16[16,88,256]{2,1,0:T(8,128)(2,1)} %get-tuple-element.447), calls=%async_computation.5 | async-start | bytes 1441792 | tf_op jit(solution)/shard_map/all_to_all | solution.py:283
  274.1 5.5 %collective-permute-done.52.refs_5_ = bf16[64,4096]{1,0:T(8,128)(2,1)S(1)} collective-permute-done((bf16[64,4096]{1,0:T(8,128)(2,1)}, bf16[64,4096]{1,0:T(8,128)(2,1)S(1)}, u32[]{:S(2)}, u32[]{:S(2)}) %collective-permute-start.52) | collective-permute-done | bytes 524320 | tf_op jit(solution)/shard_map/ppermute | solution.py:287
  294.6 5.4 %project.7 = (bf16[16,272,128]{2,1,0:T(8,128)(2,1)}, bf16[4,64,4096]{2,1,0:T(8,128)(2,1)}) custom-call(s32[3]{0:T(128)S(1)} %pad_add_fusion.scalars, bf16[88,256]{1,0:T(8,128)(2,1)S(1)} %close.6.refs_0_.x_ref, bf16[88,256]{1,0:T(8,128)(2,1)S(1)} %collective-permute-done.49.refs_1_, bf16[88,256]{1,0:T(8,128)(2,1)S(1)} %collective-permute-done.50.refs_2_, ...), custom_call_target="tpu_custom_call" | custom-call | flops 415236096 | bytes 6000000 | tf_op jit(solution)/shard_map/project/pallas_call | solution.py:155
  302.1 22.2 %all_to_all.40.recv_ref = bf16[16,272,128]{2,1,0:T(8,128)(2,1)S(1)} all-to-all(bf16[16,272,128]{2,1,0:T(8,128)(2,1)} %get-tuple-element.464), channel_id=1, replica_groups=mesh['z'=4,'x'=4,'y'=4,'c'=2] {'x','y'}, dimensions={0} | all-to-all | bytes 2228224 | tf_op jit(solution)/shard_map/all_to_all | solution.py:283
  336.6 6.2 %all-to-all-start.7 = ((bf16[16,88,256]{2,1,0:T(8,128)(2,1)}), bf16[16,88,256]{2,1,0:T(8,128)(2,1)S(1)}, u32[]{:S(2)}, u32[]{:S(2)}) async-start(bf16[16,88,256]{2,1,0:T(8,128)(2,1)} %output.7), calls=%async_computation.7 | async-start | bytes 1441792 | tf_op jit(solution)/shard_map/all_to_all | solution.py:283
  342.8 7.7 %all-to-all-done.7.recv_ref = bf16[16,88,256]{2,1,0:T(8,128)(2,1)S(1)} async-done(((bf16[16,88,256]{2,1,0:T(8,128)(2,1)}), bf16[16,88,256]{2,1,0:T(8,128)(2,1)S(1)}, u32[]{:S(2)}, u32[]{:S(2)}) %all-to-all-start.7) | async-done | bytes 720928 | tf_op jit(solution)/shard_map/all_to_all | solution.py:283
  350.6 7.5 %collective-permute-start.63 = (bf16[88,256]{1,0:T(8,128)(2,1)S(1)}, bf16[88,256]{1,0:T(8,128)(2,1)S(1)}, u32[]{:S(2)}, u32[]{:S(2)}) collective-permute-start(bf16[88,256]{1,0:T(8,128)(2,1)S(1)} %get-tuple-element.482), channel_id=1, source_target_pairs={{0,96},{1,32},{2,0},{3,64},{4,97},{5,33},{6,1},{7,65},{8,98},{9,34... | collective-permute-start | bytes 135176 | tf_op jit(solution)/shard_map/ppermute | solution.py:385
  369.3 6.3 %collective-permute-done.60 = bf16[88,256]{1,0:T(8,128)(2,1)S(1)} collective-permute-done((bf16[88,256]{1,0:T(8,128)(2,1)S(1)}, bf16[88,256]{1,0:T(8,128)(2,1)S(1)}, u32[]{:S(2)}, u32[]{:S(2)}) %collective-permute-start.60) | collective-permute-done | bytes 45088 | tf_op jit(solution)/shard_map/ppermute | solution.py:385
  (209 shorter events, 200.0 us)
Async XLA Ops:
  19.7 16.2 %collective-permute-start.5 = (bf16[128,2304]{1,0:T(8,128)(2,1)}, bf16[128,2304]{1,0:T(8,128)(2,1)S(1)}, u32[]{:S(2)}, u32[]{:S(2)}) collective-permute-start(bf16[128,2304]{1,0:T(8,128)(2,1)} %get-tuple-element.247), channel_id=1, source_target_pairs={{0,96},{32,64},{64,32},{96,0},{1,97},{33,65},{65,33},{97,1},{2,98}... | collective-permute-start | bytes 1769480 | tf_op jit(solution)/shard_map/ppermute | solution.py:287
  22.0 16.0 %collective-permute-start.7 = (bf16[64,4096]{1,0:T(8,128)(2,1)S(1)}, bf16[64,4096]{1,0:T(8,128)(2,1)S(1)}, u32[]{:S(2)}, u32[]{:S(2)}) collective-permute-start(bf16[64,4096]{1,0:T(8,128)(2,1)S(1)} %copy-done.20), channel_id=1, source_target_pairs={{0,2},{2,0},{4,6},{6,4},{1,3},{3,1},{5,7},{7,5},{8,10},{10,8},{12,... | collective-permute-start | bytes 1572872 | tf_op jit(solution)/shard_map/ppermute | solution.py:287
  22.0 16.0 %collective-permute-start.8 = (bf16[64,4096]{1,0:T(8,128)(2,1)S(1)}, bf16[64,4096]{1,0:T(8,128)(2,1)S(1)}, u32[]{:S(2)}, u32[]{:S(2)}) collective-permute-start(bf16[64,4096]{1,0:T(8,128)(2,1)S(1)} %copy-done.19), channel_id=1, source_target_pairs={{0,6},{2,4},{4,2},{6,0},{1,7},{3,5},{5,3},{7,1},{8,14},{10,12},{12... | collective-permute-start | bytes 1572872 | tf_op jit(solution)/shard_map/ppermute | solution.py:287
  35.9 18.1 %collective-permute-start.6 = (bf16[128,2304]{1,0:T(8,128)(2,1)}, bf16[128,2304]{1,0:T(8,128)(2,1)S(1)}, u32[]{:S(2)}, u32[]{:S(2)}) collective-permute-start(bf16[128,2304]{1,0:T(8,128)(2,1)} %get-tuple-element.250), channel_id=1, source_target_pairs={{0,64},{32,96},{64,0},{96,32},{1,65},{33,97},{65,1},{97,33},{2,66}... | collective-permute-start | bytes 1769480 | tf_op jit(solution)/shard_map/ppermute | solution.py:287
  70.8 25.1 %collective-permute-start.14 = (bf16[4,64,4096]{2,1,0:T(8,128)(2,1)}, bf16[4,64,4096]{2,1,0:T(8,128)(2,1)}, u32[]{:S(2)}, u32[]{:S(2)}) collective-permute-start(bf16[4,64,4096]{2,1,0:T(8,128)(2,1)} %get-tuple-element.325.refs_4_), channel_id=1, source_target_pairs={{0,1},{1,0},{2,3},{3,2},{4,5},{5,4},{6,7},{7,6},{8,9},{9,8},{10,11... | collective-permute-start | bytes 6291464 | tf_op jit(solution)/shard_map/ppermute | solution.py:306
  73.6 16.0 %collective-permute-start.19 = (bf16[128,2304]{1,0:T(8,128)(2,1)}, bf16[128,2304]{1,0:T(8,128)(2,1)S(1)}, u32[]{:S(2)}, u32[]{:S(2)}) collective-permute-start(bf16[128,2304]{1,0:T(8,128)(2,1)} %get-tuple-element.312), channel_id=1, source_target_pairs={{0,96},{32,64},{64,32},{96,0},{1,97},{33,65},{65,33},{97,1},{2,98}... | collective-permute-start | bytes 1769480 | tf_op jit(solution)/shard_map/ppermute | solution.py:287
  74.3 21.6 %all-to-all-start = ((bf16[16,272,128]{2,1,0:T(8,128)(2,1)}), bf16[16,272,128]{2,1,0:T(8,128)(2,1)S(1)}, u32[]{:S(2)}, u32[]{:S(2)}) async-start(bf16[16,272,128]{2,1,0:T(8,128)(2,1)} %get-tuple-element.298), calls=%async_computation | async-start | bytes 2228224 | tf_op jit(solution)/shard_map/all_to_all | solution.py:283
  89.5 15.5 %collective-permute-start.20 = (bf16[128,2304]{1,0:T(8,128)(2,1)}, bf16[128,2304]{1,0:T(8,128)(2,1)}, u32[]{:S(2)}, u32[]{:S(2)}) collective-permute-start(bf16[128,2304]{1,0:T(8,128)(2,1)} %get-tuple-element.315), channel_id=1, source_target_pairs={{0,64},{32,96},{64,0},{96,32},{1,65},{33,97},{65,1},{97,33},{2,66}... | collective-permute-start | bytes 1769480 | tf_op jit(solution)/shard_map/ppermute | solution.py:287
  110.4 31.4 %collective-permute-start.27 = (bf16[4,128,2304]{2,1,0:T(8,128)(2,1)}, bf16[4,128,2304]{2,1,0:T(8,128)(2,1)}, u32[]{:S(2)}, u32[]{:S(2)}) collective-permute-start(bf16[4,128,2304]{2,1,0:T(8,128)(2,1)} %get-tuple-element.355.refs_9_.refs_11_), channel_id=1, source_target_pairs={{0,1},{1,0},{2,3},{3,2},{4,5},{5,4},{6,7},{7,6},{8,9},{9,8},{10,11... | collective-permute-start | bytes 7077896 | tf_op jit(solution)/shard_map/ppermute | solution.py:306
  114.8 18.0 %all-to-all-start.1 = ((bf16[16,88,256]{2,1,0:T(8,128)(2,1)}), bf16[16,88,256]{2,1,0:T(8,128)(2,1)S(1)}, u32[]{:S(2)}, u32[]{:S(2)}) async-start(bf16[16,88,256]{2,1,0:T(8,128)(2,1)} %get-tuple-element.331), calls=%async_computation.1 | async-start | bytes 1441792 | tf_op jit(solution)/shard_map/all_to_all | solution.py:283
  147.2 25.8 %collective-permute-start.28 = (bf16[4,64,4096]{2,1,0:T(8,128)(2,1)}, bf16[4,64,4096]{2,1,0:T(8,128)(2,1)}, u32[]{:S(2)}, u32[]{:S(2)}) collective-permute-start(bf16[4,64,4096]{2,1,0:T(8,128)(2,1)} %get-tuple-element.385.refs_4_), channel_id=1, source_target_pairs={{0,1},{1,0},{2,3},{3,2},{4,5},{5,4},{6,7},{7,6},{8,9},{9,8},{10,11... | collective-permute-start | bytes 6291464 | tf_op jit(solution)/shard_map/ppermute | solution.py:306
  150.0 16.0 %collective-permute-start.33 = (bf16[128,2304]{1,0:T(8,128)(2,1)}, bf16[128,2304]{1,0:T(8,128)(2,1)S(1)}, u32[]{:S(2)}, u32[]{:S(2)}) collective-permute-start(bf16[128,2304]{1,0:T(8,128)(2,1)} %get-tuple-element.372), channel_id=1, source_target_pairs={{0,96},{32,64},{64,32},{96,0},{1,97},{33,65},{65,33},{97,1},{2,98}... | collective-permute-start | bytes 1769480 | tf_op jit(solution)/shard_map/ppermute | solution.py:287
  151.7 21.3 %all-to-all-start.2 = ((bf16[16,272,128]{2,1,0:T(8,128)(2,1)}), bf16[16,272,128]{2,1,0:T(8,128)(2,1)S(1)}, u32[]{:S(2)}, u32[]{:S(2)}) async-start(bf16[16,272,128]{2,1,0:T(8,128)(2,1)} %get-tuple-element.358), calls=%async_computation.2 | async-start | bytes 2228224 | tf_op jit(solution)/shard_map/all_to_all | solution.py:283
  166.0 15.5 %collective-permute-start.34 = (bf16[128,2304]{1,0:T(8,128)(2,1)}, bf16[128,2304]{1,0:T(8,128)(2,1)}, u32[]{:S(2)}, u32[]{:S(2)}) collective-permute-start(bf16[128,2304]{1,0:T(8,128)(2,1)} %get-tuple-element.375), channel_id=1, source_target_pairs={{0,64},{32,96},{64,0},{96,32},{1,65},{33,97},{65,1},{97,33},{2,66}... | collective-permute-start | bytes 1769480 | tf_op jit(solution)/shard_map/ppermute | solution.py:287
  186.9 32.3 %collective-permute-start.41 = (bf16[4,128,2304]{2,1,0:T(8,128)(2,1)}, bf16[4,128,2304]{2,1,0:T(8,128)(2,1)}, u32[]{:S(2)}, u32[]{:S(2)}) collective-permute-start(bf16[4,128,2304]{2,1,0:T(8,128)(2,1)} %get-tuple-element.415.refs_9_.refs_11_), channel_id=1, source_target_pairs={{0,1},{1,0},{2,3},{3,2},{4,5},{5,4},{6,7},{7,6},{8,9},{9,8},{10,11... | collective-permute-start | bytes 7077896 | tf_op jit(solution)/shard_map/ppermute | solution.py:306
  192.1 16.7 %all-to-all-start.3 = ((bf16[16,88,256]{2,1,0:T(8,128)(2,1)}), bf16[16,88,256]{2,1,0:T(8,128)(2,1)S(1)}, u32[]{:S(2)}, u32[]{:S(2)}) async-start(bf16[16,88,256]{2,1,0:T(8,128)(2,1)} %get-tuple-element.391), calls=%async_computation.3 | async-start | bytes 1441792 | tf_op jit(solution)/shard_map/all_to_all | solution.py:283
  224.5 23.4 %collective-permute-start.42 = (bf16[4,64,4096]{2,1,0:T(8,128)(2,1)}, bf16[4,64,4096]{2,1,0:T(8,128)(2,1)}, u32[]{:S(2)}, u32[]{:S(2)}) collective-permute-start(bf16[4,64,4096]{2,1,0:T(8,128)(2,1)} %get-tuple-element.441.refs_4_), channel_id=1, source_target_pairs={{0,1},{1,0},{2,3},{3,2},{4,5},{5,4},{6,7},{7,6},{8,9},{9,8},{10,11... | collective-permute-start | bytes 6291464 | tf_op jit(solution)/shard_map/ppermute | solution.py:306
  227.2 16.1 %collective-permute-start.47 = (bf16[128,2304]{1,0:T(8,128)(2,1)}, bf16[128,2304]{1,0:T(8,128)(2,1)}, u32[]{:S(2)}, u32[]{:S(2)}) collective-permute-start(bf16[128,2304]{1,0:T(8,128)(2,1)} %get-tuple-element.428), channel_id=1, source_target_pairs={{0,96},{32,64},{64,32},{96,0},{1,97},{33,65},{65,33},{97,1},{2,98}... | collective-permute-start | bytes 1769480 | tf_op jit(solution)/shard_map/ppermute | solution.py:287
  227.7 20.2 %all-to-all-start.4 = ((bf16[16,272,128]{2,1,0:T(8,128)(2,1)}), bf16[16,272,128]{2,1,0:T(8,128)(2,1)S(1)}, u32[]{:S(2)}, u32[]{:S(2)}) async-start(bf16[16,272,128]{2,1,0:T(8,128)(2,1)} %get-tuple-element.418), calls=%async_computation.4 | async-start | bytes 2228224 | tf_op jit(solution)/shard_map/all_to_all | solution.py:283
  243.3 15.4 %collective-permute-start.48 = (bf16[128,2304]{1,0:T(8,128)(2,1)}, bf16[128,2304]{1,0:T(8,128)(2,1)S(1)}, u32[]{:S(2)}, u32[]{:S(2)}) collective-permute-start(bf16[128,2304]{1,0:T(8,128)(2,1)} %get-tuple-element.431), channel_id=1, source_target_pairs={{0,64},{32,96},{64,0},{96,32},{1,65},{33,97},{65,1},{97,33},{2,66}... | collective-permute-start | bytes 1769480 | tf_op jit(solution)/shard_map/ppermute | solution.py:287
  263.8 30.8 %collective-permute-start.55 = (bf16[4,128,2304]{2,1,0:T(8,128)(2,1)}, bf16[4,128,2304]{2,1,0:T(8,128)(2,1)}, u32[]{:S(2)}, u32[]{:S(2)}) collective-permute-start(bf16[4,128,2304]{2,1,0:T(8,128)(2,1)} %get-tuple-element.463.refs_9_.refs_11_), channel_id=1, source_target_pairs={{0,1},{1,0},{2,3},{3,2},{4,5},{5,4},{6,7},{7,6},{8,9},{9,8},{10,11... | collective-permute-start | bytes 7077896 | tf_op jit(solution)/shard_map/ppermute | solution.py:306
  267.7 17.8 %all-to-all-start.5 = ((bf16[16,88,256]{2,1,0:T(8,128)(2,1)}), bf16[16,88,256]{2,1,0:T(8,128)(2,1)S(1)}, u32[]{:S(2)}, u32[]{:S(2)}) async-start(bf16[16,88,256]{2,1,0:T(8,128)(2,1)} %get-tuple-element.447), calls=%async_computation.5 | async-start | bytes 1441792 | tf_op jit(solution)/shard_map/all_to_all | solution.py:283
  300.0 24.3 %collective-permute-start.56 = (bf16[4,64,4096]{2,1,0:T(8,128)(2,1)}, bf16[4,64,4096]{2,1,0:T(8,128)(2,1)S(1)}, u32[]{:S(2)}, u32[]{:S(2)}) collective-permute-start(bf16[4,64,4096]{2,1,0:T(8,128)(2,1)} %get-tuple-element.467.refs_4_), channel_id=1, source_target_pairs={{0,1},{1,0},{2,3},{3,2},{4,5},{5,4},{6,7},{7,6},{8,9},{9,8},{10,11... | collective-permute-start | bytes 6291464 | tf_op jit(solution)/shard_map/ppermute | solution.py:306
  350.6 17.4 %collective-permute-start.63 = (bf16[88,256]{1,0:T(8,128)(2,1)S(1)}, bf16[88,256]{1,0:T(8,128)(2,1)S(1)}, u32[]{:S(2)}, u32[]{:S(2)}) collective-permute-start(bf16[88,256]{1,0:T(8,128)(2,1)S(1)} %get-tuple-element.482), channel_id=1, source_target_pairs={{0,96},{1,32},{2,0},{3,64},{4,97},{5,33},{6,1},{7,65},{8,98},{9,34... | collective-permute-start | bytes 135176 | tf_op jit(solution)/shard_map/ppermute | solution.py:385
  (68 other events, 676.4 us)

commit v4 on v3

--- a/solution.py
+++ b/solution.py
@@ -111,11 +111,15 @@
 
 
 def project_kernel(layer, scalars, *refs):
-    xs, pieces, refs = refs[:4], refs[4:8], refs[8:]
-    gain_ref, own, other, kv_own, kv_other, out_ref, joined_ref, xg_ref, lead_ref = refs
+    xs, (gain_ref, own, other, kv_own, kv_other), refs = refs[:4], refs[4:9], refs[9:]
+    if len(refs) == 8:
+        pieces, out_ref, joined_ref = refs[:4], refs[4], refs[5]
+        for k in range(4):
+            joined_ref[k] = pieces[k][...]
+    else:
+        out_ref = refs[0]
+    xg_ref, lead_ref = refs[-2:]
     z, core = scalars[0], scalars[2]
-    for k in range(4):
-        joined_ref[k] = pieces[k][...]
 
     @pl.when(pl.program_id(0) == 0)
     def _():
@@ -152,28 +156,26 @@
 
 
 def project(layer, scalars, xs, gains, weights, pieces):
+    specs = [SMEM] + [whole(SEQ, COLS)] * 4 + [whole(4, 4, COLS)]
+    specs += [pl.BlockSpec((4, 128, 512), lambda s: (0, 0, s))] * 2
+    specs += [pl.BlockSpec((4, 128, 256), lambda s: (0, 0, 8))] * 2
+    outs = [pltpu.HBM((16, ROWS, 128), bf16)]
+    out_specs = [pl.BlockSpec((4, ROWS, 128), lambda s: (s, 0, 0))]
+    if pieces:
+        specs += [pl.BlockSpec((64, 1024), lambda s: (0, s))] * 4
+        outs.append(pltpu.HBM((4, 64, OCOLS), bf16))
+        out_specs.append(pl.BlockSpec((4, 64, 1024), lambda s: (0, 0, s)))
     return pl.pallas_call(
         functools.partial(project_kernel, layer),
         grid=(4,),
-        in_specs=[SMEM]
-        + [whole(SEQ, COLS)] * 4
-        + [pl.BlockSpec((64, 1024), lambda s: (0, s))] * 4
-        + [whole(4, 4, COLS)]
-        + [pl.BlockSpec((4, 128, 512), lambda s: (0, 0, s))] * 2
-        + [pl.BlockSpec((4, 128, 256), lambda s: (0, 0, 8))] * 2,
-        out_specs=[
-            pl.BlockSpec((4, ROWS, 128), lambda s: (s, 0, 0)),
-            pl.BlockSpec((4, 64, 1024), lambda s: (0, 0, s)),
-        ],
-        out_shape=[
-            jax.ShapeDtypeStruct((16, ROWS, 128), bf16),
-            jax.ShapeDtypeStruct((4, 64, OCOLS), bf16),
-        ],
+        in_specs=specs,
+        out_specs=out_specs,
+        out_shape=outs,
         scratch_shapes=[pltpu.VMEM((SEQ, 1024), bf16), pltpu.VMEM((8 + 2 * SEQ, 128), f32)],
         compiler_params=PARAMS,
-        cost_estimate=cost(2 * SEQ * 1024 * SLAB, 6_000_000),
+        cost_estimate=cost(2 * SEQ * 1024 * SLAB, 10_000_000),
         name="project",
-    )(scalars, *xs, *pieces, gains, *weights, *weights)
+    )(scalars, *xs, gains, *weights, *weights, *pieces)
 
 
 def attend_kernel(recv_ref, out_ref, acc):
@@ -288,8 +290,7 @@
 
 
 def line(value, axis):
-    near, far = (across_line(value, axis, by) for by in (1, 2))
-    return [value, near, far, across_line(near, axis, 2)]
+    return [value] + [across_line(value, axis, k) for k in range(1, 4)]
 
 
 def after(gate, values):
@@ -325,9 +326,11 @@
         gain = lax.dynamic_slice(norm_gain, (0, lax.rem(s, 2) * COLS), (1, COLS))
         piece = jnp.concatenate([piece, jnp.broadcast_to(gain, (8, COLS))], axis=0)
         rounds.append(lax.ppermute(piece, ALL, pairs))
-    rounds, (slab, cut) = after(rounds, (inward(0), slab_out(0, scalars, output_weight)))
-    ins = relay(slab, "z")
-    outs = relay(cut, "y")
+    slab, cut = inward(0), slab_out(0, scalars, output_weight)
+    near = [across_line(slab[k], "z", k) for k in (1, 3)]
+    rounds, (near, far, cut) = after(rounds, (near, slab[2], cut))
+    ins = [slab[0], near[0], across_line(far, "z", 2), near[1]]
+    near = [across_line(cut[k], "y", k) for k in (1, 3)]
     rounds = jnp.stack(rounds)
     xs = [
         lax.dynamic_index_in_dim(
@@ -342,16 +345,23 @@
         ]
     )
     ahead = inward(1)
-    ins, (outs, ahead, xs, gains) = after(ins, (outs, ahead, xs, gains))
+    ins, (near, far, ahead, xs, gains) = after(ins, (near, cut[2], ahead, xs, gains))
+    outs = [cut[0], near[0], across_line(far, "y", 2), near[1]]
     ins = swapped(join(ins))
     gains = jnp.stack(line(gains, "z")).astype(f32)
     states = []
     for layer in range(4):
-        xs, outs = after(xs, outs)
+        if layer:
+            xs, outs = after(xs, outs)
         if layer < 3:
             xs, slab = after(xs, ahead)
             ins_next = relay(slab, "z")
-        partial, outs = project(layer, scalars, xs, gains, ins, outs)
+        if layer:
+            partial, outs = project(layer, scalars, xs, gains, ins, outs)
+        else:
+            partial = project(layer, scalars, xs, gains, ins, [])[0]
+            partial, outs = after(partial, outs)
+            outs = join(outs)
         if layer < 3:
             ins = ins_next
             partial, scalars = after(partial, scalars)

time: 378 us -> 366 us (0.968)
  waiting for transfers between devices: 144 us -> 122 us
  starting transfers between devices: 135 us -> 143 us
    ppermute x48, waiting for transfers between devices: 114 us -> 90.3 us  [across_line(): return lax.ppermute(value, axis, [(i, i ^ by) for i in range(4)])]
    ppermute x48, starting transfers between devices: 48.1 us -> 52.6 us  [across_line(): return lax.ppermute(value, axis, [(i, i ^ by) for i in range(4)])]
  transfers between devices with their start and end apart: 71 -> 71, of which waited for: 48 -> 42; matrix products, arithmetic and copies ran while one was open for 0% -> 0% of each run, Pallas kernels for 7% -> 7%
where the time goes in v4:
time: 366 us; the launch traced here: 365 us
  starting transfers between devices  143 us (39%)
  waiting for transfers between devices  122 us (33%)
  Pallas kernels  71.4 us (20%)
  blocking collectives  22.1 us (6%)
  local copies, waits for them, and re-layouts  4.6 us (1%)
    ppermute x48, waiting for transfers between devices, across_line(): return lax.ppermute(value, axis, [(i, i ^ by) for i in range(4)])  90.3 us
    ppermute x48, starting transfers between devices, across_line(): return lax.ppermute(value, axis, [(i, i ^ by) for i in range(4)])  52.6 us
    all_to_all x7, starting transfers between devices, exchange(): return lax.all_to_all(value, axes, 0, 0, tiled=True)  46.1 us
    ppermute x8, starting transfers between devices, body(): rounds.append(lax.ppermute(piece, ALL, pairs))  28.5 us
    all_to_all x1, blocking collectives, exchange(): return lax.all_to_all(value, axes, 0, 0, tiled=True)  22.1 us
    pallas_call x4, Pallas kernels, project(): pl.pallas_call(functools.partial(project_kernel, layer), grid=(4,), in_sp...  20.9 us
    all_to_all x7, waiting for transfers between devices, exchange(): return lax.all_to_all(value, axes, 0, 0, tiled=True)  20.9 us
    pallas_call x4, Pallas kernels, output(): pl.pallas_call(output_kernel, grid=(4,), in_specs=specs, out_specs=out_sp...  20.5 us
  transfers between devices with their start and end apart: 71, of which 42 were waited for; matrix products, arithmetic and copies ran while one was open for 0% of the time, Pallas kernels for 7%

profile of v4, /device:TPU:5, one launch (start us, length us, event | category | flops | bytes accessed | tf_op | source)
XLA Modules:
  0.0 364.5 jit_solution(7295126797364525382)
XLA Ops:
  30.9 8.1 %collective-permute-done.7.refs_1_ = bf16[64,4096]{1,0:T(8,128)(2,1)S(1)} collective-permute-done((bf16[64,4096]{1,0:T(8,128)(2,1)}, bf16[64,4096]{1,0:T(8,128)(2,1)S(1)}, u32[]{:S(2)}, u32[]{:S(2)}) %collective-permute-start.7) | collective-permute-done | bytes 524320 | tf_op jit(solution)/shard_map/ppermute | solution.py:289
  66.0 6.7 %all-to-all-start = ((bf16[16,272,128]{2,1,0:T(8,128)(2,1)}), bf16[16,272,128]{2,1,0:T(8,128)(2,1)S(1)}, u32[]{:S(2)}, u32[]{:S(2)}) async-start(bf16[16,272,128]{2,1,0:T(8,128)(2,1)} %project.4), calls=%async_computation | async-start | bytes 2228224 | tf_op jit(solution)/shard_map/all_to_all | solution.py:285
  72.7 6.8 %collective-permute-done.18.refs_7_ = bf16[128,2304]{1,0:T(8,128)(2,1)S(1)} collective-permute-done((bf16[128,2304]{1,0:T(8,128)(2,1)}, bf16[128,2304]{1,0:T(8,128)(2,1)S(1)}, u32[]{:S(2)}, u32[]{:S(2)}) %collective-permute-start.18) | collective-permute-done | bytes 589856 | tf_op jit(solution)/shard_map/ppermute | solution.py:289
  96.7 5.3 %output.4 = (bf16[16,88,256]{2,1,0:T(8,128)(2,1)}, bf16[4,128,2304]{2,1,0:T(8,128)(2,1)}) custom-call(s32[3]{0:T(128)S(1)} %pad_add_fusion.scalars, bf16[88,128]{1,0:T(8,128)(2,1)S(1)} %attend.4.refs_0_, bf16[88,128]{1,0:T(8,128)(2,1)S(1)} %collective-permute-done.15.refs_1_, bf16[88,128]{1,0:T(8,128)(2,1)S(1)} %collective-permute-done.16.refs_2_, ...), custom_call_target="tpu_custom_call" | custom-call | flops 369098752 | bytes 10000000 | tf_op jit(solution)/shard_map/output/pallas_call | solution.py:254
  105.3 6.9 %all-to-all-start.1 = ((bf16[16,88,256]{2,1,0:T(8,128)(2,1)}), bf16[16,88,256]{2,1,0:T(8,128)(2,1)S(1)}, u32[]{:S(2)}, u32[]{:S(2)}) async-start(bf16[16,88,256]{2,1,0:T(8,128)(2,1)} %get-tuple-element.305), calls=%async_computation.1 | async-start | bytes 1441792 | tf_op jit(solution)/shard_map/all_to_all | solution.py:285
  112.2 5.6 %collective-permute-done.24.refs_10_ = bf16[64,4096]{1,0:T(8,128)(2,1)S(1)} collective-permute-done((bf16[64,4096]{1,0:T(8,128)(2,1)}, bf16[64,4096]{1,0:T(8,128)(2,1)S(1)}, u32[]{:S(2)}, u32[]{:S(2)}) %collective-permute-start.24) | collective-permute-done | bytes 524320 | tf_op jit(solution)/shard_map/ppermute | solution.py:289
  133.2 5.4 %project.5 = (bf16[16,272,128]{2,1,0:T(8,128)(2,1)}, bf16[4,64,4096]{2,1,0:T(8,128)(2,1)}) custom-call(s32[3]{0:T(128)S(1)} %pad_add_fusion.scalars, bf16[88,256]{1,0:T(8,128)(2,1)S(1)} %close.4.refs_0_.x_ref, bf16[88,256]{1,0:T(8,128)(2,1)S(1)} %collective-permute-done.21.refs_1_, bf16[88,256]{1,0:T(8,128)(2,1)S(1)} %collective-permute-done.22.refs_2_, ...), custom_call_target="tpu_custom_call" | custom-call | flops 415236096 | bytes 10000000 | tf_op jit(solution)/shard_map/project/pallas_call | solution.py:168
  141.8 7.3 %all-to-all-start.2 = ((bf16[16,272,128]{2,1,0:T(8,128)(2,1)}), bf16[16,272,128]{2,1,0:T(8,128)(2,1)S(1)}, u32[]{:S(2)}, u32[]{:S(2)}) async-start(bf16[16,272,128]{2,1,0:T(8,128)(2,1)} %get-tuple-element.332), calls=%async_computation.2 | async-start | bytes 2228224 | tf_op jit(solution)/shard_map/all_to_all | solution.py:285
  149.1 6.6 %collective-permute-done.32.refs_7_ = bf16[128,2304]{1,0:T(8,128)(2,1)S(1)} collective-permute-done((bf16[128,2304]{1,0:T(8,128)(2,1)}, bf16[128,2304]{1,0:T(8,128)(2,1)S(1)}, u32[]{:S(2)}, u32[]{:S(2)}) %collective-permute-start.32) | collective-permute-done | bytes 589856 | tf_op jit(solution)/shard_map/ppermute | solution.py:289
  172.5 5.3 %output.5 = (bf16[16,88,256]{2,1,0:T(8,128)(2,1)}, bf16[4,128,2304]{2,1,0:T(8,128)(2,1)}) custom-call(s32[3]{0:T(128)S(1)} %pad_add_fusion.scalars, bf16[88,128]{1,0:T(8,128)(2,1)S(1)} %attend.5.refs_0_, bf16[88,128]{1,0:T(8,128)(2,1)S(1)} %collective-permute-done.29.refs_1_, bf16[88,128]{1,0:T(8,128)(2,1)S(1)} %collective-permute-done.30.refs_2_, ...), custom_call_target="tpu_custom_call" | custom-call | flops 369098752 | bytes 10000000 | tf_op jit(solution)/shard_map/output/pallas_call | solution.py:254
  181.6 6.5 %all-to-all-start.3 = ((bf16[16,88,256]{2,1,0:T(8,128)(2,1)}), bf16[16,88,256]{2,1,0:T(8,128)(2,1)S(1)}, u32[]{:S(2)}, u32[]{:S(2)}) async-start(bf16[16,88,256]{2,1,0:T(8,128)(2,1)} %get-tuple-element.365), calls=%async_computation.3 | async-start | bytes 1441792 | tf_op jit(solution)/shard_map/all_to_all | solution.py:285
  188.1 5.6 %collective-permute-done.38.refs_10_ = bf16[64,4096]{1,0:T(8,128)(2,1)S(1)} collective-permute-done((bf16[64,4096]{1,0:T(8,128)(2,1)}, bf16[64,4096]{1,0:T(8,128)(2,1)S(1)}, u32[]{:S(2)}, u32[]{:S(2)}) %collective-permute-start.38) | collective-permute-done | bytes 524320 | tf_op jit(solution)/shard_map/ppermute | solution.py:289
  208.5 5.3 %project.6 = (bf16[16,272,128]{2,1,0:T(8,128)(2,1)}, bf16[4,64,4096]{2,1,0:T(8,128)(2,1)}) custom-call(s32[3]{0:T(128)S(1)} %pad_add_fusion.scalars, bf16[88,256]{1,0:T(8,128)(2,1)S(1)} %close.5.refs_0_.x_ref, bf16[88,256]{1,0:T(8,128)(2,1)S(1)} %collective-permute-done.35.refs_1_, bf16[88,256]{1,0:T(8,128)(2,1)S(1)} %collective-permute-done.36.refs_2_, ...), custom_call_target="tpu_custom_call" | custom-call | flops 415236096 | bytes 10000000 | tf_op jit(solution)/shard_map/project/pallas_call | solution.py:168
  217.5 6.8 %all-to-all-start.4 = ((bf16[16,272,128]{2,1,0:T(8,128)(2,1)}), bf16[16,272,128]{2,1,0:T(8,128)(2,1)S(1)}, u32[]{:S(2)}, u32[]{:S(2)}) async-start(bf16[16,272,128]{2,1,0:T(8,128)(2,1)} %get-tuple-element.392), calls=%async_computation.4 | async-start | bytes 2228224 | tf_op jit(solution)/shard_map/all_to_all | solution.py:285
  224.3 6.8 %collective-permute-done.46.refs_7_ = bf16[128,2304]{1,0:T(8,128)(2,1)S(1)} collective-permute-done((bf16[128,2304]{1,0:T(8,128)(2,1)}, bf16[128,2304]{1,0:T(8,128)(2,1)S(1)}, u32[]{:S(2)}, u32[]{:S(2)}) %collective-permute-start.46) | collective-permute-done | bytes 589856 | tf_op jit(solution)/shard_map/ppermute | solution.py:289
  256.8 6.3 %all-to-all-start.5 = ((bf16[16,88,256]{2,1,0:T(8,128)(2,1)}), bf16[16,88,256]{2,1,0:T(8,128)(2,1)S(1)}, u32[]{:S(2)}, u32[]{:S(2)}) async-start(bf16[16,88,256]{2,1,0:T(8,128)(2,1)} %get-tuple-element.421), calls=%async_computation.5 | async-start | bytes 1441792 | tf_op jit(solution)/shard_map/all_to_all | solution.py:285
  263.1 5.6 %collective-permute-done.52.refs_10_ = bf16[64,4096]{1,0:T(8,128)(2,1)S(1)} collective-permute-done((bf16[64,4096]{1,0:T(8,128)(2,1)}, bf16[64,4096]{1,0:T(8,128)(2,1)S(1)}, u32[]{:S(2)}, u32[]{:S(2)}) %collective-permute-start.52) | collective-permute-done | bytes 524320 | tf_op jit(solution)/shard_map/ppermute | solution.py:289
  283.7 5.3 %project.7 = (bf16[16,272,128]{2,1,0:T(8,128)(2,1)}, bf16[4,64,4096]{2,1,0:T(8,128)(2,1)}) custom-call(s32[3]{0:T(128)S(1)} %pad_add_fusion.scalars, bf16[88,256]{1,0:T(8,128)(2,1)S(1)} %close.6.refs_0_.x_ref, bf16[88,256]{1,0:T(8,128)(2,1)S(1)} %collective-permute-done.49.refs_1_, bf16[88,256]{1,0:T(8,128)(2,1)S(1)} %collective-permute-done.50.refs_2_, ...), custom_call_target="tpu_custom_call" | custom-call | flops 415236096 | bytes 10000000 | tf_op jit(solution)/shard_map/project/pallas_call | solution.py:168
  291.1 22.1 %all_to_all.40.recv_ref = bf16[16,272,128]{2,1,0:T(8,128)(2,1)S(1)} all-to-all(bf16[16,272,128]{2,1,0:T(8,128)(2,1)} %get-tuple-element.438), channel_id=1, replica_groups=mesh['z'=4,'x'=4,'y'=4,'c'=2] {'x','y'}, dimensions={0} | all-to-all | bytes 2228224 | tf_op jit(solution)/shard_map/all_to_all | solution.py:285
  324.8 5.5 %all-to-all-start.7 = ((bf16[16,88,256]{2,1,0:T(8,128)(2,1)}), bf16[16,88,256]{2,1,0:T(8,128)(2,1)S(1)}, u32[]{:S(2)}, u32[]{:S(2)}) async-start(bf16[16,88,256]{2,1,0:T(8,128)(2,1)} %output.7), calls=%async_computation.7 | async-start | bytes 1441792 | tf_op jit(solution)/shard_map/all_to_all | solution.py:285
  330.3 7.7 %all-to-all-done.7.recv_ref = bf16[16,88,256]{2,1,0:T(8,128)(2,1)S(1)} async-done(((bf16[16,88,256]{2,1,0:T(8,128)(2,1)}), bf16[16,88,256]{2,1,0:T(8,128)(2,1)S(1)}, u32[]{:S(2)}, u32[]{:S(2)}) %all-to-all-start.7) | async-done | bytes 720928 | tf_op jit(solution)/shard_map/all_to_all | solution.py:285
  338.2 6.3 %collective-permute-start.63 = (bf16[88,256]{1,0:T(8,128)(2,1)S(1)}, bf16[88,256]{1,0:T(8,128)(2,1)S(1)}, u32[]{:S(2)}, u32[]{:S(2)}) collective-permute-start(bf16[88,256]{1,0:T(8,128)(2,1)S(1)} %get-tuple-element.456), channel_id=1, source_target_pairs={{0,96},{1,32},{2,0},{3,64},{4,97},{5,33},{6,1},{7,65},{8,98},{9,34... | collective-permute-start | bytes 135176 | tf_op jit(solution)/shard_map/ppermute | solution.py:395
  345.4 6.6 %collective-permute-start.61 = (bf16[88,256]{1,0:T(8,128)(2,1)S(1)}, bf16[88,256]{1,0:T(8,128)(2,1)S(1)}, u32[]{:S(2)}, u32[]{:S(2)}) collective-permute-start(bf16[88,256]{1,0:T(8,128)(2,1)S(1)} %get-tuple-element.458), channel_id=1, source_target_pairs={{0,32},{1,96},{2,64},{3,0},{4,33},{5,97},{6,65},{7,1},{8,34},{9,98... | collective-permute-start | bytes 135176 | tf_op jit(solution)/shard_map/ppermute | solution.py:395
  355.7 8.0 %collective-permute-done.60 = bf16[88,256]{1,0:T(8,128)(2,1)S(1)} collective-permute-done((bf16[88,256]{1,0:T(8,128)(2,1)S(1)}, bf16[88,256]{1,0:T(8,128)(2,1)S(1)}, u32[]{:S(2)}, u32[]{:S(2)}) %collective-permute-start.60) | collective-permute-done | bytes 45088 | tf_op jit(solution)/shard_map/ppermute | solution.py:395
  (208 shorter events, 195.5 us)
Async XLA Ops:
  4.9 20.4 %collective-permute-start.4 = (bf16[128,2304]{1,0:T(8,128)(2,1)}, bf16[128,2304]{1,0:T(8,128)(2,1)S(1)}, u32[]{:S(2)}, u32[]{:S(2)}) collective-permute-start(bf16[128,2304]{1,0:T(8,128)(2,1)} %get-tuple-element.225), channel_id=1, source_target_pairs={{0,32},{32,0},{64,96},{96,64},{1,33},{33,1},{65,97},{97,65},{2,34}... | collective-permute-start | bytes 1769480 | tf_op jit(solution)/shard_map/ppermute | solution.py:289
  6.6 18.8 %collective-permute-start.5 = (bf16[128,2304]{1,0:T(8,128)(2,1)}, bf16[128,2304]{1,0:T(8,128)(2,1)S(1)}, u32[]{:S(2)}, u32[]{:S(2)}) collective-permute-start(bf16[128,2304]{1,0:T(8,128)(2,1)} %get-tuple-element.226), channel_id=1, source_target_pairs={{0,96},{32,64},{64,32},{96,0},{1,97},{33,65},{65,33},{97,1},{2,98}... | collective-permute-start | bytes 1769480 | tf_op jit(solution)/shard_map/ppermute | solution.py:289
  63.5 24.0 %collective-permute-start.14 = (bf16[4,64,4096]{2,1,0:T(8,128)(2,1)}, bf16[4,64,4096]{2,1,0:T(8,128)(2,1)}, u32[]{:S(2)}, u32[]{:S(2)}) collective-permute-start(bf16[4,64,4096]{2,1,0:T(8,128)(2,1)} %join.3.refs_4_), channel_id=1, source_target_pairs={{0,1},{1,0},{2,3},{3,2},{4,5},{5,4},{6,7},{7,6},{8,9},{9,8},{10,11... | collective-permute-start | bytes 6291464 | tf_op jit(solution)/shard_map/ppermute | solution.py:307
  64.3 15.2 %collective-permute-start.18 = (bf16[128,2304]{1,0:T(8,128)(2,1)}, bf16[128,2304]{1,0:T(8,128)(2,1)S(1)}, u32[]{:S(2)}, u32[]{:S(2)}) collective-permute-start(bf16[128,2304]{1,0:T(8,128)(2,1)} %get-tuple-element.285), channel_id=1, source_target_pairs={{0,32},{32,0},{64,96},{96,64},{1,33},{33,1},{65,97},{97,65},{2,34}... | collective-permute-start | bytes 1769480 | tf_op jit(solution)/shard_map/ppermute | solution.py:289
  65.0 16.1 %collective-permute-start.19 = (bf16[128,2304]{1,0:T(8,128)(2,1)}, bf16[128,2304]{1,0:T(8,128)(2,1)S(1)}, u32[]{:S(2)}, u32[]{:S(2)}) collective-permute-start(bf16[128,2304]{1,0:T(8,128)(2,1)} %get-tuple-element.286), channel_id=1, source_target_pairs={{0,96},{32,64},{64,32},{96,0},{1,97},{33,65},{65,33},{97,1},{2,98}... | collective-permute-start | bytes 1769480 | tf_op jit(solution)/shard_map/ppermute | solution.py:289
  66.0 21.5 %all-to-all-start = ((bf16[16,272,128]{2,1,0:T(8,128)(2,1)}), bf16[16,272,128]{2,1,0:T(8,128)(2,1)S(1)}, u32[]{:S(2)}, u32[]{:S(2)}) async-start(bf16[16,272,128]{2,1,0:T(8,128)(2,1)} %project.4), calls=%async_computation | async-start | bytes 2228224 | tf_op jit(solution)/shard_map/all_to_all | solution.py:285
  81.1 15.5 %collective-permute-start.20 = (bf16[128,2304]{1,0:T(8,128)(2,1)}, bf16[128,2304]{1,0:T(8,128)(2,1)}, u32[]{:S(2)}, u32[]{:S(2)}) collective-permute-start(bf16[128,2304]{1,0:T(8,128)(2,1)} %get-tuple-element.289), channel_id=1, source_target_pairs={{0,64},{32,96},{64,0},{96,32},{1,65},{33,97},{65,1},{97,33},{2,66}... | collective-permute-start | bytes 1769480 | tf_op jit(solution)/shard_map/ppermute | solution.py:289
  102.0 31.2 %collective-permute-start.27 = (bf16[4,128,2304]{2,1,0:T(8,128)(2,1)}, bf16[4,128,2304]{2,1,0:T(8,128)(2,1)}, u32[]{:S(2)}, u32[]{:S(2)}) collective-permute-start(bf16[4,128,2304]{2,1,0:T(8,128)(2,1)} %get-tuple-element.325.refs_5_.refs_7_), channel_id=1, source_target_pairs={{0,1},{1,0},{2,3},{3,2},{4,5},{5,4},{6,7},{7,6},{8,9},{9,8},{10,11... | collective-permute-start | bytes 7077896 | tf_op jit(solution)/shard_map/ppermute | solution.py:307
  105.3 18.5 %all-to-all-start.1 = ((bf16[16,88,256]{2,1,0:T(8,128)(2,1)}), bf16[16,88,256]{2,1,0:T(8,128)(2,1)S(1)}, u32[]{:S(2)}, u32[]{:S(2)}) async-start(bf16[16,88,256]{2,1,0:T(8,128)(2,1)} %get-tuple-element.305), calls=%async_computation.1 | async-start | bytes 1441792 | tf_op jit(solution)/shard_map/all_to_all | solution.py:285
  138.6 24.7 %collective-permute-start.28 = (bf16[4,64,4096]{2,1,0:T(8,128)(2,1)}, bf16[4,64,4096]{2,1,0:T(8,128)(2,1)}, u32[]{:S(2)}, u32[]{:S(2)}) collective-permute-start(bf16[4,64,4096]{2,1,0:T(8,128)(2,1)} %get-tuple-element.359.refs_4_), channel_id=1, source_target_pairs={{0,1},{1,0},{2,3},{3,2},{4,5},{5,4},{6,7},{7,6},{8,9},{9,8},{10,11... | collective-permute-start | bytes 6291464 | tf_op jit(solution)/shard_map/ppermute | solution.py:307
  140.6 16.2 %collective-permute-start.33 = (bf16[128,2304]{1,0:T(8,128)(2,1)}, bf16[128,2304]{1,0:T(8,128)(2,1)S(1)}, u32[]{:S(2)}, u32[]{:S(2)}) collective-permute-start(bf16[128,2304]{1,0:T(8,128)(2,1)} %get-tuple-element.346), channel_id=1, source_target_pairs={{0,96},{32,64},{64,32},{96,0},{1,97},{33,65},{65,33},{97,1},{2,98}... | collective-permute-start | bytes 1769480 | tf_op jit(solution)/shard_map/ppermute | solution.py:289
  141.8 21.5 %all-to-all-start.2 = ((bf16[16,272,128]{2,1,0:T(8,128)(2,1)}), bf16[16,272,128]{2,1,0:T(8,128)(2,1)S(1)}, u32[]{:S(2)}, u32[]{:S(2)}) async-start(bf16[16,272,128]{2,1,0:T(8,128)(2,1)} %get-tuple-element.332), calls=%async_computation.2 | async-start | bytes 2228224 | tf_op jit(solution)/shard_map/all_to_all | solution.py:285
  156.8 15.7 %collective-permute-start.34 = (bf16[128,2304]{1,0:T(8,128)(2,1)}, bf16[128,2304]{1,0:T(8,128)(2,1)}, u32[]{:S(2)}, u32[]{:S(2)}) collective-permute-start(bf16[128,2304]{1,0:T(8,128)(2,1)} %get-tuple-element.349), channel_id=1, source_target_pairs={{0,64},{32,96},{64,0},{96,32},{1,65},{33,97},{65,1},{97,33},{2,66}... | collective-permute-start | bytes 1769480 | tf_op jit(solution)/shard_map/ppermute | solution.py:289
  177.8 30.7 %collective-permute-start.41 = (bf16[4,128,2304]{2,1,0:T(8,128)(2,1)}, bf16[4,128,2304]{2,1,0:T(8,128)(2,1)}, u32[]{:S(2)}, u32[]{:S(2)}) collective-permute-start(bf16[4,128,2304]{2,1,0:T(8,128)(2,1)} %get-tuple-element.385.refs_5_.refs_7_), channel_id=1, source_target_pairs={{0,1},{1,0},{2,3},{3,2},{4,5},{5,4},{6,7},{7,6},{8,9},{9,8},{10,11... | collective-permute-start | bytes 7077896 | tf_op jit(solution)/shard_map/ppermute | solution.py:307
  181.6 17.9 %all-to-all-start.3 = ((bf16[16,88,256]{2,1,0:T(8,128)(2,1)}), bf16[16,88,256]{2,1,0:T(8,128)(2,1)S(1)}, u32[]{:S(2)}, u32[]{:S(2)}) async-start(bf16[16,88,256]{2,1,0:T(8,128)(2,1)} %get-tuple-element.365), calls=%async_computation.3 | async-start | bytes 1441792 | tf_op jit(solution)/shard_map/all_to_all | solution.py:285
  213.8 24.7 %collective-permute-start.42 = (bf16[4,64,4096]{2,1,0:T(8,128)(2,1)}, bf16[4,64,4096]{2,1,0:T(8,128)(2,1)}, u32[]{:S(2)}, u32[]{:S(2)}) collective-permute-start(bf16[4,64,4096]{2,1,0:T(8,128)(2,1)} %get-tuple-element.415.refs_4_), channel_id=1, source_target_pairs={{0,1},{1,0},{2,3},{3,2},{4,5},{5,4},{6,7},{7,6},{8,9},{9,8},{10,11... | collective-permute-start | bytes 6291464 | tf_op jit(solution)/shard_map/ppermute | solution.py:307
  215.9 15.2 %collective-permute-start.46 = (bf16[128,2304]{1,0:T(8,128)(2,1)}, bf16[128,2304]{1,0:T(8,128)(2,1)S(1)}, u32[]{:S(2)}, u32[]{:S(2)}) collective-permute-start(bf16[128,2304]{1,0:T(8,128)(2,1)} %get-tuple-element.401), channel_id=1, source_target_pairs={{0,32},{32,0},{64,96},{96,64},{1,33},{33,1},{65,97},{97,65},{2,34}... | collective-permute-start | bytes 1769480 | tf_op jit(solution)/shard_map/ppermute | solution.py:289
  216.2 16.1 %collective-permute-start.47 = (bf16[128,2304]{1,0:T(8,128)(2,1)}, bf16[128,2304]{1,0:T(8,128)(2,1)}, u32[]{:S(2)}, u32[]{:S(2)}) collective-permute-start(bf16[128,2304]{1,0:T(8,128)(2,1)} %get-tuple-element.402), channel_id=1, source_target_pairs={{0,96},{32,64},{64,32},{96,0},{1,97},{33,65},{65,33},{97,1},{2,98}... | collective-permute-start | bytes 1769480 | tf_op jit(solution)/shard_map/ppermute | solution.py:289
  217.5 21.0 %all-to-all-start.4 = ((bf16[16,272,128]{2,1,0:T(8,128)(2,1)}), bf16[16,272,128]{2,1,0:T(8,128)(2,1)S(1)}, u32[]{:S(2)}, u32[]{:S(2)}) async-start(bf16[16,272,128]{2,1,0:T(8,128)(2,1)} %get-tuple-element.392), calls=%async_computation.4 | async-start | bytes 2228224 | tf_op jit(solution)/shard_map/all_to_all | solution.py:285
  232.3 15.4 %collective-permute-start.48 = (bf16[128,2304]{1,0:T(8,128)(2,1)}, bf16[128,2304]{1,0:T(8,128)(2,1)S(1)}, u32[]{:S(2)}, u32[]{:S(2)}) collective-permute-start(bf16[128,2304]{1,0:T(8,128)(2,1)} %get-tuple-element.405), channel_id=1, source_target_pairs={{0,64},{32,96},{64,0},{96,32},{1,65},{33,97},{65,1},{97,33},{2,66}... | collective-permute-start | bytes 1769480 | tf_op jit(solution)/shard_map/ppermute | solution.py:289
  252.9 30.9 %collective-permute-start.55 = (bf16[4,128,2304]{2,1,0:T(8,128)(2,1)}, bf16[4,128,2304]{2,1,0:T(8,128)(2,1)}, u32[]{:S(2)}, u32[]{:S(2)}) collective-permute-start(bf16[4,128,2304]{2,1,0:T(8,128)(2,1)} %get-tuple-element.433.refs_5_.refs_7_), channel_id=1, source_target_pairs={{0,1},{1,0},{2,3},{3,2},{4,5},{5,4},{6,7},{7,6},{8,9},{9,8},{10,11... | collective-permute-start | bytes 7077896 | tf_op jit(solution)/shard_map/ppermute | solution.py:307
  256.8 17.7 %all-to-all-start.5 = ((bf16[16,88,256]{2,1,0:T(8,128)(2,1)}), bf16[16,88,256]{2,1,0:T(8,128)(2,1)S(1)}, u32[]{:S(2)}, u32[]{:S(2)}) async-start(bf16[16,88,256]{2,1,0:T(8,128)(2,1)} %get-tuple-element.421), calls=%async_computation.5 | async-start | bytes 1441792 | tf_op jit(solution)/shard_map/all_to_all | solution.py:285
  289.0 24.2 %collective-permute-start.56 = (bf16[4,64,4096]{2,1,0:T(8,128)(2,1)}, bf16[4,64,4096]{2,1,0:T(8,128)(2,1)S(1)}, u32[]{:S(2)}, u32[]{:S(2)}) collective-permute-start(bf16[4,64,4096]{2,1,0:T(8,128)(2,1)} %get-tuple-element.441.refs_4_), channel_id=1, source_target_pairs={{0,1},{1,0},{2,3},{3,2},{4,5},{5,4},{6,7},{7,6},{8,9},{9,8},{10,11... | collective-permute-start | bytes 6291464 | tf_op jit(solution)/shard_map/ppermute | solution.py:307
  338.2 16.3 %collective-permute-start.63 = (bf16[88,256]{1,0:T(8,128)(2,1)S(1)}, bf16[88,256]{1,0:T(8,128)(2,1)S(1)}, u32[]{:S(2)}, u32[]{:S(2)}) collective-permute-start(bf16[88,256]{1,0:T(8,128)(2,1)S(1)} %get-tuple-element.456), channel_id=1, source_target_pairs={{0,96},{1,32},{2,0},{3,64},{4,97},{5,33},{6,1},{7,65},{8,98},{9,34... | collective-permute-start | bytes 135176 | tf_op jit(solution)/shard_map/ppermute | solution.py:395
  (67 other events, 632.9 us)

commit v5 on v4

--- a/solution.py
+++ b/solution.py
@@ -62,7 +62,7 @@
         ],
         out_specs=[pl.BlockSpec((64, SLAB), lambda s: (s, 0))] * 4,
         out_shape=[pltpu.HBM((128, SLAB), bf16)] * 4,
-        compiler_params=PARAMS,
+        compiler_params=PARAMS if layer else pltpu.CompilerParams(vmem_limit_bytes=62 * 1024 * 1024),
         cost_estimate=cost(0, 4_700_000),
         name="slab_in",
     )(scalars, q, k, v)
@@ -147,9 +147,9 @@
         lead_ref[8 : 8 + SEQ] = kv[:, :128]
         lead_ref[8 + SEQ :] = kv[:, 128:]
 
-    q = dot(xg_ref[:, :512], own[...].reshape(512, 512))
-    q += dot(xg_ref[:, 512:], other[...].reshape(512, 512))
-    for h in range(4):
+    q = dot(xg_ref[:, :512], own[...].reshape(512, 1024))
+    q += dot(xg_ref[:, 512:], other[...].reshape(512, 1024))
+    for h in range(8):
         out_ref[h] = jnp.concatenate(
             [lead_ref[...], q[:, HEAD * h : HEAD * h + HEAD]], axis=0
         ).astype(bf16)
@@ -157,17 +157,17 @@
 
 def project(layer, scalars, xs, gains, weights, pieces):
     specs = [SMEM] + [whole(SEQ, COLS)] * 4 + [whole(4, 4, COLS)]
-    specs += [pl.BlockSpec((4, 128, 512), lambda s: (0, 0, s))] * 2
+    specs += [pl.BlockSpec((4, 128, 1024), lambda s: (0, 0, s))] * 2
     specs += [pl.BlockSpec((4, 128, 256), lambda s: (0, 0, 8))] * 2
     outs = [pltpu.HBM((16, ROWS, 128), bf16)]
-    out_specs = [pl.BlockSpec((4, ROWS, 128), lambda s: (s, 0, 0))]
+    out_specs = [pl.BlockSpec((8, ROWS, 128), lambda s: (s, 0, 0))]
     if pieces:
-        specs += [pl.BlockSpec((64, 1024), lambda s: (0, s))] * 4
+        specs += [pl.BlockSpec((64, 2048), lambda s: (0, s))] * 4
         outs.append(pltpu.HBM((4, 64, OCOLS), bf16))
-        out_specs.append(pl.BlockSpec((4, 64, 1024), lambda s: (0, 0, s)))
+        out_specs.append(pl.BlockSpec((4, 64, 2048), lambda s: (0, 0, s)))
     return pl.pallas_call(
         functools.partial(project_kernel, layer),
-        grid=(4,),
+        grid=(2,),
         in_specs=specs,
         out_specs=out_specs,
         out_shape=outs,
@@ -237,23 +237,23 @@
             scalars[2] == 1, jnp.concatenate(high + low, axis=1), jnp.concatenate(low + high, axis=1)
         ).astype(bf16)
 
-    o = dot(mixed_ref[:, :256], own[...].reshape(256, 1024))
-    o += dot(mixed_ref[:, 256:], other[...].reshape(256, 1024))
-    for i in range(4):
+    o = dot(mixed_ref[:, :256], own[...].reshape(256, 2048))
+    o += dot(mixed_ref[:, 256:], other[...].reshape(256, 2048))
+    for i in range(8):
         out_ref[i] = o[:, COLS * i : COLS * i + COLS].astype(bf16)
 
 
 def output(scalars, mixed, weights, pieces):
-    specs = [SMEM] + [whole(SEQ, HEAD)] * 4 + [pl.BlockSpec((4, 64, 1024), lambda s: (0, 0, s))] * 2
+    specs = [SMEM] + [whole(SEQ, HEAD)] * 4 + [pl.BlockSpec((4, 64, 2048), lambda s: (0, 0, s))] * 2
     outs = [pltpu.HBM((16, SEQ, COLS), bf16)]
-    out_specs = [pl.BlockSpec((4, SEQ, COLS), lambda s: (s, 0, 0))]
+    out_specs = [pl.BlockSpec((8, SEQ, COLS), lambda s: (s, 0, 0))]
     if pieces:
-        specs += [pl.BlockSpec((32, SLAB), lambda s: (s, 0))] * 4
+        specs += [pl.BlockSpec((64, SLAB), lambda s: (s, 0))] * 4
         outs.append(pltpu.HBM((4, 128, SLAB), bf16))
-        out_specs.append(pl.BlockSpec((4, 32, SLAB), lambda s: (0, s, 0)))
+        out_specs.append(pl.BlockSpec((4, 64, SLAB), lambda s: (0, s, 0)))
     return pl.pallas_call(
         output_kernel,
-        grid=(4,),
+        grid=(2,),
         in_specs=specs,
         out_specs=out_specs,
         out_shape=outs,

time: 366 us -> 356 us (0.973)
  Pallas kernels: 71.4 us -> 62.7 us
    pallas_call x8, Pallas kernels: 41.4 us -> 32.6 us  [the longest x4 16.6 us: project(): pl.pallas_call(functools.partial(project_kernel, layer), grid=(2,), in_sp...]
where the time goes in v5:
time: 356 us; the launch traced here: 355 us
  starting transfers between devices  142 us (40%)
  waiting for transfers between devices  123 us (35%)
  Pallas kernels  62.7 us (18%)
  blocking collectives  22.2 us (6%)
    ppermute x48, waiting for transfers between devices, across_line(): return lax.ppermute(value, axis, [(i, i ^ by) for i in range(4)])  91.4 us
    ppermute x48, starting transfers between devices, across_line(): return lax.ppermute(value, axis, [(i, i ^ by) for i in range(4)])  51.8 us
    all_to_all x7, starting transfers between devices, exchange(): return lax.all_to_all(value, axes, 0, 0, tiled=True)  45.9 us
    ppermute x8, starting transfers between devices, body(): rounds.append(lax.ppermute(piece, ALL, pairs))  28.5 us
    all_to_all x1, blocking collectives, exchange(): return lax.all_to_all(value, axes, 0, 0, tiled=True)  22.2 us
    all_to_all x7, waiting for transfers between devices, exchange(): return lax.all_to_all(value, axes, 0, 0, tiled=True)  21.4 us
    pallas_call x4, Pallas kernels, project(): pl.pallas_call(functools.partial(project_kernel, layer), grid=(2,), in_sp...  16.6 us
    ppermute x8, starting transfers between devices, swapped(): return (joined, lax.ppermute(joined, 'c', [(0, 1), (1, 0)]))  16.3 us
  transfers between devices with their start and end apart: 71, of which 42 were waited for; matrix products, arithmetic and copies ran while one was open for 0% of the time, Pallas kernels for 7%

profile of v5, /device:TPU:5, one launch (start us, length us, event | category | flops | bytes accessed | tf_op | source)
XLA Modules:
  0.0 355.1 jit_solution(9407706446947541584)
XLA Ops:
  7.5 4.8 %collective-permute-start = (bf16[96,256]{1,0:T(8,128)(2,1)S(1)}, bf16[96,256]{1,0:T(8,128)(2,1)S(1)}, u32[]{:S(2)}, u32[]{:S(2)}) collective-permute-start(bf16[96,256]{1,0:T(8,128)(2,1)S(1)} %pad_maximum_fusion.3), channel_id=1, source_target_pairs={{0,0},{1,4},{2,8},{3,12},{4,16},{5,20},{6,24},{7,28},{8,2},{9,6},{... | collective-permute-start | bytes 147464 | tf_op jit(solution)/shard_map/ppermute | solution.py:328
  29.4 8.1 %collective-permute-done.7.refs_1_ = bf16[64,4096]{1,0:T(8,128)(2,1)S(1)} collective-permute-done((bf16[64,4096]{1,0:T(8,128)(2,1)}, bf16[64,4096]{1,0:T(8,128)(2,1)S(1)}, u32[]{:S(2)}, u32[]{:S(2)}) %collective-permute-start.7) | collective-permute-done | bytes 524320 | tf_op jit(solution)/shard_map/ppermute | solution.py:289
  64.5 6.2 %all-to-all-start = ((bf16[16,272,128]{2,1,0:T(8,128)(2,1)}), bf16[16,272,128]{2,1,0:T(8,128)(2,1)S(1)}, u32[]{:S(2)}, u32[]{:S(2)}) async-start(bf16[16,272,128]{2,1,0:T(8,128)(2,1)} %project.4), calls=%async_computation | async-start | bytes 2228224 | tf_op jit(solution)/shard_map/all_to_all | solution.py:285
  70.7 7.3 %collective-permute-done.18.refs_7_ = bf16[128,2304]{1,0:T(8,128)(2,1)S(1)} collective-permute-done((bf16[128,2304]{1,0:T(8,128)(2,1)}, bf16[128,2304]{1,0:T(8,128)(2,1)S(1)}, u32[]{:S(2)}, u32[]{:S(2)}) %collective-permute-start.18) | collective-permute-done | bytes 589856 | tf_op jit(solution)/shard_map/ppermute | solution.py:289
  90.7 4.5 %collective-permute-done.20.refs_8_ = bf16[128,2304]{1,0:T(8,128)(2,1)} collective-permute-done((bf16[128,2304]{1,0:T(8,128)(2,1)}, bf16[128,2304]{1,0:T(8,128)(2,1)}, u32[]{:S(2)}, u32[]{:S(2)}) %collective-permute-start.20) | collective-permute-done | bytes 589856 | tf_op jit(solution)/shard_map/ppermute | solution.py:289
  102.2 7.4 %all-to-all-start.1 = ((bf16[16,88,256]{2,1,0:T(8,128)(2,1)}), bf16[16,88,256]{2,1,0:T(8,128)(2,1)S(1)}, u32[]{:S(2)}, u32[]{:S(2)}) async-start(bf16[16,88,256]{2,1,0:T(8,128)(2,1)} %get-tuple-element.305), calls=%async_computation.1 | async-start | bytes 1441792 | tf_op jit(solution)/shard_map/all_to_all | solution.py:285
  109.6 5.7 %collective-permute-done.24.refs_10_ = bf16[64,4096]{1,0:T(8,128)(2,1)S(1)} collective-permute-done((bf16[64,4096]{1,0:T(8,128)(2,1)}, bf16[64,4096]{1,0:T(8,128)(2,1)S(1)}, u32[]{:S(2)}, u32[]{:S(2)}) %collective-permute-start.24) | collective-permute-done | bytes 524320 | tf_op jit(solution)/shard_map/ppermute | solution.py:289
  116.9 4.4 %all-to-all-done.1.recv_ref = bf16[16,88,256]{2,1,0:T(8,128)(2,1)S(1)} async-done(((bf16[16,88,256]{2,1,0:T(8,128)(2,1)}), bf16[16,88,256]{2,1,0:T(8,128)(2,1)S(1)}, u32[]{:S(2)}, u32[]{:S(2)}) %all-to-all-start.1) | async-done | bytes 720928 | tf_op jit(solution)/shard_map/all_to_all | solution.py:285
  130.7 4.3 %project.5 = (bf16[16,272,128]{2,1,0:T(8,128)(2,1)}, bf16[4,64,4096]{2,1,0:T(8,128)(2,1)}) custom-call(s32[3]{0:T(128)S(1)} %copy-done.10, bf16[88,256]{1,0:T(8,128)(2,1)S(1)} %close.4.refs_0_.x_ref, bf16[88,256]{1,0:T(8,128)(2,1)S(1)} %collective-permute-done.21.refs_1_, bf16[88,256]{1,0:T(8,128)(2,1)S(1)} %collective-permute-done.22.refs_2_, ...), custom_call_target="tpu_custom_call" | custom-call | flops 415236096 | bytes 10000000 | tf_op jit(solution)/shard_map/project/pallas_call | solution.py:168
  138.0 7.3 %all-to-all-start.2 = ((bf16[16,272,128]{2,1,0:T(8,128)(2,1)}), bf16[16,272,128]{2,1,0:T(8,128)(2,1)S(1)}, u32[]{:S(2)}, u32[]{:S(2)}) async-start(bf16[16,272,128]{2,1,0:T(8,128)(2,1)} %get-tuple-element.332), calls=%async_computation.2 | async-start | bytes 2228224 | tf_op jit(solution)/shard_map/all_to_all | solution.py:285
  145.3 6.7 %collective-permute-done.32.refs_7_ = bf16[128,2304]{1,0:T(8,128)(2,1)S(1)} collective-permute-done((bf16[128,2304]{1,0:T(8,128)(2,1)}, bf16[128,2304]{1,0:T(8,128)(2,1)S(1)}, u32[]{:S(2)}, u32[]{:S(2)}) %collective-permute-start.32) | collective-permute-done | bytes 589856 | tf_op jit(solution)/shard_map/ppermute | solution.py:289
  164.1 4.6 %collective-permute-done.34.refs_8_ = bf16[128,2304]{1,0:T(8,128)(2,1)} collective-permute-done((bf16[128,2304]{1,0:T(8,128)(2,1)}, bf16[128,2304]{1,0:T(8,128)(2,1)}, u32[]{:S(2)}, u32[]{:S(2)}) %collective-permute-start.34) | collective-permute-done | bytes 589856 | tf_op jit(solution)/shard_map/ppermute | solution.py:289
  176.7 6.5 %all-to-all-start.3 = ((bf16[16,88,256]{2,1,0:T(8,128)(2,1)}), bf16[16,88,256]{2,1,0:T(8,128)(2,1)S(1)}, u32[]{:S(2)}, u32[]{:S(2)}) async-start(bf16[16,88,256]{2,1,0:T(8,128)(2,1)} %get-tuple-element.365), calls=%async_computation.3 | async-start | bytes 1441792 | tf_op jit(solution)/shard_map/all_to_all | solution.py:285
  183.2 5.6 %collective-permute-done.38.refs_10_ = bf16[64,4096]{1,0:T(8,128)(2,1)S(1)} collective-permute-done((bf16[64,4096]{1,0:T(8,128)(2,1)}, bf16[64,4096]{1,0:T(8,128)(2,1)S(1)}, u32[]{:S(2)}, u32[]{:S(2)}) %collective-permute-start.38) | collective-permute-done | bytes 524320 | tf_op jit(solution)/shard_map/ppermute | solution.py:289
  211.6 6.8 %all-to-all-start.4 = ((bf16[16,272,128]{2,1,0:T(8,128)(2,1)}), bf16[16,272,128]{2,1,0:T(8,128)(2,1)S(1)}, u32[]{:S(2)}, u32[]{:S(2)}) async-start(bf16[16,272,128]{2,1,0:T(8,128)(2,1)} %get-tuple-element.392), calls=%async_computation.4 | async-start | bytes 2228224 | tf_op jit(solution)/shard_map/all_to_all | solution.py:285
  218.4 6.8 %collective-permute-done.46.refs_7_ = bf16[128,2304]{1,0:T(8,128)(2,1)S(1)} collective-permute-done((bf16[128,2304]{1,0:T(8,128)(2,1)}, bf16[128,2304]{1,0:T(8,128)(2,1)S(1)}, u32[]{:S(2)}, u32[]{:S(2)}) %collective-permute-start.46) | collective-permute-done | bytes 589856 | tf_op jit(solution)/shard_map/ppermute | solution.py:289
  249.8 6.3 %all-to-all-start.5 = ((bf16[16,88,256]{2,1,0:T(8,128)(2,1)}), bf16[16,88,256]{2,1,0:T(8,128)(2,1)S(1)}, u32[]{:S(2)}, u32[]{:S(2)}) async-start(bf16[16,88,256]{2,1,0:T(8,128)(2,1)} %get-tuple-element.421), calls=%async_computation.5 | async-start | bytes 1441792 | tf_op jit(solution)/shard_map/all_to_all | solution.py:285
  256.1 5.6 %collective-permute-done.52.refs_10_ = bf16[64,4096]{1,0:T(8,128)(2,1)S(1)} collective-permute-done((bf16[64,4096]{1,0:T(8,128)(2,1)}, bf16[64,4096]{1,0:T(8,128)(2,1)S(1)}, u32[]{:S(2)}, u32[]{:S(2)}) %collective-permute-start.52) | collective-permute-done | bytes 524320 | tf_op jit(solution)/shard_map/ppermute | solution.py:289
  283.0 22.2 %all_to_all.40.recv_ref = bf16[16,272,128]{2,1,0:T(8,128)(2,1)S(1)} all-to-all(bf16[16,272,128]{2,1,0:T(8,128)(2,1)} %get-tuple-element.438), channel_id=1, replica_groups=mesh['z'=4,'x'=4,'y'=4,'c'=2] {'x','y'}, dimensions={0} | all-to-all | bytes 2228224 | tf_op jit(solution)/shard_map/all_to_all | solution.py:285
  315.4 5.5 %all-to-all-start.7 = ((bf16[16,88,256]{2,1,0:T(8,128)(2,1)}), bf16[16,88,256]{2,1,0:T(8,128)(2,1)S(1)}, u32[]{:S(2)}, u32[]{:S(2)}) async-start(bf16[16,88,256]{2,1,0:T(8,128)(2,1)} %output.7), calls=%async_computation.7 | async-start | bytes 1441792 | tf_op jit(solution)/shard_map/all_to_all | solution.py:285
  320.9 7.7 %all-to-all-done.7.recv_ref = bf16[16,88,256]{2,1,0:T(8,128)(2,1)S(1)} async-done(((bf16[16,88,256]{2,1,0:T(8,128)(2,1)}), bf16[16,88,256]{2,1,0:T(8,128)(2,1)S(1)}, u32[]{:S(2)}, u32[]{:S(2)}) %all-to-all-start.7) | async-done | bytes 720928 | tf_op jit(solution)/shard_map/all_to_all | solution.py:285
  328.8 6.3 %collective-permute-start.63 = (bf16[88,256]{1,0:T(8,128)(2,1)S(1)}, bf16[88,256]{1,0:T(8,128)(2,1)S(1)}, u32[]{:S(2)}, u32[]{:S(2)}) collective-permute-start(bf16[88,256]{1,0:T(8,128)(2,1)S(1)} %get-tuple-element.456), channel_id=1, source_target_pairs={{0,96},{1,32},{2,0},{3,64},{4,97},{5,33},{6,1},{7,65},{8,98},{9,34... | collective-permute-start | bytes 135176 | tf_op jit(solution)/shard_map/ppermute | solution.py:395
  336.0 6.6 %collective-permute-start.61 = (bf16[88,256]{1,0:T(8,128)(2,1)S(1)}, bf16[88,256]{1,0:T(8,128)(2,1)S(1)}, u32[]{:S(2)}, u32[]{:S(2)}) collective-permute-start(bf16[88,256]{1,0:T(8,128)(2,1)S(1)} %get-tuple-element.458), channel_id=1, source_target_pairs={{0,32},{1,96},{2,64},{3,0},{4,33},{5,97},{6,65},{7,1},{8,34},{9,98... | collective-permute-start | bytes 135176 | tf_op jit(solution)/shard_map/ppermute | solution.py:395
  346.3 8.0 %collective-permute-done.60 = bf16[88,256]{1,0:T(8,128)(2,1)S(1)} collective-permute-done((bf16[88,256]{1,0:T(8,128)(2,1)S(1)}, bf16[88,256]{1,0:T(8,128)(2,1)S(1)}, u32[]{:S(2)}, u32[]{:S(2)}) %collective-permute-start.60) | collective-permute-done | bytes 45088 | tf_op jit(solution)/shard_map/ppermute | solution.py:395
  (206 shorter events, 189.6 us)
Async XLA Ops:
  3.5 20.4 %collective-permute-start.4 = (bf16[128,2304]{1,0:T(8,128)(2,1)}, bf16[128,2304]{1,0:T(8,128)(2,1)S(1)}, u32[]{:S(2)}, u32[]{:S(2)}) collective-permute-start(bf16[128,2304]{1,0:T(8,128)(2,1)} %get-tuple-element.225), channel_id=1, source_target_pairs={{0,32},{32,0},{64,96},{96,64},{1,33},{33,1},{65,97},{97,65},{2,34}... | collective-permute-start | bytes 1769480 | tf_op jit(solution)/shard_map/ppermute | solution.py:289
  5.1 18.8 %collective-permute-start.5 = (bf16[128,2304]{1,0:T(8,128)(2,1)}, bf16[128,2304]{1,0:T(8,128)(2,1)S(1)}, u32[]{:S(2)}, u32[]{:S(2)}) collective-permute-start(bf16[128,2304]{1,0:T(8,128)(2,1)} %get-tuple-element.226), channel_id=1, source_target_pairs={{0,96},{32,64},{64,32},{96,0},{1,97},{33,65},{65,33},{97,1},{2,98}... | collective-permute-start | bytes 1769480 | tf_op jit(solution)/shard_map/ppermute | solution.py:289
  62.1 24.0 %collective-permute-start.14 = (bf16[4,64,4096]{2,1,0:T(8,128)(2,1)}, bf16[4,64,4096]{2,1,0:T(8,128)(2,1)}, u32[]{:S(2)}, u32[]{:S(2)}) collective-permute-start(bf16[4,64,4096]{2,1,0:T(8,128)(2,1)} %join.3.refs_4_), channel_id=1, source_target_pairs={{0,1},{1,0},{2,3},{3,2},{4,5},{5,4},{6,7},{7,6},{8,9},{9,8},{10,11... | collective-permute-start | bytes 6291464 | tf_op jit(solution)/shard_map/ppermute | solution.py:307
  62.8 15.2 %collective-permute-start.18 = (bf16[128,2304]{1,0:T(8,128)(2,1)}, bf16[128,2304]{1,0:T(8,128)(2,1)S(1)}, u32[]{:S(2)}, u32[]{:S(2)}) collective-permute-start(bf16[128,2304]{1,0:T(8,128)(2,1)} %get-tuple-element.285), channel_id=1, source_target_pairs={{0,32},{32,0},{64,96},{96,64},{1,33},{33,1},{65,97},{97,65},{2,34}... | collective-permute-start | bytes 1769480 | tf_op jit(solution)/shard_map/ppermute | solution.py:289
  63.6 16.1 %collective-permute-start.19 = (bf16[128,2304]{1,0:T(8,128)(2,1)}, bf16[128,2304]{1,0:T(8,128)(2,1)S(1)}, u32[]{:S(2)}, u32[]{:S(2)}) collective-permute-start(bf16[128,2304]{1,0:T(8,128)(2,1)} %get-tuple-element.286), channel_id=1, source_target_pairs={{0,96},{32,64},{64,32},{96,0},{1,97},{33,65},{65,33},{97,1},{2,98}... | collective-permute-start | bytes 1769480 | tf_op jit(solution)/shard_map/ppermute | solution.py:289
  64.5 21.5 %all-to-all-start = ((bf16[16,272,128]{2,1,0:T(8,128)(2,1)}), bf16[16,272,128]{2,1,0:T(8,128)(2,1)S(1)}, u32[]{:S(2)}, u32[]{:S(2)}) async-start(bf16[16,272,128]{2,1,0:T(8,128)(2,1)} %project.4), calls=%async_computation | async-start | bytes 2228224 | tf_op jit(solution)/shard_map/all_to_all | solution.py:285
  79.6 15.5 %collective-permute-start.20 = (bf16[128,2304]{1,0:T(8,128)(2,1)}, bf16[128,2304]{1,0:T(8,128)(2,1)}, u32[]{:S(2)}, u32[]{:S(2)}) collective-permute-start(bf16[128,2304]{1,0:T(8,128)(2,1)} %get-tuple-element.289), channel_id=1, source_target_pairs={{0,64},{32,96},{64,0},{96,32},{1,65},{33,97},{65,1},{97,33},{2,66}... | collective-permute-start | bytes 1769480 | tf_op jit(solution)/shard_map/ppermute | solution.py:289
  99.5 31.2 %collective-permute-start.27 = (bf16[4,128,2304]{2,1,0:T(8,128)(2,1)}, bf16[4,128,2304]{2,1,0:T(8,128)(2,1)}, u32[]{:S(2)}, u32[]{:S(2)}) collective-permute-start(bf16[4,128,2304]{2,1,0:T(8,128)(2,1)} %get-tuple-element.325.refs_5_.refs_7_), channel_id=1, source_target_pairs={{0,1},{1,0},{2,3},{3,2},{4,5},{5,4},{6,7},{7,6},{8,9},{9,8},{10,11... | collective-permute-start | bytes 7077896 | tf_op jit(solution)/shard_map/ppermute | solution.py:307
  102.2 19.0 %all-to-all-start.1 = ((bf16[16,88,256]{2,1,0:T(8,128)(2,1)}), bf16[16,88,256]{2,1,0:T(8,128)(2,1)S(1)}, u32[]{:S(2)}, u32[]{:S(2)}) async-start(bf16[16,88,256]{2,1,0:T(8,128)(2,1)} %get-tuple-element.305), calls=%async_computation.1 | async-start | bytes 1441792 | tf_op jit(solution)/shard_map/all_to_all | solution.py:285
  135.0 24.5 %collective-permute-start.28 = (bf16[4,64,4096]{2,1,0:T(8,128)(2,1)}, bf16[4,64,4096]{2,1,0:T(8,128)(2,1)}, u32[]{:S(2)}, u32[]{:S(2)}) collective-permute-start(bf16[4,64,4096]{2,1,0:T(8,128)(2,1)} %get-tuple-element.359.refs_4_), channel_id=1, source_target_pairs={{0,1},{1,0},{2,3},{3,2},{4,5},{5,4},{6,7},{7,6},{8,9},{9,8},{10,11... | collective-permute-start | bytes 6291464 | tf_op jit(solution)/shard_map/ppermute | solution.py:307
  136.9 16.2 %collective-permute-start.33 = (bf16[128,2304]{1,0:T(8,128)(2,1)}, bf16[128,2304]{1,0:T(8,128)(2,1)S(1)}, u32[]{:S(2)}, u32[]{:S(2)}) collective-permute-start(bf16[128,2304]{1,0:T(8,128)(2,1)} %get-tuple-element.346), channel_id=1, source_target_pairs={{0,96},{32,64},{64,32},{96,0},{1,97},{33,65},{65,33},{97,1},{2,98}... | collective-permute-start | bytes 1769480 | tf_op jit(solution)/shard_map/ppermute | solution.py:289
  138.0 21.5 %all-to-all-start.2 = ((bf16[16,272,128]{2,1,0:T(8,128)(2,1)}), bf16[16,272,128]{2,1,0:T(8,128)(2,1)S(1)}, u32[]{:S(2)}, u32[]{:S(2)}) async-start(bf16[16,272,128]{2,1,0:T(8,128)(2,1)} %get-tuple-element.332), calls=%async_computation.2 | async-start | bytes 2228224 | tf_op jit(solution)/shard_map/all_to_all | solution.py:285
  153.1 15.7 %collective-permute-start.34 = (bf16[128,2304]{1,0:T(8,128)(2,1)}, bf16[128,2304]{1,0:T(8,128)(2,1)}, u32[]{:S(2)}, u32[]{:S(2)}) collective-permute-start(bf16[128,2304]{1,0:T(8,128)(2,1)} %get-tuple-element.349), channel_id=1, source_target_pairs={{0,64},{32,96},{64,0},{96,32},{1,65},{33,97},{65,1},{97,33},{2,66}... | collective-permute-start | bytes 1769480 | tf_op jit(solution)/shard_map/ppermute | solution.py:289
  173.0 30.6 %collective-permute-start.41 = (bf16[4,128,2304]{2,1,0:T(8,128)(2,1)}, bf16[4,128,2304]{2,1,0:T(8,128)(2,1)}, u32[]{:S(2)}, u32[]{:S(2)}) collective-permute-start(bf16[4,128,2304]{2,1,0:T(8,128)(2,1)} %get-tuple-element.385.refs_5_.refs_7_), channel_id=1, source_target_pairs={{0,1},{1,0},{2,3},{3,2},{4,5},{5,4},{6,7},{7,6},{8,9},{9,8},{10,11... | collective-permute-start | bytes 7077896 | tf_op jit(solution)/shard_map/ppermute | solution.py:307
  176.7 17.9 %all-to-all-start.3 = ((bf16[16,88,256]{2,1,0:T(8,128)(2,1)}), bf16[16,88,256]{2,1,0:T(8,128)(2,1)S(1)}, u32[]{:S(2)}, u32[]{:S(2)}) async-start(bf16[16,88,256]{2,1,0:T(8,128)(2,1)} %get-tuple-element.365), calls=%async_computation.3 | async-start | bytes 1441792 | tf_op jit(solution)/shard_map/all_to_all | solution.py:285
  207.9 24.8 %collective-permute-start.42 = (bf16[4,64,4096]{2,1,0:T(8,128)(2,1)}, bf16[4,64,4096]{2,1,0:T(8,128)(2,1)}, u32[]{:S(2)}, u32[]{:S(2)}) collective-permute-start(bf16[4,64,4096]{2,1,0:T(8,128)(2,1)} %get-tuple-element.415.refs_4_), channel_id=1, source_target_pairs={{0,1},{1,0},{2,3},{3,2},{4,5},{5,4},{6,7},{7,6},{8,9},{9,8},{10,11... | collective-permute-start | bytes 6291464 | tf_op jit(solution)/shard_map/ppermute | solution.py:307
  210.0 15.2 %collective-permute-start.46 = (bf16[128,2304]{1,0:T(8,128)(2,1)}, bf16[128,2304]{1,0:T(8,128)(2,1)S(1)}, u32[]{:S(2)}, u32[]{:S(2)}) collective-permute-start(bf16[128,2304]{1,0:T(8,128)(2,1)} %get-tuple-element.401), channel_id=1, source_target_pairs={{0,32},{32,0},{64,96},{96,64},{1,33},{33,1},{65,97},{97,65},{2,34}... | collective-permute-start | bytes 1769480 | tf_op jit(solution)/shard_map/ppermute | solution.py:289
  210.1 16.1 %collective-permute-start.47 = (bf16[128,2304]{1,0:T(8,128)(2,1)}, bf16[128,2304]{1,0:T(8,128)(2,1)}, u32[]{:S(2)}, u32[]{:S(2)}) collective-permute-start(bf16[128,2304]{1,0:T(8,128)(2,1)} %get-tuple-element.402), channel_id=1, source_target_pairs={{0,96},{32,64},{64,32},{96,0},{1,97},{33,65},{65,33},{97,1},{2,98}... | collective-permute-start | bytes 1769480 | tf_op jit(solution)/shard_map/ppermute | solution.py:289
  211.6 21.0 %all-to-all-start.4 = ((bf16[16,272,128]{2,1,0:T(8,128)(2,1)}), bf16[16,272,128]{2,1,0:T(8,128)(2,1)S(1)}, u32[]{:S(2)}, u32[]{:S(2)}) async-start(bf16[16,272,128]{2,1,0:T(8,128)(2,1)} %get-tuple-element.392), calls=%async_computation.4 | async-start | bytes 2228224 | tf_op jit(solution)/shard_map/all_to_all | solution.py:285
  226.1 15.4 %collective-permute-start.48 = (bf16[128,2304]{1,0:T(8,128)(2,1)}, bf16[128,2304]{1,0:T(8,128)(2,1)S(1)}, u32[]{:S(2)}, u32[]{:S(2)}) collective-permute-start(bf16[128,2304]{1,0:T(8,128)(2,1)} %get-tuple-element.405), channel_id=1, source_target_pairs={{0,64},{32,96},{64,0},{96,32},{1,65},{33,97},{65,1},{97,33},{2,66}... | collective-permute-start | bytes 1769480 | tf_op jit(solution)/shard_map/ppermute | solution.py:289
  245.6 31.0 %collective-permute-start.55 = (bf16[4,128,2304]{2,1,0:T(8,128)(2,1)}, bf16[4,128,2304]{2,1,0:T(8,128)(2,1)}, u32[]{:S(2)}, u32[]{:S(2)}) collective-permute-start(bf16[4,128,2304]{2,1,0:T(8,128)(2,1)} %get-tuple-element.433.refs_5_.refs_7_), channel_id=1, source_target_pairs={{0,1},{1,0},{2,3},{3,2},{4,5},{5,4},{6,7},{7,6},{8,9},{9,8},{10,11... | collective-permute-start | bytes 7077896 | tf_op jit(solution)/shard_map/ppermute | solution.py:307
  249.8 17.7 %all-to-all-start.5 = ((bf16[16,88,256]{2,1,0:T(8,128)(2,1)}), bf16[16,88,256]{2,1,0:T(8,128)(2,1)S(1)}, u32[]{:S(2)}, u32[]{:S(2)}) async-start(bf16[16,88,256]{2,1,0:T(8,128)(2,1)} %get-tuple-element.421), calls=%async_computation.5 | async-start | bytes 1441792 | tf_op jit(solution)/shard_map/all_to_all | solution.py:285
  280.9 24.3 %collective-permute-start.56 = (bf16[4,64,4096]{2,1,0:T(8,128)(2,1)}, bf16[4,64,4096]{2,1,0:T(8,128)(2,1)S(1)}, u32[]{:S(2)}, u32[]{:S(2)}) collective-permute-start(bf16[4,64,4096]{2,1,0:T(8,128)(2,1)} %get-tuple-element.441.refs_4_), channel_id=1, source_target_pairs={{0,1},{1,0},{2,3},{3,2},{4,5},{5,4},{6,7},{7,6},{8,9},{9,8},{10,11... | collective-permute-start | bytes 6291464 | tf_op jit(solution)/shard_map/ppermute | solution.py:307
  328.8 16.3 %collective-permute-start.63 = (bf16[88,256]{1,0:T(8,128)(2,1)S(1)}, bf16[88,256]{1,0:T(8,128)(2,1)S(1)}, u32[]{:S(2)}, u32[]{:S(2)}) collective-permute-start(bf16[88,256]{1,0:T(8,128)(2,1)S(1)} %get-tuple-element.456), channel_id=1, source_target_pairs={{0,96},{1,32},{2,0},{3,64},{4,97},{5,33},{6,1},{7,65},{8,98},{9,34... | collective-permute-start | bytes 135176 | tf_op jit(solution)/shard_map/ppermute | solution.py:395
  (66 other events, 650.0 us)

commit v6 on v5

--- a/solution.py
+++ b/solution.py
@@ -301,6 +301,11 @@
     near = [across_line(slabs[k], axis, k) for k in (1, 3)]
     near, far = after(near, slabs[2])
     return [slabs[0], near[0], across_line(far, axis, 2), near[1]]
+
+
+def relay_far(slabs, axis):
+    far, near = after(across_line(slabs[2], axis, 2), (slabs[1], slabs[3]))
+    return [slabs[0], across_line(near[0], axis, 1), far, across_line(near[1], axis, 3)]
 
 
 def swapped(joined):
@@ -355,7 +360,7 @@
             xs, outs = after(xs, outs)
         if layer < 3:
             xs, slab = after(xs, ahead)
-            ins_next = relay(slab, "z")
+            ins_next = relay_far(slab, "z")
         if layer:
             partial, outs = project(layer, scalars, xs, gains, ins, outs)
         else:

time: 356 us -> 357 us (level)
  transfers between devices with their start and end apart: 71 -> 71, of which waited for: 42 -> 41; matrix products, arithmetic and copies ran while one was open for 0% -> 0% of each run, Pallas kernels for 7% -> 7%
where the time goes in v6:
time: 357 us; the launch traced here: 356 us
  starting transfers between devices  145 us (41%)
  waiting for transfers between devices  122 us (34%)
  Pallas kernels  62.5 us (18%)
  blocking collectives  22.3 us (6%)
    ppermute x48, waiting for transfers between devices, across_line(): return lax.ppermute(value, axis, [(i, i ^ by) for i in range(4)])  89.4 us
    ppermute x48, starting transfers between devices, across_line(): return lax.ppermute(value, axis, [(i, i ^ by) for i in range(4)])  52.5 us
    all_to_all x7, starting transfers between devices, exchange(): return lax.all_to_all(value, axes, 0, 0, tiled=True)  47.8 us
    ppermute x8, starting transfers between devices, body(): rounds.append(lax.ppermute(piece, ALL, pairs))  28.5 us
    all_to_all x7, waiting for transfers between devices, exchange(): return lax.all_to_all(value, axes, 0, 0, tiled=True)  22.5 us
    all_to_all x1, blocking collectives, exchange(): return lax.all_to_all(value, axes, 0, 0, tiled=True)  22.3 us
    pallas_call x4, Pallas kernels, project(): pl.pallas_call(functools.partial(project_kernel, layer), grid=(2,), in_sp...  16.4 us
    pallas_call x4, Pallas kernels, output(): pl.pallas_call(output_kernel, grid=(2,), in_specs=specs, out_specs=out_sp...  16 us
  transfers between devices with their start and end apart: 71, of which 41 were waited for; matrix products, arithmetic and copies ran while one was open for 0% of the time, Pallas kernels for 7%

profile of v6, /device:TPU:5, one launch (start us, length us, event | category | flops | bytes accessed | tf_op | source)
XLA Modules:
  0.0 356.2 jit_solution(801052366270566361)
XLA Ops:
  7.5 4.8 %collective-permute-start = (bf16[96,256]{1,0:T(8,128)(2,1)S(1)}, bf16[96,256]{1,0:T(8,128)(2,1)S(1)}, u32[]{:S(2)}, u32[]{:S(2)}) collective-permute-start(bf16[96,256]{1,0:T(8,128)(2,1)S(1)} %pad_maximum_fusion.3), channel_id=1, source_target_pairs={{0,0},{1,4},{2,8},{3,12},{4,16},{5,20},{6,24},{7,28},{8,2},{9,6},{... | collective-permute-start | bytes 147464 | tf_op jit(solution)/shard_map/ppermute | solution.py:333
  29.4 8.0 %collective-permute-done.7.refs_1_ = bf16[64,4096]{1,0:T(8,128)(2,1)S(1)} collective-permute-done((bf16[64,4096]{1,0:T(8,128)(2,1)}, bf16[64,4096]{1,0:T(8,128)(2,1)S(1)}, u32[]{:S(2)}, u32[]{:S(2)}) %collective-permute-start.7) | collective-permute-done | bytes 524320 | tf_op jit(solution)/shard_map/ppermute | solution.py:289
  64.2 6.2 %all-to-all-start = ((bf16[16,272,128]{2,1,0:T(8,128)(2,1)}), bf16[16,272,128]{2,1,0:T(8,128)(2,1)S(1)}, u32[]{:S(2)}, u32[]{:S(2)}) async-start(bf16[16,272,128]{2,1,0:T(8,128)(2,1)} %project.4), calls=%async_computation | async-start | bytes 2228224 | tf_op jit(solution)/shard_map/all_to_all | solution.py:285
  70.4 8.9 %collective-permute-done.18.refs_8_ = bf16[128,2304]{1,0:T(8,128)(2,1)S(1)} collective-permute-done((bf16[128,2304]{1,0:T(8,128)(2,1)S(1)}, bf16[128,2304]{1,0:T(8,128)(2,1)S(1)}, u32[]{:S(2)}, u32[]{:S(2)}) %collective-permute-start.18) | collective-permute-done | bytes 589856 | tf_op jit(solution)/shard_map/ppermute | solution.py:289
  102.4 7.3 %all-to-all-start.1 = ((bf16[16,88,256]{2,1,0:T(8,128)(2,1)}), bf16[16,88,256]{2,1,0:T(8,128)(2,1)S(1)}, u32[]{:S(2)}, u32[]{:S(2)}) async-start(bf16[16,88,256]{2,1,0:T(8,128)(2,1)} %get-tuple-element.305), calls=%async_computation.1 | async-start | bytes 1441792 | tf_op jit(solution)/shard_map/all_to_all | solution.py:285
  109.7 5.7 %collective-permute-done.24.refs_10_ = bf16[64,4096]{1,0:T(8,128)(2,1)S(1)} collective-permute-done((bf16[64,4096]{1,0:T(8,128)(2,1)}, bf16[64,4096]{1,0:T(8,128)(2,1)S(1)}, u32[]{:S(2)}, u32[]{:S(2)}) %collective-permute-start.24) | collective-permute-done | bytes 524320 | tf_op jit(solution)/shard_map/ppermute | solution.py:289
  117.0 4.3 %all-to-all-done.1.recv_ref = bf16[16,88,256]{2,1,0:T(8,128)(2,1)S(1)} async-done(((bf16[16,88,256]{2,1,0:T(8,128)(2,1)}), bf16[16,88,256]{2,1,0:T(8,128)(2,1)S(1)}, u32[]{:S(2)}, u32[]{:S(2)}) %all-to-all-start.1) | async-done | bytes 720928 | tf_op jit(solution)/shard_map/all_to_all | solution.py:285
  130.7 4.3 %project.5 = (bf16[16,272,128]{2,1,0:T(8,128)(2,1)}, bf16[4,64,4096]{2,1,0:T(8,128)(2,1)}) custom-call(s32[3]{0:T(128)S(1)} %copy-done.10, bf16[88,256]{1,0:T(8,128)(2,1)S(1)} %close.4.refs_0_.x_ref, bf16[88,256]{1,0:T(8,128)(2,1)S(1)} %collective-permute-done.21.refs_1_, bf16[88,256]{1,0:T(8,128)(2,1)S(1)} %collective-permute-done.22.refs_2_, ...), custom_call_target="tpu_custom_call" | custom-call | flops 415236096 | bytes 10000000 | tf_op jit(solution)/shard_map/project/pallas_call | solution.py:168
  137.8 7.1 %all-to-all-start.2 = ((bf16[16,272,128]{2,1,0:T(8,128)(2,1)}), bf16[16,272,128]{2,1,0:T(8,128)(2,1)S(1)}, u32[]{:S(2)}, u32[]{:S(2)}) async-start(bf16[16,272,128]{2,1,0:T(8,128)(2,1)} %get-tuple-element.332), calls=%async_computation.2 | async-start | bytes 2228224 | tf_op jit(solution)/shard_map/all_to_all | solution.py:285
  144.9 8.6 %collective-permute-done.32.refs_8_ = bf16[128,2304]{1,0:T(8,128)(2,1)S(1)} collective-permute-done((bf16[128,2304]{1,0:T(8,128)(2,1)}, bf16[128,2304]{1,0:T(8,128)(2,1)S(1)}, u32[]{:S(2)}, u32[]{:S(2)}) %collective-permute-start.32) | collective-permute-done | bytes 589856 | tf_op jit(solution)/shard_map/ppermute | solution.py:289
  169.0 4.3 %output.5 = (bf16[16,88,256]{2,1,0:T(8,128)(2,1)}, bf16[4,128,2304]{2,1,0:T(8,128)(2,1)}) custom-call(s32[3]{0:T(128)S(1)} %copy-done.10, bf16[88,128]{1,0:T(8,128)(2,1)S(1)} %attend.5.refs_0_, bf16[88,128]{1,0:T(8,128)(2,1)S(1)} %collective-permute-done.29.refs_1_, bf16[88,128]{1,0:T(8,128)(2,1)S(1)} %collective-permute-done.30.refs_2_, ...), custom_call_target="tpu_custom_call" | custom-call | flops 369098752 | bytes 10000000 | tf_op jit(solution)/shard_map/output/pallas_call | solution.py:254
  176.6 7.2 %all-to-all-start.3 = ((bf16[16,88,256]{2,1,0:T(8,128)(2,1)}), bf16[16,88,256]{2,1,0:T(8,128)(2,1)S(1)}, u32[]{:S(2)}, u32[]{:S(2)}) async-start(bf16[16,88,256]{2,1,0:T(8,128)(2,1)} %get-tuple-element.365), calls=%async_computation.3 | async-start | bytes 1441792 | tf_op jit(solution)/shard_map/all_to_all | solution.py:285
  183.9 5.0 %collective-permute-done.38.refs_10_ = bf16[64,4096]{1,0:T(8,128)(2,1)S(1)} collective-permute-done((bf16[64,4096]{1,0:T(8,128)(2,1)}, bf16[64,4096]{1,0:T(8,128)(2,1)S(1)}, u32[]{:S(2)}, u32[]{:S(2)}) %collective-permute-start.38) | collective-permute-done | bytes 524320 | tf_op jit(solution)/shard_map/ppermute | solution.py:289
  191.3 4.3 %all-to-all-done.3.recv_ref = bf16[16,88,256]{2,1,0:T(8,128)(2,1)S(1)} async-done(((bf16[16,88,256]{2,1,0:T(8,128)(2,1)}), bf16[16,88,256]{2,1,0:T(8,128)(2,1)S(1)}, u32[]{:S(2)}, u32[]{:S(2)}) %all-to-all-start.3) | async-done | bytes 720928 | tf_op jit(solution)/shard_map/all_to_all | solution.py:285
  211.5 7.5 %all-to-all-start.4 = ((bf16[16,272,128]{2,1,0:T(8,128)(2,1)}), bf16[16,272,128]{2,1,0:T(8,128)(2,1)S(1)}, u32[]{:S(2)}, u32[]{:S(2)}) async-start(bf16[16,272,128]{2,1,0:T(8,128)(2,1)} %get-tuple-element.392), calls=%async_computation.4 | async-start | bytes 2228224 | tf_op jit(solution)/shard_map/all_to_all | solution.py:285
  219.0 7.6 %collective-permute-done.46.refs_8_ = bf16[128,2304]{1,0:T(8,128)(2,1)S(1)} collective-permute-done((bf16[128,2304]{1,0:T(8,128)(2,1)}, bf16[128,2304]{1,0:T(8,128)(2,1)S(1)}, u32[]{:S(2)}, u32[]{:S(2)}) %collective-permute-start.46) | collective-permute-done | bytes 589856 | tf_op jit(solution)/shard_map/ppermute | solution.py:289
  250.6 6.8 %all-to-all-start.5 = ((bf16[16,88,256]{2,1,0:T(8,128)(2,1)}), bf16[16,88,256]{2,1,0:T(8,128)(2,1)S(1)}, u32[]{:S(2)}, u32[]{:S(2)}) async-start(bf16[16,88,256]{2,1,0:T(8,128)(2,1)} %get-tuple-element.421), calls=%async_computation.5 | async-start | bytes 1441792 | tf_op jit(solution)/shard_map/all_to_all | solution.py:285
  257.4 5.3 %collective-permute-done.52.refs_10_ = bf16[64,4096]{1,0:T(8,128)(2,1)S(1)} collective-permute-done((bf16[64,4096]{1,0:T(8,128)(2,1)}, bf16[64,4096]{1,0:T(8,128)(2,1)S(1)}, u32[]{:S(2)}, u32[]{:S(2)}) %collective-permute-start.52) | collective-permute-done | bytes 524320 | tf_op jit(solution)/shard_map/ppermute | solution.py:289
  283.8 22.3 %all_to_all.40.recv_ref = bf16[16,272,128]{2,1,0:T(8,128)(2,1)S(1)} all-to-all(bf16[16,272,128]{2,1,0:T(8,128)(2,1)} %get-tuple-element.438), channel_id=1, replica_groups=mesh['z'=4,'x'=4,'y'=4,'c'=2] {'x','y'}, dimensions={0} | all-to-all | bytes 2228224 | tf_op jit(solution)/shard_map/all_to_all | solution.py:285
  316.4 5.7 %all-to-all-start.7 = ((bf16[16,88,256]{2,1,0:T(8,128)(2,1)}), bf16[16,88,256]{2,1,0:T(8,128)(2,1)S(1)}, u32[]{:S(2)}, u32[]{:S(2)}) async-start(bf16[16,88,256]{2,1,0:T(8,128)(2,1)} %output.7), calls=%async_computation.7 | async-start | bytes 1441792 | tf_op jit(solution)/shard_map/all_to_all | solution.py:285
  322.0 7.7 %all-to-all-done.7.recv_ref = bf16[16,88,256]{2,1,0:T(8,128)(2,1)S(1)} async-done(((bf16[16,88,256]{2,1,0:T(8,128)(2,1)}), bf16[16,88,256]{2,1,0:T(8,128)(2,1)S(1)}, u32[]{:S(2)}, u32[]{:S(2)}) %all-to-all-start.7) | async-done | bytes 720928 | tf_op jit(solution)/shard_map/all_to_all | solution.py:285
  330.0 6.3 %collective-permute-start.63 = (bf16[88,256]{1,0:T(8,128)(2,1)S(1)}, bf16[88,256]{1,0:T(8,128)(2,1)S(1)}, u32[]{:S(2)}, u32[]{:S(2)}) collective-permute-start(bf16[88,256]{1,0:T(8,128)(2,1)S(1)} %get-tuple-element.456), channel_id=1, source_target_pairs={{0,96},{1,32},{2,0},{3,64},{4,97},{5,33},{6,1},{7,65},{8,98},{9,34... | collective-permute-start | bytes 135176 | tf_op jit(solution)/shard_map/ppermute | solution.py:400
  337.2 6.6 %collective-permute-start.61 = (bf16[88,256]{1,0:T(8,128)(2,1)S(1)}, bf16[88,256]{1,0:T(8,128)(2,1)S(1)}, u32[]{:S(2)}, u32[]{:S(2)}) collective-permute-start(bf16[88,256]{1,0:T(8,128)(2,1)S(1)} %get-tuple-element.458), channel_id=1, source_target_pairs={{0,32},{1,96},{2,64},{3,0},{4,33},{5,97},{6,65},{7,1},{8,34},{9,98... | collective-permute-start | bytes 135176 | tf_op jit(solution)/shard_map/ppermute | solution.py:400
  347.4 8.0 %collective-permute-done.60 = bf16[88,256]{1,0:T(8,128)(2,1)S(1)} collective-permute-done((bf16[88,256]{1,0:T(8,128)(2,1)S(1)}, bf16[88,256]{1,0:T(8,128)(2,1)S(1)}, u32[]{:S(2)}, u32[]{:S(2)}) %collective-permute-start.60) | collective-permute-done | bytes 45088 | tf_op jit(solution)/shard_map/ppermute | solution.py:400
  (204 shorter events, 185.9 us)
Async XLA Ops:
  3.5 20.4 %collective-permute-start.4 = (bf16[128,2304]{1,0:T(8,128)(2,1)}, bf16[128,2304]{1,0:T(8,128)(2,1)S(1)}, u32[]{:S(2)}, u32[]{:S(2)}) collective-permute-start(bf16[128,2304]{1,0:T(8,128)(2,1)} %get-tuple-element.225), channel_id=1, source_target_pairs={{0,32},{32,0},{64,96},{96,64},{1,33},{33,1},{65,97},{97,65},{2,34}... | collective-permute-start | bytes 1769480 | tf_op jit(solution)/shard_map/ppermute | solution.py:289
  5.1 18.8 %collective-permute-start.5 = (bf16[128,2304]{1,0:T(8,128)(2,1)}, bf16[128,2304]{1,0:T(8,128)(2,1)S(1)}, u32[]{:S(2)}, u32[]{:S(2)}) collective-permute-start(bf16[128,2304]{1,0:T(8,128)(2,1)} %get-tuple-element.226), channel_id=1, source_target_pairs={{0,96},{32,64},{64,32},{96,0},{1,97},{33,65},{65,33},{97,1},{2,98}... | collective-permute-start | bytes 1769480 | tf_op jit(solution)/shard_map/ppermute | solution.py:289
  44.7 15.1 %collective-permute-start.13 = (bf16[64,4096]{1,0:T(8,128)(2,1)S(1)}, bf16[64,4096]{1,0:T(8,128)(2,1)S(1)}, u32[]{:S(2)}, u32[]{:S(2)}) collective-permute-start(bf16[64,4096]{1,0:T(8,128)(2,1)S(1)} %copy-done.17), channel_id=1, source_target_pairs={{0,4},{2,6},{4,0},{6,2},{1,5},{3,7},{5,1},{7,3},{8,12},{10,14},{12... | collective-permute-start | bytes 1572872 | tf_op jit(solution)/shard_map/ppermute | solution.py:289
  62.1 24.5 %collective-permute-start.14 = (bf16[4,64,4096]{2,1,0:T(8,128)(2,1)}, bf16[4,64,4096]{2,1,0:T(8,128)(2,1)}, u32[]{:S(2)}, u32[]{:S(2)}) collective-permute-start(bf16[4,64,4096]{2,1,0:T(8,128)(2,1)} %join.3.refs_4_), channel_id=1, source_target_pairs={{0,1},{1,0},{2,3},{3,2},{4,5},{5,4},{6,7},{7,6},{8,9},{9,8},{10,11... | collective-permute-start | bytes 6291464 | tf_op jit(solution)/shard_map/ppermute | solution.py:312
  62.8 16.5 %collective-permute-start.18 = (bf16[128,2304]{1,0:T(8,128)(2,1)S(1)}, bf16[128,2304]{1,0:T(8,128)(2,1)S(1)}, u32[]{:S(2)}, u32[]{:S(2)}) collective-permute-start(bf16[128,2304]{1,0:T(8,128)(2,1)S(1)} %copy-done.16), channel_id=1, source_target_pairs={{0,64},{32,96},{64,0},{96,32},{1,65},{33,97},{65,1},{97,33},{2,66}... | collective-permute-start | bytes 1769480 | tf_op jit(solution)/shard_map/ppermute | solution.py:289
  64.2 22.3 %all-to-all-start = ((bf16[16,272,128]{2,1,0:T(8,128)(2,1)}), bf16[16,272,128]{2,1,0:T(8,128)(2,1)S(1)}, u32[]{:S(2)}, u32[]{:S(2)}) async-start(bf16[16,272,128]{2,1,0:T(8,128)(2,1)} %project.4), calls=%async_computation | async-start | bytes 2228224 | tf_op jit(solution)/shard_map/all_to_all | solution.py:285
  80.1 15.3 %collective-permute-start.20 = (bf16[128,2304]{1,0:T(8,128)(2,1)}, bf16[128,2304]{1,0:T(8,128)(2,1)}, u32[]{:S(2)}, u32[]{:S(2)}) collective-permute-start(bf16[128,2304]{1,0:T(8,128)(2,1)} %get-tuple-element.290), channel_id=1, source_target_pairs={{0,96},{32,64},{64,32},{96,0},{1,97},{33,65},{65,33},{97,1},{2,98}... | collective-permute-start | bytes 1769480 | tf_op jit(solution)/shard_map/ppermute | solution.py:289
  99.6 31.1 %collective-permute-start.27 = (bf16[4,128,2304]{2,1,0:T(8,128)(2,1)}, bf16[4,128,2304]{2,1,0:T(8,128)(2,1)}, u32[]{:S(2)}, u32[]{:S(2)}) collective-permute-start(bf16[4,128,2304]{2,1,0:T(8,128)(2,1)} %get-tuple-element.325.refs_5_.refs_7_), channel_id=1, source_target_pairs={{0,1},{1,0},{2,3},{3,2},{4,5},{5,4},{6,7},{7,6},{8,9},{9,8},{10,11... | collective-permute-start | bytes 7077896 | tf_op jit(solution)/shard_map/ppermute | solution.py:312
  101.6 14.9 %collective-permute-start.25 = (bf16[64,4096]{1,0:T(8,128)(2,1)}, bf16[64,4096]{1,0:T(8,128)(2,1)}, u32[]{:S(2)}, u32[]{:S(2)}) collective-permute-start(bf16[64,4096]{1,0:T(8,128)(2,1)} %get-tuple-element.308), channel_id=1, source_target_pairs={{0,6},{2,4},{4,2},{6,0},{1,7},{3,5},{5,3},{7,1},{8,14},{10,12},{12... | collective-permute-start | bytes 1572872 | tf_op jit(solution)/shard_map/ppermute | solution.py:289
  102.4 19.0 %all-to-all-start.1 = ((bf16[16,88,256]{2,1,0:T(8,128)(2,1)}), bf16[16,88,256]{2,1,0:T(8,128)(2,1)S(1)}, u32[]{:S(2)}, u32[]{:S(2)}) async-start(bf16[16,88,256]{2,1,0:T(8,128)(2,1)} %get-tuple-element.305), calls=%async_computation.1 | async-start | bytes 1441792 | tf_op jit(solution)/shard_map/all_to_all | solution.py:285
  135.0 25.3 %collective-permute-start.28 = (bf16[4,64,4096]{2,1,0:T(8,128)(2,1)}, bf16[4,64,4096]{2,1,0:T(8,128)(2,1)}, u32[]{:S(2)}, u32[]{:S(2)}) collective-permute-start(bf16[4,64,4096]{2,1,0:T(8,128)(2,1)} %get-tuple-element.359.refs_4_), channel_id=1, source_target_pairs={{0,1},{1,0},{2,3},{3,2},{4,5},{5,4},{6,7},{7,6},{8,9},{9,8},{10,11... | collective-permute-start | bytes 6291464 | tf_op jit(solution)/shard_map/ppermute | solution.py:312
  136.9 16.6 %collective-permute-start.32 = (bf16[128,2304]{1,0:T(8,128)(2,1)}, bf16[128,2304]{1,0:T(8,128)(2,1)S(1)}, u32[]{:S(2)}, u32[]{:S(2)}) collective-permute-start(bf16[128,2304]{1,0:T(8,128)(2,1)} %get-tuple-element.345), channel_id=1, source_target_pairs={{0,64},{32,96},{64,0},{96,32},{1,65},{33,97},{65,1},{97,33},{2,66}... | collective-permute-start | bytes 1769480 | tf_op jit(solution)/shard_map/ppermute | solution.py:289
  137.8 22.5 %all-to-all-start.2 = ((bf16[16,272,128]{2,1,0:T(8,128)(2,1)}), bf16[16,272,128]{2,1,0:T(8,128)(2,1)S(1)}, u32[]{:S(2)}, u32[]{:S(2)}) async-start(bf16[16,272,128]{2,1,0:T(8,128)(2,1)} %get-tuple-element.332), calls=%async_computation.2 | async-start | bytes 2228224 | tf_op jit(solution)/shard_map/all_to_all | solution.py:285
  153.5 15.5 %collective-permute-start.34 = (bf16[128,2304]{1,0:T(8,128)(2,1)}, bf16[128,2304]{1,0:T(8,128)(2,1)}, u32[]{:S(2)}, u32[]{:S(2)}) collective-permute-start(bf16[128,2304]{1,0:T(8,128)(2,1)} %get-tuple-element.350), channel_id=1, source_target_pairs={{0,96},{32,64},{64,32},{96,0},{1,97},{33,65},{65,33},{97,1},{2,98}... | collective-permute-start | bytes 1769480 | tf_op jit(solution)/shard_map/ppermute | solution.py:289
  173.3 30.5 %collective-permute-start.41 = (bf16[4,128,2304]{2,1,0:T(8,128)(2,1)}, bf16[4,128,2304]{2,1,0:T(8,128)(2,1)}, u32[]{:S(2)}, u32[]{:S(2)}) collective-permute-start(bf16[4,128,2304]{2,1,0:T(8,128)(2,1)} %get-tuple-element.385.refs_5_.refs_7_), channel_id=1, source_target_pairs={{0,1},{1,0},{2,3},{3,2},{4,5},{5,4},{6,7},{7,6},{8,9},{9,8},{10,11... | collective-permute-start | bytes 7077896 | tf_op jit(solution)/shard_map/ppermute | solution.py:312
  176.6 18.9 %all-to-all-start.3 = ((bf16[16,88,256]{2,1,0:T(8,128)(2,1)}), bf16[16,88,256]{2,1,0:T(8,128)(2,1)S(1)}, u32[]{:S(2)}, u32[]{:S(2)}) async-start(bf16[16,88,256]{2,1,0:T(8,128)(2,1)} %get-tuple-element.365), calls=%async_computation.3 | async-start | bytes 1441792 | tf_op jit(solution)/shard_map/all_to_all | solution.py:285
  208.0 25.8 %collective-permute-start.42 = (bf16[4,64,4096]{2,1,0:T(8,128)(2,1)}, bf16[4,64,4096]{2,1,0:T(8,128)(2,1)}, u32[]{:S(2)}, u32[]{:S(2)}) collective-permute-start(bf16[4,64,4096]{2,1,0:T(8,128)(2,1)} %get-tuple-element.415.refs_4_), channel_id=1, source_target_pairs={{0,1},{1,0},{2,3},{3,2},{4,5},{5,4},{6,7},{7,6},{8,9},{9,8},{10,11... | collective-permute-start | bytes 6291464 | tf_op jit(solution)/shard_map/ppermute | solution.py:312
  210.1 16.6 %collective-permute-start.46 = (bf16[128,2304]{1,0:T(8,128)(2,1)}, bf16[128,2304]{1,0:T(8,128)(2,1)S(1)}, u32[]{:S(2)}, u32[]{:S(2)}) collective-permute-start(bf16[128,2304]{1,0:T(8,128)(2,1)} %get-tuple-element.401), channel_id=1, source_target_pairs={{0,64},{32,96},{64,0},{96,32},{1,65},{33,97},{65,1},{97,33},{2,66}... | collective-permute-start | bytes 1769480 | tf_op jit(solution)/shard_map/ppermute | solution.py:289
  211.5 22.2 %all-to-all-start.4 = ((bf16[16,272,128]{2,1,0:T(8,128)(2,1)}), bf16[16,272,128]{2,1,0:T(8,128)(2,1)S(1)}, u32[]{:S(2)}, u32[]{:S(2)}) async-start(bf16[16,272,128]{2,1,0:T(8,128)(2,1)} %get-tuple-element.392), calls=%async_computation.4 | async-start | bytes 2228224 | tf_op jit(solution)/shard_map/all_to_all | solution.py:285
  227.4 15.2 %collective-permute-start.48 = (bf16[128,2304]{1,0:T(8,128)(2,1)}, bf16[128,2304]{1,0:T(8,128)(2,1)}, u32[]{:S(2)}, u32[]{:S(2)}) collective-permute-start(bf16[128,2304]{1,0:T(8,128)(2,1)} %get-tuple-element.406), channel_id=1, source_target_pairs={{0,96},{32,64},{64,32},{96,0},{1,97},{33,65},{65,33},{97,1},{2,98}... | collective-permute-start | bytes 1769480 | tf_op jit(solution)/shard_map/ppermute | solution.py:289
  246.7 30.8 %collective-permute-start.55 = (bf16[4,128,2304]{2,1,0:T(8,128)(2,1)}, bf16[4,128,2304]{2,1,0:T(8,128)(2,1)}, u32[]{:S(2)}, u32[]{:S(2)}) collective-permute-start(bf16[4,128,2304]{2,1,0:T(8,128)(2,1)} %get-tuple-element.433.refs_5_.refs_7_), channel_id=1, source_target_pairs={{0,1},{1,0},{2,3},{3,2},{4,5},{5,4},{6,7},{7,6},{8,9},{9,8},{10,11... | collective-permute-start | bytes 7077896 | tf_op jit(solution)/shard_map/ppermute | solution.py:312
  250.6 18.2 %all-to-all-start.5 = ((bf16[16,88,256]{2,1,0:T(8,128)(2,1)}), bf16[16,88,256]{2,1,0:T(8,128)(2,1)S(1)}, u32[]{:S(2)}, u32[]{:S(2)}) async-start(bf16[16,88,256]{2,1,0:T(8,128)(2,1)} %get-tuple-element.421), calls=%async_computation.5 | async-start | bytes 1441792 | tf_op jit(solution)/shard_map/all_to_all | solution.py:285
  281.7 24.5 %collective-permute-start.56 = (bf16[4,64,4096]{2,1,0:T(8,128)(2,1)}, bf16[4,64,4096]{2,1,0:T(8,128)(2,1)S(1)}, u32[]{:S(2)}, u32[]{:S(2)}) collective-permute-start(bf16[4,64,4096]{2,1,0:T(8,128)(2,1)} %get-tuple-element.441.refs_4_), channel_id=1, source_target_pairs={{0,1},{1,0},{2,3},{3,2},{4,5},{5,4},{6,7},{7,6},{8,9},{9,8},{10,11... | collective-permute-start | bytes 6291464 | tf_op jit(solution)/shard_map/ppermute | solution.py:312
  330.0 16.3 %collective-permute-start.63 = (bf16[88,256]{1,0:T(8,128)(2,1)S(1)}, bf16[88,256]{1,0:T(8,128)(2,1)S(1)}, u32[]{:S(2)}, u32[]{:S(2)}) collective-permute-start(bf16[88,256]{1,0:T(8,128)(2,1)S(1)} %get-tuple-element.456), channel_id=1, source_target_pairs={{0,96},{1,32},{2,0},{3,64},{4,97},{5,33},{6,1},{7,65},{8,98},{9,34... | collective-permute-start | bytes 135176 | tf_op jit(solution)/shard_map/ppermute | solution.py:400
  (65 other events, 651.1 us)

commit v7 on v5

--- a/solution.py
+++ b/solution.py
@@ -373,10 +373,11 @@
             received, (cut, ahead) = after(received, (cut, ahead))
         mixed = line(attend(received), "y")
         if layer < 3:
-            mixed, (ins, cut) = after(mixed, (ins, cut))
+            mixed, cut = after(mixed, cut)
             outs_next = relay(cut, "y")
-            partial, ins = output(scalars, mixed, outs, ins)
-            ins = swapped(ins)
+            partial = output(scalars, mixed, outs, [])[0]
+            partial, ins = after(partial, ins)
+            ins = swapped(join(ins))
             outs = outs_next
         else:
             partial = output(scalars, mixed, outs, [])[0]

time: 356 us -> 360 us (1.011)
  Pallas kernels: 62.7 us -> 67.1 us
  starting transfers between devices: 142 us -> 146 us
    pallas_call x2 -> x5, Pallas kernels: 4.82 us -> 12 us  [join(): pl.pallas_call(join_kernel, grid=(2,), in_specs=[pl.BlockSpec((half, colu...]
  transfers between devices with their start and end apart: 71 -> 71, of which waited for: 42 -> 45; matrix products, arithmetic and copies ran while one was open for 0% -> 0% of each run, Pallas kernels for 7% -> 10%
where the time goes in v7:
time: 360 us; the launch traced here: 359 us
  starting transfers between devices  146 us (41%)
  waiting for transfers between devices  121 us (34%)
  Pallas kernels  67.1 us (19%)
  blocking collectives  21.2 us (6%)
    ppermute x48, waiting for transfers between devices, across_line(): return lax.ppermute(value, axis, [(i, i ^ by) for i in range(4)])  88.6 us
    ppermute x48, starting transfers between devices, across_line(): return lax.ppermute(value, axis, [(i, i ^ by) for i in range(4)])  52.8 us
    all_to_all x7, starting transfers between devices, exchange(): return lax.all_to_all(value, axes, 0, 0, tiled=True)  44.8 us
    ppermute x8, starting transfers between devices, body(): rounds.append(lax.ppermute(piece, ALL, pairs))  28.5 us
    all_to_all x7, waiting for transfers between devices, exchange(): return lax.all_to_all(value, axes, 0, 0, tiled=True)  21.3 us
    all_to_all x1, blocking collectives, exchange(): return lax.all_to_all(value, axes, 0, 0, tiled=True)  21.2 us
    ppermute x8, starting transfers between devices, swapped(): return (joined, lax.ppermute(joined, 'c', [(0, 1), (1, 0)]))  19.5 us
    pallas_call x4, Pallas kernels, project(): pl.pallas_call(functools.partial(project_kernel, layer), grid=(2,), in_sp...  16.4 us
  transfers between devices with their start and end apart: 71, of which 45 were waited for; matrix products, arithmetic and copies ran while one was open for 0% of the time, Pallas kernels for 10%

profile of v7, /device:TPU:5, one launch (start us, length us, event | category | flops | bytes accessed | tf_op | source)
XLA Modules:
  0.0 359.0 jit_solution(15086003366393838146)
XLA Ops:
  7.4 4.8 %collective-permute-start = (bf16[96,256]{1,0:T(8,128)(2,1)S(1)}, bf16[96,256]{1,0:T(8,128)(2,1)S(1)}, u32[]{:S(2)}, u32[]{:S(2)}) collective-permute-start(bf16[96,256]{1,0:T(8,128)(2,1)S(1)} %pad_maximum_fusion.3), channel_id=1, source_target_pairs={{0,0},{1,4},{2,8},{3,12},{4,16},{5,20},{6,24},{7,28},{8,2},{9,6},{... | collective-permute-start | bytes 147464 | tf_op jit(solution)/shard_map/ppermute | solution.py:328
  29.4 8.0 %collective-permute-done.7.refs_1_ = bf16[64,4096]{1,0:T(8,128)(2,1)S(1)} collective-permute-done((bf16[64,4096]{1,0:T(8,128)(2,1)}, bf16[64,4096]{1,0:T(8,128)(2,1)S(1)}, u32[]{:S(2)}, u32[]{:S(2)}) %collective-permute-start.7) | collective-permute-done | bytes 524320 | tf_op jit(solution)/shard_map/ppermute | solution.py:289
  64.4 6.2 %all-to-all-start = ((bf16[16,272,128]{2,1,0:T(8,128)(2,1)}), bf16[16,272,128]{2,1,0:T(8,128)(2,1)S(1)}, u32[]{:S(2)}, u32[]{:S(2)}) async-start(bf16[16,272,128]{2,1,0:T(8,128)(2,1)} %project.4), calls=%async_computation | async-start | bytes 2228224 | tf_op jit(solution)/shard_map/all_to_all | solution.py:285
  70.6 7.4 %collective-permute-done.18.refs_1_ = bf16[128,2304]{1,0:T(8,128)(2,1)S(1)} collective-permute-done((bf16[128,2304]{1,0:T(8,128)(2,1)}, bf16[128,2304]{1,0:T(8,128)(2,1)S(1)}, u32[]{:S(2)}, u32[]{:S(2)}) %collective-permute-start.18) | collective-permute-done | bytes 589856 | tf_op jit(solution)/shard_map/ppermute | solution.py:289
  103.7 7.4 %all-to-all-start.1 = ((bf16[16,88,256]{2,1,0:T(8,128)(2,1)}), bf16[16,88,256]{2,1,0:T(8,128)(2,1)S(1)}, u32[]{:S(2)}, u32[]{:S(2)}) async-start(bf16[16,88,256]{2,1,0:T(8,128)(2,1)} %output.4), calls=%async_computation.1 | async-start | bytes 1441792 | tf_op jit(solution)/shard_map/all_to_all | solution.py:285
  111.2 4.7 %collective-permute-done.24.refs_10_ = bf16[64,4096]{1,0:T(8,128)(2,1)S(1)} collective-permute-done((bf16[64,4096]{1,0:T(8,128)(2,1)}, bf16[64,4096]{1,0:T(8,128)(2,1)S(1)}, u32[]{:S(2)}, u32[]{:S(2)}) %collective-permute-start.24) | collective-permute-done | bytes 524320 | tf_op jit(solution)/shard_map/ppermute | solution.py:289
  118.5 4.5 %all-to-all-done.1.recv_ref = bf16[16,88,256]{2,1,0:T(8,128)(2,1)S(1)} async-done(((bf16[16,88,256]{2,1,0:T(8,128)(2,1)}), bf16[16,88,256]{2,1,0:T(8,128)(2,1)S(1)}, u32[]{:S(2)}, u32[]{:S(2)}) %all-to-all-start.1) | async-done | bytes 720928 | tf_op jit(solution)/shard_map/all_to_all | solution.py:285
  131.4 4.3 %project.5 = (bf16[16,272,128]{2,1,0:T(8,128)(2,1)}, bf16[4,64,4096]{2,1,0:T(8,128)(2,1)}) custom-call(s32[3]{0:T(128)S(1)} %copy-done.10, bf16[88,256]{1,0:T(8,128)(2,1)S(1)} %close.4.refs_0_.x_ref, bf16[88,256]{1,0:T(8,128)(2,1)S(1)} %collective-permute-done.21.refs_1_, bf16[88,256]{1,0:T(8,128)(2,1)S(1)} %collective-permute-done.22.refs_2_, ...), custom_call_target="tpu_custom_call" | custom-call | flops 415236096 | bytes 10000000 | tf_op jit(solution)/shard_map/project/pallas_call | solution.py:168
  138.9 8.0 %all-to-all-start.2 = ((bf16[16,272,128]{2,1,0:T(8,128)(2,1)}), bf16[16,272,128]{2,1,0:T(8,128)(2,1)S(1)}, u32[]{:S(2)}, u32[]{:S(2)}) async-start(bf16[16,272,128]{2,1,0:T(8,128)(2,1)} %get-tuple-element.328), calls=%async_computation.2 | async-start | bytes 2228224 | tf_op jit(solution)/shard_map/all_to_all | solution.py:285
  146.9 5.8 %collective-permute-done.32.refs_1_ = bf16[128,2304]{1,0:T(8,128)(2,1)S(1)} collective-permute-done((bf16[128,2304]{1,0:T(8,128)(2,1)}, bf16[128,2304]{1,0:T(8,128)(2,1)S(1)}, u32[]{:S(2)}, u32[]{:S(2)}) %collective-permute-start.32) | collective-permute-done | bytes 589856 | tf_op jit(solution)/shard_map/ppermute | solution.py:289
  180.0 6.0 %all-to-all-start.3 = ((bf16[16,88,256]{2,1,0:T(8,128)(2,1)}), bf16[16,88,256]{2,1,0:T(8,128)(2,1)S(1)}, u32[]{:S(2)}, u32[]{:S(2)}) async-start(bf16[16,88,256]{2,1,0:T(8,128)(2,1)} %output.5), calls=%async_computation.3 | async-start | bytes 1441792 | tf_op jit(solution)/shard_map/all_to_all | solution.py:285
  186.0 6.1 %collective-permute-done.38.refs_10_ = bf16[64,4096]{1,0:T(8,128)(2,1)S(1)} collective-permute-done((bf16[64,4096]{1,0:T(8,128)(2,1)}, bf16[64,4096]{1,0:T(8,128)(2,1)S(1)}, u32[]{:S(2)}, u32[]{:S(2)}) %collective-permute-start.38) | collective-permute-done | bytes 524320 | tf_op jit(solution)/shard_map/ppermute | solution.py:289
  207.5 4.2 %project.6 = (bf16[16,272,128]{2,1,0:T(8,128)(2,1)}, bf16[4,64,4096]{2,1,0:T(8,128)(2,1)}) custom-call(s32[3]{0:T(128)S(1)} %copy-done.10, bf16[88,256]{1,0:T(8,128)(2,1)S(1)} %close.5.refs_0_.x_ref, bf16[88,256]{1,0:T(8,128)(2,1)S(1)} %collective-permute-done.35.refs_1_, bf16[88,256]{1,0:T(8,128)(2,1)S(1)} %collective-permute-done.36.refs_2_, ...), custom_call_target="tpu_custom_call" | custom-call | flops 415236096 | bytes 10000000 | tf_op jit(solution)/shard_map/project/pallas_call | solution.py:168
  214.9 6.1 %all-to-all-start.4 = ((bf16[16,272,128]{2,1,0:T(8,128)(2,1)}), bf16[16,272,128]{2,1,0:T(8,128)(2,1)S(1)}, u32[]{:S(2)}, u32[]{:S(2)}) async-start(bf16[16,272,128]{2,1,0:T(8,128)(2,1)} %get-tuple-element.387), calls=%async_computation.4 | async-start | bytes 2228224 | tf_op jit(solution)/shard_map/all_to_all | solution.py:285
  221.0 7.7 %collective-permute-done.46.refs_1_ = bf16[128,2304]{1,0:T(8,128)(2,1)S(1)} collective-permute-done((bf16[128,2304]{1,0:T(8,128)(2,1)}, bf16[128,2304]{1,0:T(8,128)(2,1)S(1)}, u32[]{:S(2)}, u32[]{:S(2)}) %collective-permute-start.46) | collective-permute-done | bytes 589856 | tf_op jit(solution)/shard_map/ppermute | solution.py:289
  254.3 5.9 %all-to-all-start.5 = ((bf16[16,88,256]{2,1,0:T(8,128)(2,1)}), bf16[16,88,256]{2,1,0:T(8,128)(2,1)S(1)}, u32[]{:S(2)}, u32[]{:S(2)}) async-start(bf16[16,88,256]{2,1,0:T(8,128)(2,1)} %output.6), calls=%async_computation.5 | async-start | bytes 1441792 | tf_op jit(solution)/shard_map/all_to_all | solution.py:285
  260.1 6.3 %collective-permute-done.52.refs_10_ = bf16[64,4096]{1,0:T(8,128)(2,1)S(1)} collective-permute-done((bf16[64,4096]{1,0:T(8,128)(2,1)}, bf16[64,4096]{1,0:T(8,128)(2,1)S(1)}, u32[]{:S(2)}, u32[]{:S(2)}) %collective-permute-start.52) | collective-permute-done | bytes 524320 | tf_op jit(solution)/shard_map/ppermute | solution.py:289
  281.9 4.2 %project.7 = (bf16[16,272,128]{2,1,0:T(8,128)(2,1)}, bf16[4,64,4096]{2,1,0:T(8,128)(2,1)}) custom-call(s32[3]{0:T(128)S(1)} %copy-done.10, bf16[88,256]{1,0:T(8,128)(2,1)S(1)} %close.6.refs_0_.x_ref, bf16[88,256]{1,0:T(8,128)(2,1)S(1)} %collective-permute-done.49.refs_1_, bf16[88,256]{1,0:T(8,128)(2,1)S(1)} %collective-permute-done.50.refs_2_, ...), custom_call_target="tpu_custom_call" | custom-call | flops 415236096 | bytes 10000000 | tf_op jit(solution)/shard_map/project/pallas_call | solution.py:168
  287.8 21.2 %all_to_all.40.recv_ref = bf16[16,272,128]{2,1,0:T(8,128)(2,1)S(1)} all-to-all(bf16[16,272,128]{2,1,0:T(8,128)(2,1)} %get-tuple-element.432), channel_id=1, replica_groups=mesh['z'=4,'x'=4,'y'=4,'c'=2] {'x','y'}, dimensions={0} | all-to-all | bytes 2228224 | tf_op jit(solution)/shard_map/all_to_all | solution.py:285
  319.3 5.3 %all-to-all-start.7 = ((bf16[16,88,256]{2,1,0:T(8,128)(2,1)}), bf16[16,88,256]{2,1,0:T(8,128)(2,1)S(1)}, u32[]{:S(2)}, u32[]{:S(2)}) async-start(bf16[16,88,256]{2,1,0:T(8,128)(2,1)} %output.7), calls=%async_computation.7 | async-start | bytes 1441792 | tf_op jit(solution)/shard_map/all_to_all | solution.py:285
  324.5 7.7 %all-to-all-done.7.recv_ref = bf16[16,88,256]{2,1,0:T(8,128)(2,1)S(1)} async-done(((bf16[16,88,256]{2,1,0:T(8,128)(2,1)}), bf16[16,88,256]{2,1,0:T(8,128)(2,1)S(1)}, u32[]{:S(2)}, u32[]{:S(2)}) %all-to-all-start.7) | async-done | bytes 720928 | tf_op jit(solution)/shard_map/all_to_all | solution.py:285
  332.5 6.3 %collective-permute-start.63 = (bf16[88,256]{1,0:T(8,128)(2,1)S(1)}, bf16[88,256]{1,0:T(8,128)(2,1)S(1)}, u32[]{:S(2)}, u32[]{:S(2)}) collective-permute-start(bf16[88,256]{1,0:T(8,128)(2,1)S(1)} %get-tuple-element.450), channel_id=1, source_target_pairs={{0,96},{1,32},{2,0},{3,64},{4,97},{5,33},{6,1},{7,65},{8,98},{9,34... | collective-permute-start | bytes 135176 | tf_op jit(solution)/shard_map/ppermute | solution.py:396
  339.7 6.8 %collective-permute-start.61 = (bf16[88,256]{1,0:T(8,128)(2,1)S(1)}, bf16[88,256]{1,0:T(8,128)(2,1)S(1)}, u32[]{:S(2)}, u32[]{:S(2)}) collective-permute-start(bf16[88,256]{1,0:T(8,128)(2,1)S(1)} %get-tuple-element.452), channel_id=1, source_target_pairs={{0,32},{1,96},{2,64},{3,0},{4,33},{5,97},{6,65},{7,1},{8,34},{9,98... | collective-permute-start | bytes 135176 | tf_op jit(solution)/shard_map/ppermute | solution.py:396
  349.7 8.5 %collective-permute-done.60 = bf16[88,256]{1,0:T(8,128)(2,1)S(1)} collective-permute-done((bf16[88,256]{1,0:T(8,128)(2,1)S(1)}, bf16[88,256]{1,0:T(8,128)(2,1)S(1)}, u32[]{:S(2)}, u32[]{:S(2)}) %collective-permute-start.60) | collective-permute-done | bytes 45088 | tf_op jit(solution)/shard_map/ppermute | solution.py:396
  (205 shorter events, 195.1 us)
Async XLA Ops:
  3.4 20.4 %collective-permute-start.4 = (bf16[128,2304]{1,0:T(8,128)(2,1)}, bf16[128,2304]{1,0:T(8,128)(2,1)S(1)}, u32[]{:S(2)}, u32[]{:S(2)}) collective-permute-start(bf16[128,2304]{1,0:T(8,128)(2,1)} %get-tuple-element.222), channel_id=1, source_target_pairs={{0,32},{32,0},{64,96},{96,64},{1,33},{33,1},{65,97},{97,65},{2,34}... | collective-permute-start | bytes 1769480 | tf_op jit(solution)/shard_map/ppermute | solution.py:289
  5.1 18.8 %collective-permute-start.5 = (bf16[128,2304]{1,0:T(8,128)(2,1)}, bf16[128,2304]{1,0:T(8,128)(2,1)S(1)}, u32[]{:S(2)}, u32[]{:S(2)}) collective-permute-start(bf16[128,2304]{1,0:T(8,128)(2,1)} %get-tuple-element.223), channel_id=1, source_target_pairs={{0,96},{32,64},{64,32},{96,0},{1,97},{33,65},{65,33},{97,1},{2,98}... | collective-permute-start | bytes 1769480 | tf_op jit(solution)/shard_map/ppermute | solution.py:289
  62.0 23.9 %collective-permute-start.14 = (bf16[4,64,4096]{2,1,0:T(8,128)(2,1)}, bf16[4,64,4096]{2,1,0:T(8,128)(2,1)}, u32[]{:S(2)}, u32[]{:S(2)}) collective-permute-start(bf16[4,64,4096]{2,1,0:T(8,128)(2,1)} %join.6.refs_4_), channel_id=1, source_target_pairs={{0,1},{1,0},{2,3},{3,2},{4,5},{5,4},{6,7},{7,6},{8,9},{9,8},{10,11... | collective-permute-start | bytes 6291464 | tf_op jit(solution)/shard_map/ppermute | solution.py:307
  62.8 15.3 %collective-permute-start.18 = (bf16[128,2304]{1,0:T(8,128)(2,1)}, bf16[128,2304]{1,0:T(8,128)(2,1)S(1)}, u32[]{:S(2)}, u32[]{:S(2)}) collective-permute-start(bf16[128,2304]{1,0:T(8,128)(2,1)} %get-tuple-element.292), channel_id=1, source_target_pairs={{0,32},{32,0},{64,96},{96,64},{1,33},{33,1},{65,97},{97,65},{2,34}... | collective-permute-start | bytes 1769480 | tf_op jit(solution)/shard_map/ppermute | solution.py:289
  63.5 16.2 %collective-permute-start.19 = (bf16[128,2304]{1,0:T(8,128)(2,1)}, bf16[128,2304]{1,0:T(8,128)(2,1)}, u32[]{:S(2)}, u32[]{:S(2)}) collective-permute-start(bf16[128,2304]{1,0:T(8,128)(2,1)} %get-tuple-element.293), channel_id=1, source_target_pairs={{0,96},{32,64},{64,32},{96,0},{1,97},{33,65},{65,33},{97,1},{2,98}... | collective-permute-start | bytes 1769480 | tf_op jit(solution)/shard_map/ppermute | solution.py:289
  64.4 21.5 %all-to-all-start = ((bf16[16,272,128]{2,1,0:T(8,128)(2,1)}), bf16[16,272,128]{2,1,0:T(8,128)(2,1)S(1)}, u32[]{:S(2)}, u32[]{:S(2)}) async-start(bf16[16,272,128]{2,1,0:T(8,128)(2,1)} %project.4), calls=%async_computation | async-start | bytes 2228224 | tf_op jit(solution)/shard_map/all_to_all | solution.py:285
  79.7 16.4 %collective-permute-start.20 = (bf16[128,2304]{1,0:T(8,128)(2,1)}, bf16[128,2304]{1,0:T(8,128)(2,1)S(1)}, u32[]{:S(2)}, u32[]{:S(2)}) collective-permute-start(bf16[128,2304]{1,0:T(8,128)(2,1)} %get-tuple-element.296), channel_id=1, source_target_pairs={{0,64},{32,96},{64,0},{96,32},{1,65},{33,97},{65,1},{97,33},{2,66}... | collective-permute-start | bytes 1769480 | tf_op jit(solution)/shard_map/ppermute | solution.py:289
  98.5 32.9 %collective-permute-start.27 = (bf16[4,128,2304]{2,1,0:T(8,128)(2,1)}, bf16[4,128,2304]{2,1,0:T(8,128)(2,1)}, u32[]{:S(2)}, u32[]{:S(2)}) collective-permute-start(bf16[4,128,2304]{2,1,0:T(8,128)(2,1)} %join.7.refs_5_.refs_7_), channel_id=1, source_target_pairs={{0,1},{1,0},{2,3},{3,2},{4,5},{5,4},{6,7},{7,6},{8,9},{9,8},{10,11... | collective-permute-start | bytes 7077896 | tf_op jit(solution)/shard_map/ppermute | solution.py:307
  103.7 19.2 %all-to-all-start.1 = ((bf16[16,88,256]{2,1,0:T(8,128)(2,1)}), bf16[16,88,256]{2,1,0:T(8,128)(2,1)S(1)}, u32[]{:S(2)}, u32[]{:S(2)}) async-start(bf16[16,88,256]{2,1,0:T(8,128)(2,1)} %output.4), calls=%async_computation.1 | async-start | bytes 1441792 | tf_op jit(solution)/shard_map/all_to_all | solution.py:285
  135.7 25.4 %collective-permute-start.28 = (bf16[4,64,4096]{2,1,0:T(8,128)(2,1)}, bf16[4,64,4096]{2,1,0:T(8,128)(2,1)}, u32[]{:S(2)}, u32[]{:S(2)}) collective-permute-start(bf16[4,64,4096]{2,1,0:T(8,128)(2,1)} %get-tuple-element.348.refs_4_), channel_id=1, source_target_pairs={{0,1},{1,0},{2,3},{3,2},{4,5},{5,4},{6,7},{7,6},{8,9},{9,8},{10,11... | collective-permute-start | bytes 6291464 | tf_op jit(solution)/shard_map/ppermute | solution.py:307
  137.5 15.2 %collective-permute-start.32 = (bf16[128,2304]{1,0:T(8,128)(2,1)}, bf16[128,2304]{1,0:T(8,128)(2,1)S(1)}, u32[]{:S(2)}, u32[]{:S(2)}) collective-permute-start(bf16[128,2304]{1,0:T(8,128)(2,1)} %get-tuple-element.351), channel_id=1, source_target_pairs={{0,32},{32,0},{64,96},{96,64},{1,33},{33,1},{65,97},{97,65},{2,34}... | collective-permute-start | bytes 1769480 | tf_op jit(solution)/shard_map/ppermute | solution.py:289
  138.2 16.1 %collective-permute-start.33 = (bf16[128,2304]{1,0:T(8,128)(2,1)}, bf16[128,2304]{1,0:T(8,128)(2,1)}, u32[]{:S(2)}, u32[]{:S(2)}) collective-permute-start(bf16[128,2304]{1,0:T(8,128)(2,1)} %get-tuple-element.352), channel_id=1, source_target_pairs={{0,96},{32,64},{64,32},{96,0},{1,97},{33,65},{65,33},{97,1},{2,98}... | collective-permute-start | bytes 1769480 | tf_op jit(solution)/shard_map/ppermute | solution.py:289
  138.9 22.2 %all-to-all-start.2 = ((bf16[16,272,128]{2,1,0:T(8,128)(2,1)}), bf16[16,272,128]{2,1,0:T(8,128)(2,1)S(1)}, u32[]{:S(2)}, u32[]{:S(2)}) async-start(bf16[16,272,128]{2,1,0:T(8,128)(2,1)} %get-tuple-element.328), calls=%async_computation.2 | async-start | bytes 2228224 | tf_op jit(solution)/shard_map/all_to_all | solution.py:285
  154.3 17.9 %collective-permute-start.34 = (bf16[128,2304]{1,0:T(8,128)(2,1)}, bf16[128,2304]{1,0:T(8,128)(2,1)S(1)}, u32[]{:S(2)}, u32[]{:S(2)}) collective-permute-start(bf16[128,2304]{1,0:T(8,128)(2,1)} %get-tuple-element.355), channel_id=1, source_target_pairs={{0,64},{32,96},{64,0},{96,32},{1,65},{33,97},{65,1},{97,33},{2,66}... | collective-permute-start | bytes 1769480 | tf_op jit(solution)/shard_map/ppermute | solution.py:289
  174.6 32.9 %collective-permute-start.41 = (bf16[4,128,2304]{2,1,0:T(8,128)(2,1)}, bf16[4,128,2304]{2,1,0:T(8,128)(2,1)}, u32[]{:S(2)}, u32[]{:S(2)}) collective-permute-start(bf16[4,128,2304]{2,1,0:T(8,128)(2,1)} %join.8.refs_5_.refs_7_), channel_id=1, source_target_pairs={{0,1},{1,0},{2,3},{3,2},{4,5},{5,4},{6,7},{7,6},{8,9},{9,8},{10,11... | collective-permute-start | bytes 7077896 | tf_op jit(solution)/shard_map/ppermute | solution.py:307
  180.0 17.8 %all-to-all-start.3 = ((bf16[16,88,256]{2,1,0:T(8,128)(2,1)}), bf16[16,88,256]{2,1,0:T(8,128)(2,1)S(1)}, u32[]{:S(2)}, u32[]{:S(2)}) async-start(bf16[16,88,256]{2,1,0:T(8,128)(2,1)} %output.5), calls=%async_computation.3 | async-start | bytes 1441792 | tf_op jit(solution)/shard_map/all_to_all | solution.py:285
  211.7 23.8 %collective-permute-start.42 = (bf16[4,64,4096]{2,1,0:T(8,128)(2,1)}, bf16[4,64,4096]{2,1,0:T(8,128)(2,1)}, u32[]{:S(2)}, u32[]{:S(2)}) collective-permute-start(bf16[4,64,4096]{2,1,0:T(8,128)(2,1)} %get-tuple-element.403.refs_4_), channel_id=1, source_target_pairs={{0,1},{1,0},{2,3},{3,2},{4,5},{5,4},{6,7},{7,6},{8,9},{9,8},{10,11... | collective-permute-start | bytes 6291464 | tf_op jit(solution)/shard_map/ppermute | solution.py:307
  213.6 16.1 %collective-permute-start.47 = (bf16[128,2304]{1,0:T(8,128)(2,1)}, bf16[128,2304]{1,0:T(8,128)(2,1)}, u32[]{:S(2)}, u32[]{:S(2)}) collective-permute-start(bf16[128,2304]{1,0:T(8,128)(2,1)} %get-tuple-element.407), channel_id=1, source_target_pairs={{0,96},{32,64},{64,32},{96,0},{1,97},{33,65},{65,33},{97,1},{2,98}... | collective-permute-start | bytes 1769480 | tf_op jit(solution)/shard_map/ppermute | solution.py:289
  214.9 20.6 %all-to-all-start.4 = ((bf16[16,272,128]{2,1,0:T(8,128)(2,1)}), bf16[16,272,128]{2,1,0:T(8,128)(2,1)S(1)}, u32[]{:S(2)}, u32[]{:S(2)}) async-start(bf16[16,272,128]{2,1,0:T(8,128)(2,1)} %get-tuple-element.387), calls=%async_computation.4 | async-start | bytes 2228224 | tf_op jit(solution)/shard_map/all_to_all | solution.py:285
  229.7 17.3 %collective-permute-start.48 = (bf16[128,2304]{1,0:T(8,128)(2,1)}, bf16[128,2304]{1,0:T(8,128)(2,1)S(1)}, u32[]{:S(2)}, u32[]{:S(2)}) collective-permute-start(bf16[128,2304]{1,0:T(8,128)(2,1)} %get-tuple-element.410), channel_id=1, source_target_pairs={{0,64},{32,96},{64,0},{96,32},{1,65},{33,97},{65,1},{97,33},{2,66}... | collective-permute-start | bytes 1769480 | tf_op jit(solution)/shard_map/ppermute | solution.py:289
  249.3 32.5 %collective-permute-start.55 = (bf16[4,128,2304]{2,1,0:T(8,128)(2,1)}, bf16[4,128,2304]{2,1,0:T(8,128)(2,1)}, u32[]{:S(2)}, u32[]{:S(2)}) collective-permute-start(bf16[4,128,2304]{2,1,0:T(8,128)(2,1)} %join.9.refs_5_.refs_7_), channel_id=1, source_target_pairs={{0,1},{1,0},{2,3},{3,2},{4,5},{5,4},{6,7},{7,6},{8,9},{9,8},{10,11... | collective-permute-start | bytes 7077896 | tf_op jit(solution)/shard_map/ppermute | solution.py:307
  254.3 17.7 %all-to-all-start.5 = ((bf16[16,88,256]{2,1,0:T(8,128)(2,1)}), bf16[16,88,256]{2,1,0:T(8,128)(2,1)S(1)}, u32[]{:S(2)}, u32[]{:S(2)}) async-start(bf16[16,88,256]{2,1,0:T(8,128)(2,1)} %output.6), calls=%async_computation.5 | async-start | bytes 1441792 | tf_op jit(solution)/shard_map/all_to_all | solution.py:285
  286.1 23.0 %collective-permute-start.56 = (bf16[4,64,4096]{2,1,0:T(8,128)(2,1)}, bf16[4,64,4096]{2,1,0:T(8,128)(2,1)S(1)}, u32[]{:S(2)}, u32[]{:S(2)}) collective-permute-start(bf16[4,64,4096]{2,1,0:T(8,128)(2,1)} %get-tuple-element.435.refs_4_), channel_id=1, source_target_pairs={{0,1},{1,0},{2,3},{3,2},{4,5},{5,4},{6,7},{7,6},{8,9},{9,8},{10,11... | collective-permute-start | bytes 6291464 | tf_op jit(solution)/shard_map/ppermute | solution.py:307
  332.5 16.3 %collective-permute-start.63 = (bf16[88,256]{1,0:T(8,128)(2,1)S(1)}, bf16[88,256]{1,0:T(8,128)(2,1)S(1)}, u32[]{:S(2)}, u32[]{:S(2)}) collective-permute-start(bf16[88,256]{1,0:T(8,128)(2,1)S(1)} %get-tuple-element.450), channel_id=1, source_target_pairs={{0,96},{1,32},{2,0},{3,64},{4,97},{5,33},{6,1},{7,65},{8,98},{9,34... | collective-permute-start | bytes 135176 | tf_op jit(solution)/shard_map/ppermute | solution.py:396
  (64 other events, 609.8 us)
